TPU v7x, 256 devices: a whole 4x4x8 slice. The times are simulated.
256 devices in a mesh: occ: 64 (over z, x_lo, y), slab: 4 (over x_hi, core).
Axes of the slice: x: 4 (x_hi: 2, x_lo: 2; x = x_hi * 2 + x_lo), y: 4, z: 8, core: 2. Of those that a mesh axis runs over, the one named last changes fastest.
Arguments:
- three_centre: bfloat16 [64, 640, 4096], P(None, 'slab', 'occ'), may hold values from -0.75 to 0.75
- eps_occ: float32 [16], replicated, may hold values from -3 to -0.5
- eps_vir: float32 [2560], replicated, may hold values from 0.2 to 4
- block_owner: int32 [64], replicated, may hold values from 0 to 63, each once
- round_order: int32 [2], replicated, may hold values from 0 to 63
Outputs:
- gamma: bfloat16 [64, 640, 4096], P('occ', 'slab')
Inputs may be any that keep to these rules, and one draw needn't show every extreme that they name: `block_owner`: each owner position holds a different block.
All inputs are finite; a program needn't handle non-finite values.
Results may differ from a plain program's by a relative error of at most 0.0045.
Values may be sent and summed in bfloat16 or wider, within the bound.
No kernel may reach another device: no remote copies, remote signals or barrier semaphores. Data moves between devices by JAX's collectives and lax.ppermute only.
A program may use at most 64 MiB of HBM per device.

v0:
```python
import jax
import jax.numpy as jnp
from jax import lax
from jax.sharding import PartitionSpec as P

ROUNDS = 2


def spread(block, axis, owner):
    block = jnp.where(lax.axis_index(axis) == owner, block, jnp.zeros_like(block))
    return lax.psum(block, axis)


def on_device(three_centre, eps_occ, eps_vir, block_owner, round_order):
    my_block = lax.all_to_all(three_centre, "occ", split_axis=0, concat_axis=2, tiled=True)
    row_count = my_block.shape[1]
    slab_count = lax.axis_size("slab")
    block_span = row_count * slab_count
    vir_count = eps_vir.shape[0]

    def energies(owner_slot, row_offset, span_rows):
        first_pair = block_owner[owner_slot] * block_span + row_offset
        occ_level = lax.dynamic_slice_in_dim(eps_occ, first_pair // vir_count, 1)
        vir_level = lax.dynamic_slice_in_dim(eps_vir, first_pair % vir_count, span_rows)
        return occ_level - vir_level

    left_gap = energies(lax.axis_index("occ"), lax.axis_index("slab") * row_count, row_count)
    local_rows = my_block[0]
    gamma_sum = jnp.zeros((row_count, my_block.shape[2]), jnp.float32)
    full_block = lax.all_gather(my_block, "slab", axis=1, tiled=True)
    for round_step in range(ROUNDS):
        root_slot = round_order[round_step]
        sent_block = spread(full_block, "occ", root_slot)
        piece_rows = sent_block.shape[1]
        intersection = lax.dot_general(
            local_rows, sent_block[0], (((1,), (1,)), ((), ())), preferred_element_type=jnp.float32
        )
        denominator = left_gap[:, None] + energies(root_slot, 0, piece_rows)[None, :]
        amplitude = (intersection / denominator).astype(jnp.bfloat16)
        gamma_sum = gamma_sum + jnp.dot(
            amplitude, sent_block[0], preferred_element_type=jnp.float32
        )
    return gamma_sum.astype(jnp.bfloat16)[None]


def solution(mesh):
    in_specs = (P(None, "slab", "occ"), P(), P(), P(), P())
    out_specs = P("occ", "slab", None)
    return jax.shard_map(
        on_device, mesh=mesh, in_specs=in_specs, out_specs=out_specs, check_vma=False
    )
```

profile of v0, /device:TPU:8, one launch (start us, length us, event | category | flops | bytes accessed | tf_op | source)
XLA Modules:
  0.0 798.8 jit_solution(1864262255521082837)
XLA Ops:
  6.5 0.0 copy-start.3
  6.5 0.0 all-gather.2.cloned.1.call-start
  6.5 63.5 %all_to_all.18 = bf16[64,160,64]{1,2,0:T(8,128)(2,1)S(1)} all-to-all(bf16[64,160,64]{1,2,0:T(8,128)(2,1)} %param.5), channel_id=1, replica_groups=mesh['occ'=64,'slab'=4] {'occ'}, dimensions={0} | all-to-all | bytes 2621440 | tf_op jit(solution)/shard_map/all_to_all | solution.py:15
  70.1 2.6 copy.8
  72.7 0.0 all-gather.2.cloned.1.call-update
  72.7 0.0 all-reduce.3.cloned.1.call-start
  72.8 0.0 copy-done.3
  72.8 0.6 fusion.15
  74.8 42.4 %all-gather.2.cloned.1.call-done = bf16[1,640,4096]{2,1,0:T(8,128)(2,1)} async-done(((bf16[1,160,4096]{2,1,0:T(8,128)(2,1)}), bf16[1,640,4096]{2,1,0:T(8,128)(2,1)}) %all-gather.2.cloned.1.call-update) | async-done | bytes 5242896 | tf_op jit(solution)/shard_map/all_gather | solution.py:30
  117.2 7.0 select_bitcast_fusion
  124.2 0.0 copy-start.1
  124.2 0.0 copy-start.2
  124.2 0.0 copy-start
  124.2 0.0 all-reduce.3.cloned.1.call-update
  128.4 0.0 copy-done.1
  128.4 0.7 fusion.14
  131.2 0.0 copy-done.2
  131.2 0.7 fusion.13
  131.8 0.0 copy-done
  131.9 0.7 dynamic-slice_subtract_fusion.2
  132.6 1.4 dynamic-slice_subtract_fusion
  134.0 639.6 %all-reduce.3.cloned.1.call-done = (bf16[640,4096]{1,0:T(8,128)(2,1)}, bf16[640,4096]{1,0:T(8,128)(2,1)}) async-done(((bf16[640,4096]{1,0:T(8,128)(2,1)}, bf16[640,4096]{1,0:T(8,128)(2,1)}), (bf16[640,4096]{1,0:T(8,128)(2,1)}, bf16[640,4096]{1,0:T(8,128)(2,1)})) %all-reduce.3.cloned.1.call-update) | async-done | bytes 10485776 | tf_op jit(solution)/shard_map/psum | solution.py:11
  773.6 9.1 %fusion.6 = f32[160,4096]{1,0:T(8,128)} fusion(bf16[640,4096]{1,0:T(8,128)(2,1)} %get-tuple-element.5, bf16[160,4096]{0,1:T(8,128)(2,1)S(1)} %bitcast.48, f32[640]{0:T(1024)S(1)} %get-tuple-element.10, f32[160]{0:T(256)S(1)} %dynamic-slice_subtract_fusion.2), kind=kOutput, calls=%fused_computation.11 | convolution fusion | flops 1678028800 | bytes 9178240 | tf_op jit(solution)/shard_map/dot_general | solution.py:40
  782.6 9.3 %fusion.1 = bf16[1,160,4096]{2,1,0:T(8,128)(2,1)} fusion(f32[160,4096]{1,0:T(8,128)} %fusion.6, bf16[640,4096]{1,0:T(8,128)(2,1)} %get-tuple-element.6, bf16[160,4096]{0,1:T(8,128)(2,1)S(1)} %bitcast.49, f32[640]{0:T(1024)S(1)} %get-tuple-element.9, f32[160]{0:T(256)S(1)} %dynamic-slice_subtract_fusion.2), kind=kOutput, calls=%fused_computation.4 | convolution fusion | flops 1679339520 | bytes 10488960 | tf_op jit(solution)/shard_map/dot_general | solution.py:40
Async XLA Ops:
  6.5 66.2 %copy-start.3 = (s32[2]{0:T(128)S(1)}, s32[2]{0:T(128)}, u32[]{:S(2)}) copy-start(s32[2]{0:T(128)} %param.9) | copy-start | bytes 28
  6.5 110.7 %all-gather.2.cloned.1.call-start = ((), (), s32[]{:S(2)}) async-start(), calls=%async_computation.1 | async-start | bytes 6553600 | tf_op jit(solution)/shard_map/all_gather | solution.py:30
  72.7 700.9 %all-reduce.3.cloned.1.call-start = ((), (), s32[]{:S(2)}) async-start(), calls=%async_computation.2 | async-start | bytes 20971520 | tf_op jit(solution)/shard_map/psum | solution.py:11
  124.2 4.1 copy-start.1
  124.2 6.9 copy-start.2
  124.2 7.6 copy-start
Sparse Core Ops, SparseCore 0:
  72.8 44.3 all-gather.1
  124.4 649.1 all-reduce.2
where the time goes:
time: 799 us
  waiting for transfers between devices  682 us (85%)
  blocking collectives  63.5 us (8%)
  between operations  21 us (3%)
  matrix products  18.3 us (2%)
  other arithmetic  9.16 us (1%)
    psum x1, waiting for transfers between devices, spread(): return lax.psum(block, axis)  640 us
    all_to_all x1, blocking collectives, on_device(): lax.all_to_all(three_centre, 'occ', split_axis=0, concat_axis=2, tiled=True)  63.5 us
    all_gather x1, waiting for transfers between devices, on_device(): full_block = lax.all_gather(my_block, 'slab', axis=1, tiled=True)  42.4 us
    dot_general x2, matrix products, on_device(): jnp.dot(amplitude, sent_block[0], preferred_element_type=jnp.float32)  18.3 us
  transfers between devices with their start and end apart: 2, of which 2 were waited for; matrix products, arithmetic and copies ran while one was open for 1% of the time, Pallas kernels for 0%

commit v1 on v0

v1 whole, which is shorter than its diff:
```python
import functools

import jax
import jax.numpy as jnp
from jax import lax
from jax.experimental import pallas as pl
from jax.experimental.pallas import tpu as pltpu
from jax.sharding import PartitionSpec as P

ROUNDS = 2
NZ, NX, NY, NC = 8, 4, 4, 2
XY = 8
COLS = 64
ROWS = 160
TAIL = ROWS - 128
PACKED = COLS + COLS * TAIL // 128
GROUPS = 128 // TAIL
GROUP_COLS = COLS // GROUPS
BOTH = ("occ", "slab")
VMEM_LIMIT = 48 * 1024 * 1024


def index(z, x, y, core):
    return ((z % NZ) * XY + (x % 2) * NY + y % NY) * 4 + (x % NX) // 2 * 2 + core


def fetch(block, dz=0, dx=0, dy=0, swap=0):
    pairs = [
        (index(z + dz, x + dx, y + dy, core ^ swap), index(z, x, y, core))
        for z in range(NZ) for x in range(NX) for y in range(NY) for core in range(NC)
    ]
    return lax.ppermute(block, BOTH, pairs)


def pack_piece(piece):
    tail = piece[:, 128:]
    tail = [tail[g * GROUP_COLS:(g + 1) * GROUP_COLS] for g in range(GROUPS)]
    return piece[:, :128], jnp.concatenate(tail, axis=1)


def pack_rounds_kernel(order, piece, out):
    main, tail = pack_piece(piece[0])
    out[0, :COLS] = main
    out[0, COLS:] = tail


def pack_all_kernel(pieces, out):
    for b in range(pieces.shape[0]):
        main, tail = pack_piece(pieces[b])
        out[b, :COLS] = main
        out[b, COLS:] = tail


def pack_rounds(columns, round_order):
    return pl.pallas_call(
        pack_rounds_kernel,
        grid_spec=pltpu.PrefetchScalarGridSpec(
            num_scalar_prefetch=1,
            grid=(ROUNDS,),
            in_specs=[pl.BlockSpec((1, COLS, ROWS), lambda k, order: (order[k], 0, 0))],
            out_specs=pl.BlockSpec((1, PACKED, 128), lambda k, order: (k, 0, 0)),
        ),
        out_shape=jax.ShapeDtypeStruct((ROUNDS, PACKED, 128), jnp.bfloat16),
    )(round_order, columns)


def pack_all(columns):
    blocks = columns.shape[0]
    step = 16
    return pl.pallas_call(
        pack_all_kernel,
        grid=(blocks // step,),
        in_specs=[pl.BlockSpec((step, COLS, ROWS), lambda b: (b, 0, 0))],
        out_specs=pl.BlockSpec((step, PACKED, 128), lambda b: (b, 0, 0)),
        out_shape=jax.ShapeDtypeStruct((blocks, PACKED, 128), jnp.bfloat16),
    )(columns)


def rows_kernel(place, packed, out):
    for dz in range(NZ):
        plane = lax.rem(place[0] + dz, NZ)
        block = packed[pl.ds(plane * XY, XY)]
        span = pl.ds(dz * XY * COLS, XY * COLS)
        out[:128, span] = block[:, :COLS].reshape(XY * COLS, 128).T
        tail = block[:, COLS:].astype(jnp.float32).reshape(XY * GROUP_COLS, 128)
        groups = [tail if g == 0 else pltpu.roll(tail, 128 - TAIL * g, 1) for g in range(GROUPS)]
        groups = [v.reshape(XY, 1, GROUP_COLS, 128) for v in groups]
        tail = jnp.concatenate(groups, axis=1).reshape(XY * COLS, 128)
        out[128:, span] = tail.T[:TAIL].astype(jnp.bfloat16)


def unpack_rows(place, packed):
    return pl.pallas_call(
        rows_kernel,
        in_specs=[pl.BlockSpec(memory_space=pltpu.SMEM), pl.BlockSpec(memory_space=pltpu.VMEM)],
        out_specs=pl.BlockSpec(memory_space=pltpu.VMEM),
        out_shape=jax.ShapeDtypeStruct((ROWS, NZ * XY * COLS), jnp.bfloat16),
        compiler_params=pltpu.CompilerParams(vmem_limit_bytes=VMEM_LIMIT),
    )(place, packed)


def gamma_kernel(layout, place, rows, left_gap, right_gap, *rest):
    count = len(layout)
    pieces, (out, weights, tails, amplitude, sems) = rest[:count], rest[count:]
    my_x, my_y, my_core = place[1], place[2], place[3]
    copies = []
    for piece, (k, along, dx, dy, swap, first) in zip(pieces, layout):
        for step in range(piece.shape[0]):
            x = lax.rem(my_x + dx + (first + step if along == "x" else 0), NX)
            y = lax.rem(my_y + dy + (first + step if along == "y" else 0), NY)
            core = 1 - my_core if swap else my_core
            spot = lax.rem(x, 2) * NY + y
            slab = lax.div(x, 2) * NC + core
            copies.append(pltpu.make_async_copy(
                piece.at[step, :, pl.ds(0, COLS)], weights.at[k * 4 + slab, :, spot], sems.at[0]))
            copies.append(pltpu.make_async_copy(
                piece.at[step, :, pl.ds(COLS, PACKED - COLS)], tails.at[k, slab, :, spot], sems.at[0]))
    for copy in copies:
        copy.start()
    for copy in copies:
        copy.wait()
    depth = NZ * XY * COLS
    source = lax.broadcasted_iota(jnp.int32, (4 * 128, 4 * 128), 0)
    target = lax.broadcasted_iota(jnp.int32, (4 * 128, 4 * 128), 1)
    moved = (source // TAIL % GROUPS) * 128 + source // 128 * TAIL + source % TAIL
    shuffle = jnp.where(moved == target, 1.0, 0.0).astype(jnp.bfloat16)
    for k in range(ROUNDS):
        lanes = [tails[k, s].reshape(NZ * XY * GROUP_COLS, 128) for s in range(4)]
        swapped = jnp.dot(jnp.concatenate(lanes, axis=1), shuffle, preferred_element_type=jnp.float32)
        swapped = swapped.astype(jnp.bfloat16)
        for g in range(GROUPS):
            part = swapped[:, g * 128:(g + 1) * 128].reshape(NZ, XY, GROUP_COLS, 128)
            weights[4 * ROUNDS + k, :, :, g * GROUP_COLS:(g + 1) * GROUP_COLS] = part
    tiles = 5 * ROUNDS
    for t in range(0, tiles, 2):
        pair = [weights[u].reshape(depth, 128) for u in (t, t + 1)]
        span = slice(t * 128, (t + 2) * 128)
        product = jnp.dot(rows[...], jnp.concatenate(pair, axis=1), preferred_element_type=jnp.float32)
        amplitude[:, span] = (product / (left_gap[...] + right_gap[:, span])).astype(jnp.bfloat16)
    for dz in range(NZ):
        plane = lax.rem(place[0] + dz, NZ)
        part = [weights[u, dz].reshape(XY * COLS, 128) for u in range(tiles)]
        part = lax.dot_general(
            amplitude[...], jnp.concatenate(part, axis=1), (((1,), (1,)), ((), ())),
            preferred_element_type=jnp.float32)
        out[:, pl.ds(pl.multiple_of(plane * (XY * COLS), XY * COLS), XY * COLS)] = part.astype(jnp.bfloat16)


def gamma(place, rows, left_gap, right_gap, pieces, layout):
    vmem = pl.BlockSpec(memory_space=pltpu.VMEM)
    return pl.pallas_call(
        functools.partial(gamma_kernel, layout),
        in_specs=[pl.BlockSpec(memory_space=pltpu.SMEM)] + [vmem] * 3
        + [pl.BlockSpec(memory_space=pl.ANY)] * len(pieces),
        out_specs=vmem,
        out_shape=jax.ShapeDtypeStruct((ROWS, NZ * XY * COLS), jnp.bfloat16),
        scratch_shapes=[
            pltpu.VMEM((5 * ROUNDS, NZ, XY, COLS, 128), jnp.bfloat16),
            pltpu.VMEM((ROUNDS, 4, NZ, XY, GROUP_COLS, 128), jnp.bfloat16),
            pltpu.VMEM((ROWS, 5 * ROUNDS * 128), jnp.bfloat16),
            pltpu.SemaphoreType.DMA((1,)),
        ],
        compiler_params=pltpu.CompilerParams(vmem_limit_bytes=VMEM_LIMIT),
    )(place, rows, left_gap, right_gap, *pieces)


def on_device(three_centre, eps_occ, eps_vir, block_owner, round_order):
    columns = jnp.swapaxes(three_centre, 1, 2)
    vir_count = eps_vir.shape[0]
    block_span = 4 * ROWS

    occ, slab = lax.axis_index("occ"), lax.axis_index("slab")
    place = jnp.stack([occ // XY, slab // 2 * 2 + occ // NY % 2, occ % NY, slab % 2]).astype(jnp.int32)

    own = pack_rounds(columns, round_order)
    pair = jnp.stack([own, fetch(own, dz=1)])
    far = [fetch(pair, dz=d) for d in (2, 4, 6)]
    line = jnp.concatenate([pair] + far)

    packed = pack_all(columns)
    packed = lax.all_to_all(packed, "occ", split_axis=0, concat_axis=0, tiled=True)

    pieces, layout = [], []

    def keep(array, *where):
        pieces.append(array)
        layout.append((where[0], where[1], where[2], where[3], 0, where[4]))
        pieces.append(fetch(array, swap=1))
        layout.append((where[0], where[1], where[2], where[3], 1, where[4]))

    for k, first, second in ((0, "y", "x"), (1, "x", "y")):
        mine = line[:, k]
        d1, d2 = "d" + first, "d" + second

        def spot(d):
            return (d, 0) if second == "x" else (0, d)

        face = jnp.stack([mine] + [fetch(mine, **{d1: d}) for d in (1, 2, 3)])
        keep(face, k, first, *spot(0), 0)
        ahead, behind = fetch(face, **{d2: 1}), fetch(face, **{d2: 3})
        keep(ahead, k, first, *spot(1), 0)
        keep(behind, k, first, *spot(3), 0)
        keep(fetch(ahead[:2], **{d2: 1}), k, first, *spot(2), 0)
        keep(fetch(behind[2:], **{d2: 3}), k, first, *spot(2), 2)

    def energies(owner_slot, row_offset, span_rows):
        first_pair = block_owner[owner_slot] * block_span + row_offset
        occ_level = lax.dynamic_slice_in_dim(eps_occ, first_pair // vir_count, 1)
        vir_level = lax.dynamic_slice_in_dim(eps_vir, first_pair % vir_count, span_rows)
        return occ_level - vir_level

    left_gap = energies(occ, slab * ROWS, ROWS)[:, None]
    right = jnp.stack([energies(round_order[k], 0, block_span) for k in range(ROUNDS)])
    right = right.reshape(ROUNDS, 4, ROWS)
    right_gap = jnp.concatenate([right[:, :, :128].reshape(1, -1), right[:, :, 128:].reshape(1, -1)], axis=1)

    rows = unpack_rows(place, packed)
    return gamma(place, rows, left_gap, right_gap, pieces, tuple(layout))[None]


def solution(mesh):
    in_specs = (P(None, "slab", "occ"), P(), P(), P(), P())
    out_specs = P("occ", "slab", None)
    return jax.shard_map(
        on_device, mesh=mesh, in_specs=in_specs, out_specs=out_specs, check_vma=False
    )
```

time: 799 us -> 139 us (0.17)
  the two profiles are of different devices: /device:TPU:8 before, /device:TPU:1 now
where the time goes in v1:
time: 139 us; the launch traced here: 138 us
  waiting for transfers between devices  52 us (37%)
  starting transfers between devices  50 us (36%)
  Pallas kernels  20.3 us (15%)
  between operations  6.24 us (4%)
  local copies, waits for them, and re-layouts  5.96 us (4%)
  other arithmetic  3.01 us (2%)
    ppermute x28, waiting for transfers between devices, fetch(): return lax.ppermute(block, BOTH, pairs)  52 us
    ppermute x28, starting transfers between devices, fetch(): return lax.ppermute(block, BOTH, pairs)  36.4 us
    all_to_all x1, starting transfers between devices, on_device(): lax.all_to_all(packed, 'occ', split_axis=0, concat_axis=0, tiled=True)  13.6 us
    pallas_call x1, Pallas kernels, gamma(): pl.pallas_call(functools.partial(gamma_kernel, layout), in_specs=[pl.Bloc...  12.5 us
    pallas_call x1, Pallas kernels, pack_all(): pl.pallas_call(pack_all_kernel, grid=(blocks // step,), in_specs=[pl.Bloc...  3.84 us
  transfers between devices with their start and end apart: 29, of which 11 were waited for; matrix products, arithmetic and copies ran while one was open for 6% of the time, Pallas kernels for 3%

profile of v1, /device:TPU:1, one launch (start us, length us, event | category | flops | bytes accessed | tf_op | source)
XLA Modules:
  0.0 137.5 jit_solution(13381819667355020918)
XLA Ops:
  0.0 3.8 %shard_map.55 = bf16[64,80,128]{2,1,0:T(8,128)(2,1)} custom-call(bf16[64,64,160]{2,1,0:T(8,128)(2,1)} %bitcast.38), custom_call_target="tpu_custom_call" | custom-call | tf_op jit(solution)/shard_map/pallas_call | solution.py:70
  3.8 13.6 %all-to-all-start = ((bf16[64,80,128]{2,1,0:T(8,128)(2,1)}), bf16[64,80,128]{2,1,0:T(8,128)(2,1)S(1)}, u32[]{:S(2)}, u32[]{:S(2)}) async-start(bf16[64,80,128]{2,1,0:T(8,128)(2,1)} %shard_map.55), calls=%async_computation | async-start | bytes 2621440 | tf_op jit(solution)/shard_map/all_to_all | solution.py:181
  17.4 2.2 %shard_map.57 = bf16[2,80,128]{2,1,0:T(8,128)(2,1)} custom-call(s32[2]{0:T(128)} %order.1, bf16[64,64,160]{2,1,0:T(8,128)(2,1)} %bitcast.39), custom_call_target="tpu_custom_call" | custom-call | tf_op jit(solution)/shard_map/pallas_call | solution.py:55
  19.6 2.5 %collective-permute-start = (bf16[2,80,128]{2,1,0:T(8,128)(2,1)}, bf16[2,80,128]{2,1,0:T(8,128)(2,1)S(1)}, u32[]{:S(2)}, u32[]{:S(2)}) collective-permute-start(bf16[2,80,128]{2,1,0:T(8,128)(2,1)} %shard_map.57), channel_id=1, source_target_pairs={{32,0},{33,1},{36,4},{37,5},{40,8},{41,9},{44,12},{45,13},{48,16},... | collective-permute-start | bytes 122888 | tf_op jit(solution)/shard_map/ppermute | solution.py:32
  22.1 0.8 constant_dynamic-update-slice_fusion.6
  22.9 23.7 %collective-permute-done = bf16[2,80,128]{2,1,0:T(8,128)(2,1)S(1)} collective-permute-done((bf16[2,80,128]{2,1,0:T(8,128)(2,1)}, bf16[2,80,128]{2,1,0:T(8,128)(2,1)S(1)}, u32[]{:S(2)}, u32[]{:S(2)}) %collective-permute-start) | collective-permute-done | bytes 40992 | tf_op jit(solution)/shard_map/ppermute | solution.py:32
  46.6 0.8 pad_maximum_fusion.2
  47.4 3.5 %collective-permute-start.1 = (bf16[2,2,80,128]{3,2,0,1:T(8,128)(2,1)S(1)}, bf16[2,2,80,128]{3,2,0,1:T(8,128)(2,1)S(1)}, u32[]{:S(2)}, u32[]{:S(2)}) collective-permute-start(bf16[2,2,80,128]{3,2,0,1:T(8,128)(2,1)S(1)} %pad_maximum_fusion.2), channel_id=1, source_target_pairs={{64,0},{65,1},{68,4},{69,5},{72,8},{73,9},{76,12},{77,13},{80,16},... | collective-permute-start | bytes 245768 | tf_op jit(solution)/shard_map/ppermute | solution.py:32
  50.9 1.8 %collective-permute-start.2 = (bf16[2,2,80,128]{3,2,0,1:T(8,128)(2,1)S(1)}, bf16[2,2,80,128]{3,2,0,1:T(8,128)(2,1)S(1)}, u32[]{:S(2)}, u32[]{:S(2)}) collective-permute-start(bf16[2,2,80,128]{3,2,0,1:T(8,128)(2,1)S(1)} %pad_maximum_fusion.2), channel_id=1, source_target_pairs={{128,0},{129,1},{132,4},{133,5},{136,8},{137,9},{140,12},{141,13},... | collective-permute-start | bytes 245768 | tf_op jit(solution)/shard_map/ppermute | solution.py:32
  52.7 2.3 %collective-permute-start.3 = (bf16[2,2,80,128]{3,2,0,1:T(8,128)(2,1)S(1)}, bf16[2,2,80,128]{3,2,0,1:T(8,128)(2,1)S(1)}, u32[]{:S(2)}, u32[]{:S(2)}) collective-permute-start(bf16[2,2,80,128]{3,2,0,1:T(8,128)(2,1)S(1)} %pad_maximum_fusion.2), channel_id=1, source_target_pairs={{192,0},{193,1},{196,4},{197,5},{200,8},{201,9},{204,12},{205,13},... | collective-permute-start | bytes 245768 | tf_op jit(solution)/shard_map/ppermute | solution.py:32
  55.0 3.2 %collective-permute-done.2 = bf16[2,2,80,128]{3,2,0,1:T(8,128)(2,1)S(1)} collective-permute-done((bf16[2,2,80,128]{3,2,0,1:T(8,128)(2,1)S(1)}, bf16[2,2,80,128]{3,2,0,1:T(8,128)(2,1)S(1)}, u32[]{:S(2)}, u32[]{:S(2)}) %collective-permute-start.2) | collective-permute-done | bytes 81952 | tf_op jit(solution)/shard_map/ppermute | solution.py:32
  58.2 1.8 %collective-permute-done.3 = bf16[2,2,80,128]{3,2,0,1:T(8,128)(2,1)S(1)} collective-permute-done((bf16[2,2,80,128]{3,2,0,1:T(8,128)(2,1)S(1)}, bf16[2,2,80,128]{3,2,0,1:T(8,128)(2,1)S(1)}, u32[]{:S(2)}, u32[]{:S(2)}) %collective-permute-start.3) | collective-permute-done | bytes 81952 | tf_op jit(solution)/shard_map/ppermute | solution.py:32
  60.1 3.9 %collective-permute-start.16 = (bf16[8,80,128]{2,1,0:T(8,128)(2,1)S(1)}, bf16[8,80,128]{2,1,0:T(8,128)(2,1)S(1)}, u32[]{:S(2)}, u32[]{:S(2)}) collective-permute-start(bf16[8,80,128]{2,1,0:T(8,128)(2,1)S(1)} %get-tuple-element.7), channel_id=1, source_target_pairs={{16,0},{17,1},{20,4},{21,5},{24,8},{25,9},{28,12},{29,13},{2,16},{... | collective-permute-start | bytes 491528 | tf_op jit(solution)/shard_map/ppermute | solution.py:32
  64.0 0.5 collective-permute-start.17
  64.5 0.2 collective-permute-start.18
  64.6 2.3 %collective-permute-start.4 = (bf16[8,80,128]{2,1,0:T(8,128)(2,1)S(1)}, bf16[8,80,128]{2,1,0:T(8,128)(2,1)S(1)}, u32[]{:S(2)}, u32[]{:S(2)}) collective-permute-start(bf16[8,80,128]{2,1,0:T(8,128)(2,1)S(1)} %get-tuple-element.6), channel_id=1, source_target_pairs={{4,0},{5,1},{8,4},{9,5},{12,8},{13,9},{0,12},{1,13},{20,16},{21,17... | collective-permute-start | bytes 491528 | tf_op jit(solution)/shard_map/ppermute | solution.py:32
  66.9 0.8 collective-permute-start.5
  67.8 0.4 collective-permute-done.16
  68.1 0.5 collective-permute-start.6
  68.6 1.1 collective-permute-done.17
  69.7 4.6 %collective-permute-done.18 = bf16[8,80,128]{2,1,0:T(8,128)(2,1)S(1)} collective-permute-done((bf16[8,80,128]{2,1,0:T(8,128)(2,1)S(1)}, bf16[8,80,128]{2,1,0:T(8,128)(2,1)S(1)}, u32[]{:S(2)}, u32[]{:S(2)}) %collective-permute-start.18) | collective-permute-done | bytes 163872 | tf_op jit(solution)/shard_map/ppermute | solution.py:32
  74.5 2.7 %collective-permute-start.20 = (bf16[4,8,80,128]{3,2,1,0:T(8,128)(2,1)S(1)}, bf16[4,8,80,128]{3,2,1,0:T(8,128)(2,1)S(1)}, u32[]{:S(2)}, u32[]{:S(2)}) collective-permute-start(bf16[4,8,80,128]{3,2,1,0:T(8,128)(2,1)S(1)} %pad_maximum_fusion.1.rest_10_), channel_id=1, source_target_pairs={{4,0},{5,1},{8,4},{9,5},{12,8},{13,9},{0,12},{1,13},{20,16},{21,17... | collective-permute-start | bytes 1966088 | tf_op jit(solution)/shard_map/ppermute | solution.py:32
  77.3 3.0 %collective-permute-start.8 = (bf16[4,8,80,128]{3,2,1,0:T(8,128)(2,1)S(1)}, bf16[4,8,80,128]{3,2,1,0:T(8,128)(2,1)S(1)}, u32[]{:S(2)}, u32[]{:S(2)}) collective-permute-start(bf16[4,8,80,128]{3,2,1,0:T(8,128)(2,1)S(1)} %pad_maximum_fusion.rest_0_), channel_id=1, source_target_pairs={{16,0},{17,1},{20,4},{21,5},{24,8},{25,9},{28,12},{29,13},{2,16},{... | collective-permute-start | bytes 1966088 | tf_op jit(solution)/shard_map/ppermute | solution.py:32
  80.3 3.5 %collective-permute-start.19 = (bf16[4,8,80,128]{3,2,1,0:T(8,128)(2,1)S(1)}, bf16[4,8,80,128]{3,2,1,0:T(8,128)(2,1)S(1)}, u32[]{:S(2)}, u32[]{:S(2)}) collective-permute-start(bf16[4,8,80,128]{3,2,1,0:T(8,128)(2,1)S(1)} %pad_maximum_fusion.1.rest_10_), channel_id=1, source_target_pairs={{1,0},{0,1},{5,4},{4,5},{9,8},{8,9},{13,12},{12,13},{17,16},{16,17... | collective-permute-start | bytes 1966088 | tf_op jit(solution)/shard_map/ppermute | solution.py:32
  83.9 6.5 %collective-permute-done.20.rest_12_ = bf16[4,8,80,128]{3,2,1,0:T(8,128)(2,1)S(1)} collective-permute-done((bf16[4,8,80,128]{3,2,1,0:T(8,128)(2,1)S(1)}, bf16[4,8,80,128]{3,2,1,0:T(8,128)(2,1)S(1)}, u32[]{:S(2)}, u32[]{:S(2)}) %collective-permute-start.20) | collective-permute-done | bytes 655392 | tf_op jit(solution)/shard_map/ppermute | solution.py:32
  90.3 1.8 %collective-permute-start.7 = (bf16[4,8,80,128]{3,2,1,0:T(8,128)(2,1)S(1)}, bf16[4,8,80,128]{3,2,1,0:T(8,128)(2,1)}, u32[]{:S(2)}, u32[]{:S(2)}) collective-permute-start(bf16[4,8,80,128]{3,2,1,0:T(8,128)(2,1)S(1)} %pad_maximum_fusion.rest_0_), channel_id=1, source_target_pairs={{1,0},{0,1},{5,4},{4,5},{9,8},{8,9},{13,12},{12,13},{17,16},{16,17... | collective-permute-start | bytes 1966088 | tf_op jit(solution)/shard_map/ppermute | solution.py:32
  92.2 1.3 collective-permute-done.22.rest_14_
  93.4 2.2 %collective-permute-start.24 = (bf16[2,8,80,128]{3,2,1,0:T(8,128)(2,1)S(1)}, bf16[2,8,80,128]{3,2,1,0:T(8,128)(2,1)}, u32[]{:S(2)}, u32[]{:S(2)}) collective-permute-start(bf16[2,8,80,128]{3,2,1,0:T(8,128)(2,1)S(1)} %slice.46), channel_id=1, source_target_pairs={{4,0},{5,1},{8,4},{9,5},{12,8},{13,9},{0,12},{1,13},{20,16},{21,17... | collective-permute-start | bytes 983048 | tf_op jit(solution)/shard_map/ppermute | solution.py:32
  95.8 0.8 slice.43
  96.6 0.8 slice.44
  97.4 1.5 %collective-permute-start.14 = (bf16[2,8,80,128]{3,2,1,0:T(8,128)(2,1)}, bf16[2,8,80,128]{3,2,1,0:T(8,128)(2,1)}, u32[]{:S(2)}, u32[]{:S(2)}) collective-permute-start(bf16[2,8,80,128]{3,2,1,0:T(8,128)(2,1)} %slice.44), channel_id=1, source_target_pairs={{18,0},{19,1},{22,4},{23,5},{26,8},{27,9},{30,12},{31,13},{0,16},{... | collective-permute-start | bytes 983048 | tf_op jit(solution)/shard_map/ppermute | solution.py:32
  98.9 3.9 %collective-permute-done.24.rest_16_ = bf16[2,8,80,128]{3,2,1,0:T(8,128)(2,1)} collective-permute-done((bf16[2,8,80,128]{3,2,1,0:T(8,128)(2,1)S(1)}, bf16[2,8,80,128]{3,2,1,0:T(8,128)(2,1)}, u32[]{:S(2)}, u32[]{:S(2)}) %collective-permute-start.24) | collective-permute-done | bytes 327712 | tf_op jit(solution)/shard_map/ppermute | solution.py:32
  102.8 0.9 collective-permute-start.25
  103.7 2.4 %collective-permute-done.26.rest_18_ = bf16[2,8,80,128]{3,2,1,0:T(8,128)(2,1)} collective-permute-done((bf16[2,8,80,128]{3,2,1,0:T(8,128)(2,1)S(1)}, bf16[2,8,80,128]{3,2,1,0:T(8,128)(2,1)}, u32[]{:S(2)}, u32[]{:S(2)}) %collective-permute-start.26) | collective-permute-done | bytes 327712 | tf_op jit(solution)/shard_map/ppermute | solution.py:32
  106.1 1.1 collective-permute-start.27
  107.2 0.6 fusion.2
  111.7 0.7 fusion.1
  114.3 0.7 fusion
  114.9 1.3 dynamic-slice_subtract_fusion
  116.5 0.5 collective-permute-start.23
  117.1 0.4 collective-permute-start.9
  117.7 0.7 dynamic-slice_subtract_fusion.2
  118.5 0.1 copy.6.left_gap
  118.6 3.1 %collective-permute-done.13.rest_7_ = bf16[2,8,80,128]{3,2,1,0:T(8,128)(2,1)} collective-permute-done((bf16[2,8,80,128]{3,2,1,0:T(8,128)(2,1)}, bf16[2,8,80,128]{3,2,1,0:T(8,128)(2,1)}, u32[]{:S(2)}, u32[]{:S(2)}) %collective-permute-start.13) | collective-permute-done | bytes 327712 | tf_op jit(solution)/shard_map/ppermute | solution.py:32
  121.7 0.1 collective-permute-start.15
  121.9 1.7 %shard_map.56.rows = bf16[160,4096]{1,0:T(8,128)(2,1)S(1)} custom-call(s32[4]{0:T(128)S(1)} %pad_add_fusion.place, bf16[64,80,128]{2,1,0:T(8,128)(2,1)S(1)} %all-to-all-done.packed), custom_call_target="tpu_custom_call" | custom-call | tf_op jit(solution)/shard_map/pallas_call | solution.py:93
  123.7 1.1 copy-done
  124.8 12.5 %shard_map.58 = bf16[160,4096]{1,0:T(8,128)(2,1)} custom-call(s32[4]{0:T(128)S(1)} %pad_add_fusion.place, bf16[160,4096]{1,0:T(8,128)(2,1)} %copy-done, f32[160,1]{1,0:T(8,128)S(1)} %copy.6.left_gap, f32[1,1280]{1,0:T(1,128)S(1)} %pad_maximum_fusion.3.right_gap, bf16[4,8,80,128]{3,2,1,0:T(8,128)(2,1)S(1)} %pad_maximum_fusion.rest_0_, ...), custom_call_target="tpu_custom_call" | custom-call | tf_op jit(solution)/shard_map/pallas_call | solution.py:151
  (60 shorter events, 1.2 us)
Async XLA Ops:
  3.8 118.1 %all-to-all-start = ((bf16[64,80,128]{2,1,0:T(8,128)(2,1)}), bf16[64,80,128]{2,1,0:T(8,128)(2,1)S(1)}, u32[]{:S(2)}, u32[]{:S(2)}) async-start(bf16[64,80,128]{2,1,0:T(8,128)(2,1)} %shard_map.55), calls=%async_computation | async-start | bytes 2621440 | tf_op jit(solution)/shard_map/all_to_all | solution.py:181
  19.6 27.0 %collective-permute-start = (bf16[2,80,128]{2,1,0:T(8,128)(2,1)}, bf16[2,80,128]{2,1,0:T(8,128)(2,1)S(1)}, u32[]{:S(2)}, u32[]{:S(2)}) collective-permute-start(bf16[2,80,128]{2,1,0:T(8,128)(2,1)} %shard_map.57), channel_id=1, source_target_pairs={{32,0},{33,1},{36,4},{37,5},{40,8},{41,9},{44,12},{45,13},{48,16},... | collective-permute-start | bytes 122888 | tf_op jit(solution)/shard_map/ppermute | solution.py:32
  47.4 7.6 %collective-permute-start.1 = (bf16[2,2,80,128]{3,2,0,1:T(8,128)(2,1)S(1)}, bf16[2,2,80,128]{3,2,0,1:T(8,128)(2,1)S(1)}, u32[]{:S(2)}, u32[]{:S(2)}) collective-permute-start(bf16[2,2,80,128]{3,2,0,1:T(8,128)(2,1)S(1)} %pad_maximum_fusion.2), channel_id=1, source_target_pairs={{64,0},{65,1},{68,4},{69,5},{72,8},{73,9},{76,12},{77,13},{80,16},... | collective-permute-start | bytes 245768 | tf_op jit(solution)/shard_map/ppermute | solution.py:32
  50.9 7.3 %collective-permute-start.2 = (bf16[2,2,80,128]{3,2,0,1:T(8,128)(2,1)S(1)}, bf16[2,2,80,128]{3,2,0,1:T(8,128)(2,1)S(1)}, u32[]{:S(2)}, u32[]{:S(2)}) collective-permute-start(bf16[2,2,80,128]{3,2,0,1:T(8,128)(2,1)S(1)} %pad_maximum_fusion.2), channel_id=1, source_target_pairs={{128,0},{129,1},{132,4},{133,5},{136,8},{137,9},{140,12},{141,13},... | collective-permute-start | bytes 245768 | tf_op jit(solution)/shard_map/ppermute | solution.py:32
  52.7 7.3 %collective-permute-start.3 = (bf16[2,2,80,128]{3,2,0,1:T(8,128)(2,1)S(1)}, bf16[2,2,80,128]{3,2,0,1:T(8,128)(2,1)S(1)}, u32[]{:S(2)}, u32[]{:S(2)}) collective-permute-start(bf16[2,2,80,128]{3,2,0,1:T(8,128)(2,1)S(1)} %pad_maximum_fusion.2), channel_id=1, source_target_pairs={{192,0},{193,1},{196,4},{197,5},{200,8},{201,9},{204,12},{205,13},... | collective-permute-start | bytes 245768 | tf_op jit(solution)/shard_map/ppermute | solution.py:32
  60.1 8.0 %collective-permute-start.16 = (bf16[8,80,128]{2,1,0:T(8,128)(2,1)S(1)}, bf16[8,80,128]{2,1,0:T(8,128)(2,1)S(1)}, u32[]{:S(2)}, u32[]{:S(2)}) collective-permute-start(bf16[8,80,128]{2,1,0:T(8,128)(2,1)S(1)} %get-tuple-element.7), channel_id=1, source_target_pairs={{16,0},{17,1},{20,4},{21,5},{24,8},{25,9},{28,12},{29,13},{2,16},{... | collective-permute-start | bytes 491528 | tf_op jit(solution)/shard_map/ppermute | solution.py:32
  64.0 5.8 %collective-permute-start.17 = (bf16[8,80,128]{2,1,0:T(8,128)(2,1)S(1)}, bf16[8,80,128]{2,1,0:T(8,128)(2,1)S(1)}, u32[]{:S(2)}, u32[]{:S(2)}) collective-permute-start(bf16[8,80,128]{2,1,0:T(8,128)(2,1)S(1)} %get-tuple-element.7), channel_id=1, source_target_pairs={{2,0},{3,1},{6,4},{7,5},{10,8},{11,9},{14,12},{15,13},{18,16},{19,... | collective-permute-start | bytes 491528 | tf_op jit(solution)/shard_map/ppermute | solution.py:32
  64.5 9.9 %collective-permute-start.18 = (bf16[8,80,128]{2,1,0:T(8,128)(2,1)S(1)}, bf16[8,80,128]{2,1,0:T(8,128)(2,1)S(1)}, u32[]{:S(2)}, u32[]{:S(2)}) collective-permute-start(bf16[8,80,128]{2,1,0:T(8,128)(2,1)S(1)} %get-tuple-element.7), channel_id=1, source_target_pairs={{18,0},{19,1},{22,4},{23,5},{26,8},{27,9},{30,12},{31,13},{0,16},{... | collective-permute-start | bytes 491528 | tf_op jit(solution)/shard_map/ppermute | solution.py:32
  64.6 12.6 %collective-permute-start.4 = (bf16[8,80,128]{2,1,0:T(8,128)(2,1)S(1)}, bf16[8,80,128]{2,1,0:T(8,128)(2,1)S(1)}, u32[]{:S(2)}, u32[]{:S(2)}) collective-permute-start(bf16[8,80,128]{2,1,0:T(8,128)(2,1)S(1)} %get-tuple-element.6), channel_id=1, source_target_pairs={{4,0},{5,1},{8,4},{9,5},{12,8},{13,9},{0,12},{1,13},{20,16},{21,17... | collective-permute-start | bytes 491528 | tf_op jit(solution)/shard_map/ppermute | solution.py:32
  66.9 10.2 %collective-permute-start.5 = (bf16[8,80,128]{2,1,0:T(8,128)(2,1)S(1)}, bf16[8,80,128]{2,1,0:T(8,128)(2,1)S(1)}, u32[]{:S(2)}, u32[]{:S(2)}) collective-permute-start(bf16[8,80,128]{2,1,0:T(8,128)(2,1)S(1)} %get-tuple-element.6), channel_id=1, source_target_pairs={{8,0},{9,1},{12,4},{13,5},{0,8},{1,9},{4,12},{5,13},{24,16},{25,17... | collective-permute-start | bytes 491528 | tf_op jit(solution)/shard_map/ppermute | solution.py:32
  68.1 9.1 %collective-permute-start.6 = (bf16[8,80,128]{2,1,0:T(8,128)(2,1)S(1)}, bf16[8,80,128]{2,1,0:T(8,128)(2,1)S(1)}, u32[]{:S(2)}, u32[]{:S(2)}) collective-permute-start(bf16[8,80,128]{2,1,0:T(8,128)(2,1)S(1)} %get-tuple-element.6), channel_id=1, source_target_pairs={{12,0},{13,1},{0,4},{1,5},{4,8},{5,9},{8,12},{9,13},{28,16},{29,17... | collective-permute-start | bytes 491528 | tf_op jit(solution)/shard_map/ppermute | solution.py:32
  74.5 21.2 %copy-start.1 = (bf16[4,8,80,128]{3,2,1,0:T(8,128)(2,1)}, bf16[4,8,80,128]{3,2,1,0:T(8,128)(2,1)S(1)}, u32[]{:S(2)}) copy-start(bf16[4,8,80,128]{3,2,1,0:T(8,128)(2,1)S(1)} %pad_maximum_fusion.1.rest_10_) | copy-start | bytes 1966084
  74.5 15.9 %collective-permute-start.20 = (bf16[4,8,80,128]{3,2,1,0:T(8,128)(2,1)S(1)}, bf16[4,8,80,128]{3,2,1,0:T(8,128)(2,1)S(1)}, u32[]{:S(2)}, u32[]{:S(2)}) collective-permute-start(bf16[4,8,80,128]{3,2,1,0:T(8,128)(2,1)S(1)} %pad_maximum_fusion.1.rest_10_), channel_id=1, source_target_pairs={{4,0},{5,1},{8,4},{9,5},{12,8},{13,9},{0,12},{1,13},{20,16},{21,17... | collective-permute-start | bytes 1966088 | tf_op jit(solution)/shard_map/ppermute | solution.py:32
  77.2 16.3 %collective-permute-start.22 = (bf16[4,8,80,128]{3,2,1,0:T(8,128)(2,1)S(1)}, bf16[4,8,80,128]{3,2,1,0:T(8,128)(2,1)S(1)}, u32[]{:S(2)}, u32[]{:S(2)}) collective-permute-start(bf16[4,8,80,128]{3,2,1,0:T(8,128)(2,1)S(1)} %pad_maximum_fusion.1.rest_10_), channel_id=1, source_target_pairs={{12,0},{13,1},{0,4},{1,5},{4,8},{5,9},{8,12},{9,13},{28,16},{29,17... | collective-permute-start | bytes 1966088 | tf_op jit(solution)/shard_map/ppermute | solution.py:32
  77.3 29.9 %copy-start.6 = (s32[2]{0:T(128)S(1)}, s32[2]{0:T(128)}, u32[]{:S(2)}) copy-start(s32[2]{0:T(128)} %order.1) | copy-start | bytes 28
  77.3 34.3 %copy-start.7 = (s32[64]{0:T(128)S(1)}, s32[64]{0:T(128)}, u32[]{:S(2)}) copy-start(s32[64]{0:T(128)} %param.8) | copy-start | bytes 772
  77.3 36.9 %copy-start.8 = (f32[16]{0:T(128)S(1)}, f32[16]{0:T(128)}, u32[]{:S(2)}) copy-start(f32[16]{0:T(128)} %param.6) | copy-start | bytes 196
  77.3 37.6 %copy-start.5 = (f32[2560]{0:T(1024)S(1)}, f32[2560]{0:T(1024)}, u32[]{:S(2)}) copy-start(f32[2560]{0:T(1024)} %param.7) | copy-start | bytes 30724
  77.3 18.4 %collective-permute-start.8 = (bf16[4,8,80,128]{3,2,1,0:T(8,128)(2,1)S(1)}, bf16[4,8,80,128]{3,2,1,0:T(8,128)(2,1)S(1)}, u32[]{:S(2)}, u32[]{:S(2)}) collective-permute-start(bf16[4,8,80,128]{3,2,1,0:T(8,128)(2,1)S(1)} %pad_maximum_fusion.rest_0_), channel_id=1, source_target_pairs={{16,0},{17,1},{20,4},{21,5},{24,8},{25,9},{28,12},{29,13},{2,16},{... | collective-permute-start | bytes 1966088 | tf_op jit(solution)/shard_map/ppermute | solution.py:32
  80.3 16.2 %collective-permute-start.10 = (bf16[4,8,80,128]{3,2,1,0:T(8,128)(2,1)S(1)}, bf16[4,8,80,128]{3,2,1,0:T(8,128)(2,1)S(1)}, u32[]{:S(2)}, u32[]{:S(2)}) collective-permute-start(bf16[4,8,80,128]{3,2,1,0:T(8,128)(2,1)S(1)} %pad_maximum_fusion.rest_0_), channel_id=1, source_target_pairs={{18,0},{19,1},{22,4},{23,5},{26,8},{27,9},{30,12},{31,13},{0,16},{... | collective-permute-start | bytes 1966088 | tf_op jit(solution)/shard_map/ppermute | solution.py:32
  80.3 17.0 %collective-permute-start.19 = (bf16[4,8,80,128]{3,2,1,0:T(8,128)(2,1)S(1)}, bf16[4,8,80,128]{3,2,1,0:T(8,128)(2,1)S(1)}, u32[]{:S(2)}, u32[]{:S(2)}) collective-permute-start(bf16[4,8,80,128]{3,2,1,0:T(8,128)(2,1)S(1)} %pad_maximum_fusion.1.rest_10_), channel_id=1, source_target_pairs={{1,0},{0,1},{5,4},{4,5},{9,8},{8,9},{13,12},{12,13},{17,16},{16,17... | collective-permute-start | bytes 1966088 | tf_op jit(solution)/shard_map/ppermute | solution.py:32
  90.3 7.0 %copy-start.2 = (bf16[4,8,80,128]{3,2,1,0:T(8,128)(2,1)}, bf16[4,8,80,128]{3,2,1,0:T(8,128)(2,1)S(1)}, u32[]{:S(2)}) copy-start(bf16[4,8,80,128]{3,2,1,0:T(8,128)(2,1)S(1)} %collective-permute-done.20.rest_12_) | copy-start | bytes 1966084
  90.3 26.0 %collective-permute-start.7 = (bf16[4,8,80,128]{3,2,1,0:T(8,128)(2,1)S(1)}, bf16[4,8,80,128]{3,2,1,0:T(8,128)(2,1)}, u32[]{:S(2)}, u32[]{:S(2)}) collective-permute-start(bf16[4,8,80,128]{3,2,1,0:T(8,128)(2,1)S(1)} %pad_maximum_fusion.rest_0_), channel_id=1, source_target_pairs={{1,0},{0,1},{5,4},{4,5},{9,8},{8,9},{13,12},{12,13},{17,16},{16,17... | collective-permute-start | bytes 1966088 | tf_op jit(solution)/shard_map/ppermute | solution.py:32
  93.4 5.4 %copy-start.3 = (bf16[4,8,80,128]{3,2,1,0:T(8,128)(2,1)}, bf16[4,8,80,128]{3,2,1,0:T(8,128)(2,1)S(1)}, u32[]{:S(2)}) copy-start(bf16[4,8,80,128]{3,2,1,0:T(8,128)(2,1)S(1)} %collective-permute-done.22.rest_14_) | copy-start | bytes 1966084
  93.4 9.4 %collective-permute-start.24 = (bf16[2,8,80,128]{3,2,1,0:T(8,128)(2,1)S(1)}, bf16[2,8,80,128]{3,2,1,0:T(8,128)(2,1)}, u32[]{:S(2)}, u32[]{:S(2)}) collective-permute-start(bf16[2,8,80,128]{3,2,1,0:T(8,128)(2,1)S(1)} %slice.46), channel_id=1, source_target_pairs={{4,0},{5,1},{8,4},{9,5},{12,8},{13,9},{0,12},{1,13},{20,16},{21,17... | collective-permute-start | bytes 983048 | tf_op jit(solution)/shard_map/ppermute | solution.py:32
  95.7 10.4 %collective-permute-start.26 = (bf16[2,8,80,128]{3,2,1,0:T(8,128)(2,1)S(1)}, bf16[2,8,80,128]{3,2,1,0:T(8,128)(2,1)}, u32[]{:S(2)}, u32[]{:S(2)}) collective-permute-start(bf16[2,8,80,128]{3,2,1,0:T(8,128)(2,1)S(1)} %slice.47), channel_id=1, source_target_pairs={{12,0},{13,1},{0,4},{1,5},{4,8},{5,9},{8,12},{9,13},{28,16},{29,17... | collective-permute-start | bytes 983048 | tf_op jit(solution)/shard_map/ppermute | solution.py:32
  96.6 19.9 %collective-permute-start.12 = (bf16[2,8,80,128]{3,2,1,0:T(8,128)(2,1)}, bf16[2,8,80,128]{3,2,1,0:T(8,128)(2,1)}, u32[]{:S(2)}, u32[]{:S(2)}) collective-permute-start(bf16[2,8,80,128]{3,2,1,0:T(8,128)(2,1)} %slice.43), channel_id=1, source_target_pairs={{16,0},{17,1},{20,4},{21,5},{24,8},{25,9},{28,12},{29,13},{2,16},{... | collective-permute-start | bytes 983048 | tf_op jit(solution)/shard_map/ppermute | solution.py:32
  97.4 5.4 %copy-start.4 = (bf16[4,8,80,128]{3,2,1,0:T(8,128)(2,1)}, bf16[4,8,80,128]{3,2,1,0:T(8,128)(2,1)S(1)}, u32[]{:S(2)}) copy-start(bf16[4,8,80,128]{3,2,1,0:T(8,128)(2,1)S(1)} %collective-permute-done.19.rest_11_) | copy-start | bytes 1966084
  97.4 19.6 %collective-permute-start.14 = (bf16[2,8,80,128]{3,2,1,0:T(8,128)(2,1)}, bf16[2,8,80,128]{3,2,1,0:T(8,128)(2,1)}, u32[]{:S(2)}, u32[]{:S(2)}) collective-permute-start(bf16[2,8,80,128]{3,2,1,0:T(8,128)(2,1)} %slice.44), channel_id=1, source_target_pairs={{18,0},{19,1},{22,4},{23,5},{26,8},{27,9},{30,12},{31,13},{0,16},{... | collective-permute-start | bytes 983048 | tf_op jit(solution)/shard_map/ppermute | solution.py:32
  102.8 14.3 %collective-permute-start.25 = (bf16[2,8,80,128]{3,2,1,0:T(8,128)(2,1)}, bf16[2,8,80,128]{3,2,1,0:T(8,128)(2,1)}, u32[]{:S(2)}, u32[]{:S(2)}) collective-permute-start(bf16[2,8,80,128]{3,2,1,0:T(8,128)(2,1)} %collective-permute-done.24.rest_16_), channel_id=1, source_target_pairs={{1,0},{0,1},{5,4},{4,5},{9,8},{8,9},{13,12},{12,13},{17,16},{16,17... | collective-permute-start | bytes 983048 | tf_op jit(solution)/shard_map/ppermute | solution.py:32
  106.1 11.4 %collective-permute-start.27 = (bf16[2,8,80,128]{3,2,1,0:T(8,128)(2,1)}, bf16[2,8,80,128]{3,2,1,0:T(8,128)(2,1)}, u32[]{:S(2)}, u32[]{:S(2)}) collective-permute-start(bf16[2,8,80,128]{3,2,1,0:T(8,128)(2,1)} %collective-permute-done.26.rest_18_), channel_id=1, source_target_pairs={{1,0},{0,1},{5,4},{4,5},{9,8},{8,9},{13,12},{12,13},{17,16},{16,17... | collective-permute-start | bytes 983048 | tf_op jit(solution)/shard_map/ppermute | solution.py:32
  116.4 8.4 %collective-permute-start.21 = (bf16[4,8,80,128]{3,2,1,0:T(8,128)(2,1)}, bf16[4,8,80,128]{3,2,1,0:T(8,128)(2,1)}, u32[]{:S(2)}, u32[]{:S(2)}) collective-permute-start(bf16[4,8,80,128]{3,2,1,0:T(8,128)(2,1)} %copy-done.2), channel_id=1, source_target_pairs={{1,0},{0,1},{5,4},{4,5},{9,8},{8,9},{13,12},{12,13},{17,16},{16,17... | collective-permute-start | bytes 1966088 | tf_op jit(solution)/shard_map/ppermute | solution.py:32
  116.5 8.3 %collective-permute-start.23 = (bf16[4,8,80,128]{3,2,1,0:T(8,128)(2,1)}, bf16[4,8,80,128]{3,2,1,0:T(8,128)(2,1)}, u32[]{:S(2)}, u32[]{:S(2)}) collective-permute-start(bf16[4,8,80,128]{3,2,1,0:T(8,128)(2,1)} %copy-done.3), channel_id=1, source_target_pairs={{1,0},{0,1},{5,4},{4,5},{9,8},{8,9},{13,12},{12,13},{17,16},{16,17... | collective-permute-start | bytes 1966088 | tf_op jit(solution)/shard_map/ppermute | solution.py:32
  117.0 7.8 %collective-permute-start.11 = (bf16[4,8,80,128]{3,2,1,0:T(8,128)(2,1)S(1)}, bf16[4,8,80,128]{3,2,1,0:T(8,128)(2,1)}, u32[]{:S(2)}, u32[]{:S(2)}) collective-permute-start(bf16[4,8,80,128]{3,2,1,0:T(8,128)(2,1)S(1)} %collective-permute-done.10.rest_4_), channel_id=1, source_target_pairs={{1,0},{0,1},{5,4},{4,5},{9,8},{8,9},{13,12},{12,13},{17,16},{16,17... | collective-permute-start | bytes 1966088 | tf_op jit(solution)/shard_map/ppermute | solution.py:32
  117.1 7.7 %collective-permute-start.9 = (bf16[4,8,80,128]{3,2,1,0:T(8,128)(2,1)S(1)}, bf16[4,8,80,128]{3,2,1,0:T(8,128)(2,1)}, u32[]{:S(2)}, u32[]{:S(2)}) collective-permute-start(bf16[4,8,80,128]{3,2,1,0:T(8,128)(2,1)S(1)} %collective-permute-done.8.rest_2_), channel_id=1, source_target_pairs={{1,0},{0,1},{5,4},{4,5},{9,8},{8,9},{13,12},{12,13},{17,16},{16,17... | collective-permute-start | bytes 1966088 | tf_op jit(solution)/shard_map/ppermute | solution.py:32
  117.5 4.2 %collective-permute-start.13 = (bf16[2,8,80,128]{3,2,1,0:T(8,128)(2,1)}, bf16[2,8,80,128]{3,2,1,0:T(8,128)(2,1)}, u32[]{:S(2)}, u32[]{:S(2)}) collective-permute-start(bf16[2,8,80,128]{3,2,1,0:T(8,128)(2,1)} %collective-permute-done.12.rest_6_), channel_id=1, source_target_pairs={{1,0},{0,1},{5,4},{4,5},{9,8},{8,9},{13,12},{12,13},{17,16},{16,17... | collective-permute-start | bytes 983048 | tf_op jit(solution)/shard_map/ppermute | solution.py:32
  121.7 3.1 %collective-permute-start.15 = (bf16[2,8,80,128]{3,2,1,0:T(8,128)(2,1)}, bf16[2,8,80,128]{3,2,1,0:T(8,128)(2,1)}, u32[]{:S(2)}, u32[]{:S(2)}) collective-permute-start(bf16[2,8,80,128]{3,2,1,0:T(8,128)(2,1)} %collective-permute-done.14.rest_8_), channel_id=1, source_target_pairs={{1,0},{0,1},{5,4},{4,5},{9,8},{8,9},{13,12},{12,13},{17,16},{16,17... | collective-permute-start | bytes 983048 | tf_op jit(solution)/shard_map/ppermute | solution.py:32
  123.7 1.1 copy-start

commit v2 on v0

v2 whole, which is shorter than its diff:
```python
import functools

import jax
import jax.numpy as jnp
from jax import lax
from jax.experimental import pallas as pl
from jax.experimental.pallas import tpu as pltpu
from jax.sharding import PartitionSpec as P

ROUNDS = 2
NZ, NX, NY, NC = 8, 4, 4, 2
XY = 8
COLS = 64
ROWS = 160
TAIL = ROWS - 128
PACKED = COLS + COLS * TAIL // 128
GROUPS = 128 // TAIL
GROUP_COLS = COLS // GROUPS
BOTH = ("occ", "slab")
LINE = 2 * COLS + COLS // 2
CHUNKS = 2
VMEM_LIMIT = 20 * 1024 * 1024


def index(z, x, y, core):
    return ((z % NZ) * XY + (x % 2) * NY + y % NY) * 4 + (x % NX) // 2 * 2 + core


def fetch(block, dz=0, first=0, second=0, swap=0):
    pairs = []
    for z in range(NZ):
        for x in range(NX):
            for y in range(NY):
                for core in range(NC):
                    dx, dy = (first, second) if core else (second, first)
                    pairs.append((index(z + dz, x + dx, y + dy, core ^ swap), index(z, x, y, core)))
    return lax.ppermute(block, BOTH, pairs)


def position():
    occ, slab = lax.axis_index("occ"), lax.axis_index("slab")
    return lax.div(occ, XY), lax.div(slab, 2) * 2 + lax.rem(lax.div(occ, NY), 2), lax.rem(occ, NY), lax.rem(slab, 2)


def pack_kernel(order, pieces, first, second, line, out):
    @pl.when(pl.program_id(0) == 0)
    def _():
        rounds = first[0], second[0]
        line[:COLS] = rounds[0][:, :128]
        line[COLS:2 * COLS] = rounds[1][:, :128]
        half = COLS // 2
        line[2 * COLS:] = jnp.concatenate([p[h:h + half, 128:] for h in (0, half) for p in rounds], axis=1)

    step = pieces.shape[0]
    for b in range(step):
        piece = pieces[b]
        z, spot = pl.program_id(0) * (step // XY) + b // XY, b % XY
        out[spot, z, :COLS] = piece[:, :128]
        tail = [piece[g * GROUP_COLS:(g + 1) * GROUP_COLS, 128:] for g in range(GROUPS)]
        out[spot, z, COLS:] = jnp.concatenate(tail, axis=1)


def pack(columns, round_order):
    blocks = columns.shape[0]
    step = 32
    return pl.pallas_call(
        pack_kernel,
        grid_spec=pltpu.PrefetchScalarGridSpec(
            num_scalar_prefetch=1,
            grid=(blocks // step,),
            in_specs=[
                pl.BlockSpec((step, COLS, ROWS), lambda i, order: (i, 0, 0)),
                pl.BlockSpec((1, COLS, ROWS), lambda i, order: (order[0], 0, 0)),
                pl.BlockSpec((1, COLS, ROWS), lambda i, order: (order[1], 0, 0)),
            ],
            out_specs=[
                pl.BlockSpec((LINE, 128), lambda i, order: (0, 0)),
                pl.BlockSpec((NZ, XY, PACKED, 128), lambda i, order: (0, 0, 0, 0)),
            ],
        ),
        out_shape=[
            jax.ShapeDtypeStruct((LINE, 128), jnp.bfloat16),
            jax.ShapeDtypeStruct((NZ, XY, PACKED, 128), jnp.bfloat16),
        ],
        compiler_params=pltpu.CompilerParams(vmem_limit_bytes=VMEM_LIMIT),
    )(round_order, columns, columns, columns)


def exchange(packed, planes):
    groups = [[m * XY + o if planes else o * XY + m for m in range(8)] for o in range(8)]
    return lax.all_to_all(packed, "occ", split_axis=0, concat_axis=0, axis_index_groups=groups, tiled=True)


def rows_kernel(owner, order, eps_occ, eps_vir, packed, out, left_gap, right_gap):
    span = 4 * ROWS
    vir_blocks = eps_vir.shape[1] // span

    def energies(slot):
        block = owner[slot]
        start = pl.multiple_of(lax.rem(block, vir_blocks) * span, 128)
        return eps_occ[lax.div(block, vir_blocks)] - eps_vir[:, pl.ds(start, span)]

    mine = energies(lax.axis_index("occ"))
    left = mine[:, :ROWS]
    for s in range(1, 4):
        left = jnp.where(lax.axis_index("slab") == s, mine[:, s * ROWS:(s + 1) * ROWS], left)
    left = jnp.concatenate([left, jnp.zeros((1, 256 - ROWS), jnp.float32)], axis=1)
    left_gap[...] = jnp.broadcast_to(left, (128, 256)).T[:ROWS]
    theirs = [energies(order[k]) for k in range(ROUNDS)]
    for s in range(4):
        right_gap[s] = jnp.concatenate([t[:, s * ROWS:s * ROWS + 128] for t in theirs], axis=1)
    tails = [t[:, s * ROWS + 128:(s + 1) * ROWS] for s in range(4) for t in theirs]
    right_gap[4] = jnp.concatenate(tails, axis=1)

    my_z = position()[0]
    for dz in range(NZ):
        plane = lax.rem(my_z + dz, NZ)
        cols = pl.ds(dz * XY * COLS, XY * COLS)
        block = packed[plane]
        out[:128, cols] = block[:, :COLS].reshape(XY * COLS, 128).T
        tail = block[:, COLS:].astype(jnp.float32).reshape(XY * GROUP_COLS, 128)
        groups = [tail if g == 0 else pltpu.roll(tail, 128 - TAIL * g, 1) for g in range(GROUPS)]
        groups = [v.reshape(XY, 1, GROUP_COLS, 128) for v in groups]
        tail = jnp.concatenate(groups, axis=1).reshape(XY * COLS, 128)
        out[128:, cols] = tail.T[:TAIL].astype(jnp.bfloat16)


def unpack_rows(block_owner, round_order, eps_occ, eps_vir, packed):
    smem = pl.BlockSpec(memory_space=pltpu.SMEM)
    vmem = pl.BlockSpec(memory_space=pltpu.VMEM)
    return pl.pallas_call(
        rows_kernel,
        in_specs=[smem] * 3 + [vmem] * 2,
        out_specs=[vmem] * 3,
        out_shape=[
            jax.ShapeDtypeStruct((ROWS, NZ * XY * COLS), jnp.bfloat16),
            jax.ShapeDtypeStruct((ROWS, 128), jnp.float32),
            jax.ShapeDtypeStruct((5, 1, 256), jnp.float32),
        ],
        compiler_params=pltpu.CompilerParams(vmem_limit_bytes=VMEM_LIMIT),
    )(block_owner, round_order, eps_occ, eps_vir[None], packed)


def gamma_kernel(layout, rows, left_gap, right_gap, *rest):
    count = len(layout)
    pieces, (out, weights, tails, product, amplitude, sems) = rest[:count], rest[count:]
    my_z, my_x, my_y, my_core = position()
    planes = NZ // CHUNKS
    plane_cols = XY * COLS

    def copy(chunk, piece, step, second, swap, begin):
        core = 1 - my_core if swap else my_core
        first = begin + step
        x = lax.rem(my_x + jnp.where(core == 0, second, first), NX)
        y = lax.rem(my_y + jnp.where(core == 0, first, second), NY)
        span = pl.ds(chunk * planes, planes)
        return pltpu.make_async_copy(
            piece.at[step, span], weights.at[lax.div(x, 2) * NC + core, span, lax.rem(x, 2) * NY + y],
            sems.at[chunk])

    copies = [
        [copy(c, piece, step, *where) for piece, where in zip(pieces, layout) for step in range(piece.shape[0])]
        for c in range(CHUNKS)
    ]
    for c in range(CHUNKS):
        for one in copies[c]:
            one.start()

    half = COLS // 2
    for c in range(CHUNKS):
        for one in copies[c]:
            one.wait()
        span = slice(c * planes, (c + 1) * planes)
        for h in range(2):
            low = weights[2 * h, span, :, 2 * COLS:]
            high = weights[2 * h + 1, span, :, 2 * COLS:]
            tails[h, span, :, :half] = jnp.concatenate([low[..., :64], high[..., :64]], axis=-1)
            tails[h, span, :, half:] = jnp.concatenate([low[..., 64:], high[..., 64:]], axis=-1)
        mine = rows[:, c * planes * plane_cols:(c + 1) * planes * plane_cols]
        for p in range(5):
            if p < 4:
                pair = [weights[p, span, :, k * COLS:(k + 1) * COLS] for k in range(ROUNDS)]
            else:
                pair = [tails[h, span] for h in range(2)]
            pair = [v.reshape(planes * plane_cols, 128) for v in pair]
            part = jnp.dot(mine, jnp.concatenate(pair, axis=1), preferred_element_type=jnp.float32)
            if c > 0:
                part += product[p]
            if c < CHUNKS - 1:
                product[p] = part
            else:
                left = jnp.concatenate([left_gap[...]] * 2, axis=1)
                amplitude[:, p * 256:(p + 1) * 256] = (part / (left + right_gap[p])).astype(jnp.bfloat16)
    for dz in range(NZ):
        plane = lax.rem(my_z + dz, NZ)
        part = [weights[p, dz, :, k * COLS:(k + 1) * COLS] for p in range(4) for k in range(ROUNDS)]
        part += [tails[h, dz] for h in range(2)]
        part = jnp.concatenate([v.reshape(plane_cols, 128) for v in part], axis=1)
        part = lax.dot_general(
            amplitude[...], part, (((1,), (1,)), ((), ())), preferred_element_type=jnp.float32)
        out[:, pl.ds(pl.multiple_of(plane * plane_cols, plane_cols), plane_cols)] = part.astype(jnp.bfloat16)


def gamma(rows, left_gap, right_gap, pieces, layout):
    vmem = pl.BlockSpec(memory_space=pltpu.VMEM)
    return pl.pallas_call(
        functools.partial(gamma_kernel, layout),
        in_specs=[vmem] * 3
        + [pl.BlockSpec(memory_space=pl.ANY)] * len(pieces),
        out_specs=vmem,
        out_shape=jax.ShapeDtypeStruct((ROWS, NZ * XY * COLS), jnp.bfloat16),
        scratch_shapes=[
            pltpu.VMEM((4, NZ, XY, LINE, 128), jnp.bfloat16),
            pltpu.VMEM((2, NZ, XY, COLS, 128), jnp.bfloat16),
            pltpu.VMEM((5, ROWS, 256), jnp.float32),
            pltpu.VMEM((ROWS, 5 * 256), jnp.bfloat16),
            pltpu.SemaphoreType.DMA((CHUNKS,)),
        ],
        compiler_params=pltpu.CompilerParams(vmem_limit_bytes=VMEM_LIMIT),
    )(rows, left_gap, right_gap, *pieces)


def on_device(three_centre, eps_occ, eps_vir, block_owner, round_order):
    columns = jnp.swapaxes(three_centre, 1, 2)

    own, packed = pack(columns, round_order)
    pair = jnp.stack([own, fetch(own, dz=1)])
    far = [fetch(pair, dz=d) for d in (2, 4, 6)]
    line = jnp.concatenate([pair] + far)

    packed = exchange(packed, False)
    packed = exchange(jnp.swapaxes(packed, 0, 1), True)

    pieces, layout = [], []

    def keep(array, second, begin):
        pieces.extend([array, fetch(array, swap=1)])
        layout.extend([(second, 0, begin), (second, 1, begin)])

    low = jnp.stack([line, fetch(line, first=1)])
    high = jnp.stack([fetch(line, first=2), fetch(line, first=3)])
    keep(low, 0, 0)
    keep(high, 0, 2)
    ahead_low, behind_high = fetch(low, second=1), fetch(high, second=3)
    ahead_high, behind_low = fetch(high, second=1), fetch(low, second=3)
    keep(ahead_low, 1, 0)
    keep(behind_high, 3, 2)
    keep(ahead_high, 1, 2)
    keep(behind_low, 3, 0)
    keep(fetch(ahead_low, second=1), 2, 0)
    keep(fetch(behind_high, second=3), 2, 2)

    rows, left_gap, right_gap = unpack_rows(block_owner, round_order, eps_occ, eps_vir, packed)
    return gamma(rows, left_gap, right_gap, pieces, tuple(layout))[None]


def solution(mesh):
    in_specs = (P(None, "slab", "occ"), P(), P(), P(), P())
    out_specs = P("occ", "slab", None)
    return jax.shard_map(
        on_device, mesh=mesh, in_specs=in_specs, out_specs=out_specs, check_vma=False
    )
```

time: 799 us -> 89.1 us (0.11)
  the two profiles are of different devices: /device:TPU:8 before, /device:TPU:1 now
where the time goes in v2:
time: 89.1 us; the launch traced here: 88.7 us
  starting transfers between devices  51.3 us (58%)
  waiting for transfers between devices  13.2 us (15%)
  Pallas kernels  13.1 us (15%)
  local copies, waits for them, and re-layouts  8.6 us (10%)
  other arithmetic  2.23 us (3%)
    ppermute x21, starting transfers between devices, fetch(): return lax.ppermute(block, BOTH, pairs)  40.8 us
    ppermute x21, waiting for transfers between devices, fetch(): return lax.ppermute(block, BOTH, pairs)  13.2 us
    all_to_all x2, starting transfers between devices, exchange(): lax.all_to_all(packed, 'occ', split_axis=0, concat_axis=0, axis_index_gro...  10.6 us
    pallas_call x1, Pallas kernels, gamma(): pl.pallas_call(functools.partial(gamma_kernel, layout), in_specs=[vmem] *...  8.89 us
    unnamed x32, local copies, waits for them, and re-layouts  7.43 us
    pallas_call x1, Pallas kernels, pack(): pl.pallas_call(pack_kernel, grid_spec=pltpu.PrefetchScalarGridSpec(num_sc...  2.13 us
    pallas_call x1, Pallas kernels, unpack_rows(): pl.pallas_call(rows_kernel, in_specs=[smem] * 3 + [vmem] * 2, out_specs=[...  2.05 us
  transfers between devices with their start and end apart: 23, of which 6 were waited for; matrix products, arithmetic and copies ran while one was open for 4% of the time, Pallas kernels for 2%

profile of v2, /device:TPU:1, one launch (start us, length us, event | category | flops | bytes accessed | tf_op | source)
XLA Modules:
  0.0 88.7 jit_solution(8529777047353062901)
XLA Ops:
  0.0 1.6 %copy-done = bf16[64,160,64]{1,2,0:T(8,128)(2,1)S(1)} copy-done((bf16[64,160,64]{1,2,0:T(8,128)(2,1)S(1)}, bf16[64,160,64]{1,2,0:T(8,128)(2,1)}, u32[]{:S(2)}) %copy-start) | copy-done | bytes 1310744
  1.6 0.7 copy-done.7
  2.2 2.1 %shard_map.55 = (bf16[160,128]{1,0:T(8,128)(2,1)S(1)}, bf16[8,8,80,128]{3,2,1,0:T(8,128)(2,1)}) custom-call(s32[2]{0:T(128)S(1)} %copy-done.7, bf16[64,64,160]{2,1,0:T(8,128)(2,1)S(1)} %bitcast.13, bf16[64,64,160]{2,1,0:T(8,128)(2,1)S(1)} %bitcast.14, bf16[64,64,160]{2,1,0:T(8,128)(2,1)S(1)} %bitcast.15), custom_call_target="tpu_custom_call" | custom-call | tf_op jit(solution)/shard_map/pallas_call | solution.py:66
  4.4 5.9 %all-to-all-start = ((bf16[8,8,80,128]{3,2,1,0:T(8,128)(2,1)}), bf16[8,8,80,128]{3,2,1,0:T(8,128)(2,1)S(1)}, u32[]{:S(2)}, u32[]{:S(2)}) async-start(bf16[8,8,80,128]{3,2,1,0:T(8,128)(2,1)} %get-tuple-element.10), calls=%async_computation | async-start | bytes 2621440 | tf_op jit(solution)/shard_map/all_to_all | solution.py:91
  10.3 5.6 %collective-permute-start = (bf16[160,128]{1,0:T(8,128)(2,1)S(1)}, bf16[160,128]{1,0:T(8,128)(2,1)S(1)}, u32[]{:S(2)}, u32[]{:S(2)}) collective-permute-start(bf16[160,128]{1,0:T(8,128)(2,1)S(1)} %get-tuple-element.14), channel_id=1, source_target_pairs={{32,0},{33,1},{36,4},{37,5},{40,8},{41,9},{44,12},{45,13},{48,16},... | collective-permute-start | bytes 122888 | tf_op jit(solution)/shard_map/ppermute | solution.py:37
  15.9 1.1 %collective-permute-done = bf16[160,128]{1,0:T(8,128)(2,1)S(1)} collective-permute-done((bf16[160,128]{1,0:T(8,128)(2,1)S(1)}, bf16[160,128]{1,0:T(8,128)(2,1)S(1)}, u32[]{:S(2)}, u32[]{:S(2)}) %collective-permute-start) | collective-permute-done | bytes 40992 | tf_op jit(solution)/shard_map/ppermute | solution.py:37
  17.0 0.1 collective-permute-start.3
  17.1 4.3 %collective-permute-start.2 = (bf16[2,160,128]{2,1,0:T(8,128)(2,1)S(1)}, bf16[2,160,128]{2,1,0:T(8,128)(2,1)S(1)}, u32[]{:S(2)}, u32[]{:S(2)}) collective-permute-start(bf16[2,160,128]{2,1,0:T(8,128)(2,1)S(1)} %pad_maximum_fusion.2), channel_id=1, source_target_pairs={{128,0},{129,1},{132,4},{133,5},{136,8},{137,9},{140,12},{141,13},... | collective-permute-start | bytes 245768 | tf_op jit(solution)/shard_map/ppermute | solution.py:37
  21.4 2.4 %collective-permute-start.1 = (bf16[2,160,128]{2,1,0:T(8,128)(2,1)S(1)}, bf16[2,160,128]{2,1,0:T(8,128)(2,1)S(1)}, u32[]{:S(2)}, u32[]{:S(2)}) collective-permute-start(bf16[2,160,128]{2,1,0:T(8,128)(2,1)S(1)} %pad_maximum_fusion.2), channel_id=1, source_target_pairs={{64,0},{65,1},{68,4},{69,5},{72,8},{73,9},{76,12},{77,13},{80,16},... | collective-permute-start | bytes 245768 | tf_op jit(solution)/shard_map/ppermute | solution.py:37
  23.8 5.6 %collective-permute-done.1 = bf16[2,160,128]{2,1,0:T(8,128)(2,1)S(1)} collective-permute-done((bf16[2,160,128]{2,1,0:T(8,128)(2,1)S(1)}, bf16[2,160,128]{2,1,0:T(8,128)(2,1)S(1)}, u32[]{:S(2)}, u32[]{:S(2)}) %collective-permute-start.1) | collective-permute-done | bytes 81952 | tf_op jit(solution)/shard_map/ppermute | solution.py:37
  29.4 0.0 collective-permute-done.3
  29.4 2.8 %collective-permute-start.4 = (bf16[8,160,128]{2,1,0:T(8,128)(2,1)S(1)}, bf16[8,160,128]{2,1,0:T(8,128)(2,1)S(1)}, u32[]{:S(2)}, u32[]{:S(2)}) collective-permute-start(bf16[8,160,128]{2,1,0:T(8,128)(2,1)S(1)} %constant_dynamic-update-slice_fusion), channel_id=1, source_target_pairs={{4,0},{17,1},{8,4},{21,5},{12,8},{25,9},{0,12},{29,13},{20,16},{3,... | collective-permute-start | bytes 983048 | tf_op jit(solution)/shard_map/ppermute | solution.py:37
  32.2 0.0 collective-permute-start.7
  32.2 1.3 %collective-permute-start.6 = (bf16[8,160,128]{2,1,0:T(8,128)(2,1)S(1)}, bf16[8,160,128]{2,1,0:T(8,128)(2,1)}, u32[]{:S(2)}, u32[]{:S(2)}) collective-permute-start(bf16[8,160,128]{2,1,0:T(8,128)(2,1)S(1)} %constant_dynamic-update-slice_fusion), channel_id=1, source_target_pairs={{8,0},{3,1},{12,4},{7,5},{0,8},{11,9},{4,12},{15,13},{24,16},{19,1... | collective-permute-start | bytes 983048 | tf_op jit(solution)/shard_map/ppermute | solution.py:37
  33.5 0.0 all-to-all-done
  33.5 1.1 %copy.9 = bf16[8,8,80,128]{3,2,0,1:T(8,128)(2,1)} copy(bf16[8,8,80,128]{3,2,1,0:T(8,128)(2,1)S(1)} %all-to-all-done) | data formatting | bytes 2621440 | tf_op jit(solution)/shard_map/all_to_all | solution.py:91
  34.7 4.6 %all-to-all-start.1 = ((bf16[8,8,80,128]{3,2,1,0:T(8,128)(2,1)}), bf16[8,8,80,128]{3,2,1,0:T(8,128)(2,1)S(1)}, u32[]{:S(2)}, u32[]{:S(2)}) async-start(bf16[8,8,80,128]{3,2,1,0:T(8,128)(2,1)} %bitcast.12), calls=%async_computation.1 | async-start | bytes 2621440 | tf_op jit(solution)/shard_map/all_to_all | solution.py:91
  39.3 0.5 collective-permute-done.4
  39.8 0.7 copy-done.12
  40.5 1.1 %pad_maximum_fusion.rest_0_ = bf16[2,8,160,128]{3,2,1,0:T(8,128)(2,1)S(1)} fusion(bf16[1,8,160,128]{3,2,1,0:T(8,128)(2,1)} %bitcast.19, bf16[1,8,160,128]{3,2,1,0:T(8,128)(2,1)S(1)} %bitcast.17), kind=kLoop, calls=%fused_computation.1 | loop fusion | flops 327680 | bytes 1310720 | tf_op jit(solution)/shard_map/stack | solution.py:240
  41.6 1.3 %collective-permute-start.15 = (bf16[2,8,160,128]{3,2,1,0:T(8,128)(2,1)S(1)}, bf16[2,8,160,128]{3,2,1,0:T(8,128)(2,1)S(1)}, u32[]{:S(2)}, u32[]{:S(2)}) collective-permute-start(bf16[2,8,160,128]{3,2,1,0:T(8,128)(2,1)S(1)} %pad_maximum_fusion.rest_0_), channel_id=1, source_target_pairs={{18,0},{13,1},{22,4},{1,5},{26,8},{5,9},{30,12},{9,13},{0,16},{29,... | collective-permute-start | bytes 1966088 | tf_op jit(solution)/shard_map/ppermute | solution.py:37
  42.8 1.5 %collective-permute-start.9 = (bf16[2,8,160,128]{3,2,1,0:T(8,128)(2,1)S(1)}, bf16[2,8,160,128]{3,2,1,0:T(8,128)(2,1)}, u32[]{:S(2)}, u32[]{:S(2)}) collective-permute-start(bf16[2,8,160,128]{3,2,1,0:T(8,128)(2,1)S(1)} %pad_maximum_fusion.rest_0_), channel_id=1, source_target_pairs={{16,0},{5,1},{20,4},{9,5},{24,8},{13,9},{28,12},{1,13},{2,16},{21,... | collective-permute-start | bytes 1966088 | tf_op jit(solution)/shard_map/ppermute | solution.py:37
  44.3 4.3 %collective-permute-start.5 = (bf16[2,8,160,128]{3,2,1,0:T(8,128)(2,1)S(1)}, bf16[2,8,160,128]{3,2,1,0:T(8,128)(2,1)S(1)}, u32[]{:S(2)}, u32[]{:S(2)}) collective-permute-start(bf16[2,8,160,128]{3,2,1,0:T(8,128)(2,1)S(1)} %pad_maximum_fusion.rest_0_), channel_id=1, source_target_pairs={{1,0},{0,1},{5,4},{4,5},{9,8},{8,9},{13,12},{12,13},{17,16},{16,17... | collective-permute-start | bytes 1966088 | tf_op jit(solution)/shard_map/ppermute | solution.py:37
  48.6 0.0 collective-permute-done.7
  48.6 0.0 collective-permute-done.6
  48.6 0.7 copy-done.11
  49.3 1.1 %pad_maximum_fusion.1.rest_2_ = bf16[2,8,160,128]{3,2,1,0:T(8,128)(2,1)S(1)} fusion(bf16[1,8,160,128]{3,2,1,0:T(8,128)(2,1)} %bitcast.18, bf16[1,8,160,128]{3,2,1,0:T(8,128)(2,1)} %bitcast.6), kind=kLoop, calls=%fused_computation.2 | loop fusion | flops 327680 | bytes 1310720 | tf_op jit(solution)/shard_map/stack | solution.py:241
  50.5 1.7 %collective-permute-start.11 = (bf16[2,8,160,128]{3,2,1,0:T(8,128)(2,1)S(1)}, bf16[2,8,160,128]{3,2,1,0:T(8,128)(2,1)}, u32[]{:S(2)}, u32[]{:S(2)}) collective-permute-start(bf16[2,8,160,128]{3,2,1,0:T(8,128)(2,1)S(1)} %pad_maximum_fusion.1.rest_2_), channel_id=1, source_target_pairs={{18,0},{13,1},{22,4},{1,5},{26,8},{5,9},{30,12},{9,13},{0,16},{29,... | collective-permute-start | bytes 1966088 | tf_op jit(solution)/shard_map/ppermute | solution.py:37
  52.1 1.1 %collective-permute-start.13 = (bf16[2,8,160,128]{3,2,1,0:T(8,128)(2,1)S(1)}, bf16[2,8,160,128]{3,2,1,0:T(8,128)(2,1)}, u32[]{:S(2)}, u32[]{:S(2)}) collective-permute-start(bf16[2,8,160,128]{3,2,1,0:T(8,128)(2,1)S(1)} %pad_maximum_fusion.1.rest_2_), channel_id=1, source_target_pairs={{16,0},{5,1},{20,4},{9,5},{24,8},{13,9},{28,12},{1,13},{2,16},{21,... | collective-permute-start | bytes 1966088 | tf_op jit(solution)/shard_map/ppermute | solution.py:37
  53.2 3.9 %collective-permute-start.8 = (bf16[2,8,160,128]{3,2,1,0:T(8,128)(2,1)S(1)}, bf16[2,8,160,128]{3,2,1,0:T(8,128)(2,1)S(1)}, u32[]{:S(2)}, u32[]{:S(2)}) collective-permute-start(bf16[2,8,160,128]{3,2,1,0:T(8,128)(2,1)S(1)} %pad_maximum_fusion.1.rest_2_), channel_id=1, source_target_pairs={{1,0},{0,1},{5,4},{4,5},{9,8},{8,9},{13,12},{12,13},{17,16},{16,17... | collective-permute-start | bytes 1966088 | tf_op jit(solution)/shard_map/ppermute | solution.py:37
  57.2 0.3 collective-permute-start.16
  57.4 0.0 collective-permute-done.5.rest_1_
  57.5 0.8 copy-done.1
  58.3 0.9 %collective-permute-start.17 = (bf16[2,8,160,128]{3,2,1,0:T(8,128)(2,1)}, bf16[2,8,160,128]{3,2,1,0:T(8,128)(2,1)}, u32[]{:S(2)}, u32[]{:S(2)}) collective-permute-start(bf16[2,8,160,128]{3,2,1,0:T(8,128)(2,1)} %collective-permute-done.9.rest_4_), channel_id=1, source_target_pairs={{16,0},{5,1},{20,4},{9,5},{24,8},{13,9},{28,12},{1,13},{2,16},{21,... | collective-permute-start | bytes 1966088 | tf_op jit(solution)/shard_map/ppermute | solution.py:37
  59.2 2.4 %collective-permute-done.11.rest_6_ = bf16[2,8,160,128]{3,2,1,0:T(8,128)(2,1)} collective-permute-done((bf16[2,8,160,128]{3,2,1,0:T(8,128)(2,1)S(1)}, bf16[2,8,160,128]{3,2,1,0:T(8,128)(2,1)}, u32[]{:S(2)}, u32[]{:S(2)}) %collective-permute-start.11) | collective-permute-done | bytes 655392 | tf_op jit(solution)/shard_map/ppermute | solution.py:37
  61.6 0.4 collective-permute-start.19
  61.9 2.5 %collective-permute-start.10 = (bf16[2,8,160,128]{3,2,1,0:T(8,128)(2,1)}, bf16[2,8,160,128]{3,2,1,0:T(8,128)(2,1)}, u32[]{:S(2)}, u32[]{:S(2)}) collective-permute-start(bf16[2,8,160,128]{3,2,1,0:T(8,128)(2,1)} %collective-permute-done.9.rest_4_), channel_id=1, source_target_pairs={{1,0},{0,1},{5,4},{4,5},{9,8},{8,9},{13,12},{12,13},{17,16},{16,17... | collective-permute-start | bytes 1966088 | tf_op jit(solution)/shard_map/ppermute | solution.py:37
  64.5 0.9 %copy-done.3 = bf16[2,8,160,128]{3,2,1,0:T(8,128)(2,1)} copy-done((bf16[2,8,160,128]{3,2,1,0:T(8,128)(2,1)}, bf16[2,8,160,128]{3,2,1,0:T(8,128)(2,1)S(1)}, u32[]{:S(2)}) %copy-start.3) | copy-done | bytes 655384
  65.4 0.0 collective-permute-start.12
  65.4 0.9 copy-done.5
  66.3 0.5 collective-permute-start.14
  66.8 2.2 %collective-permute-done.17.rest_12_ = bf16[2,8,160,128]{3,2,1,0:T(8,128)(2,1)} collective-permute-done((bf16[2,8,160,128]{3,2,1,0:T(8,128)(2,1)}, bf16[2,8,160,128]{3,2,1,0:T(8,128)(2,1)}, u32[]{:S(2)}, u32[]{:S(2)}) %collective-permute-start.17) | collective-permute-done | bytes 655392 | tf_op jit(solution)/shard_map/ppermute | solution.py:37
  69.0 2.5 %collective-permute-start.18 = (bf16[2,8,160,128]{3,2,1,0:T(8,128)(2,1)}, bf16[2,8,160,128]{3,2,1,0:T(8,128)(2,1)}, u32[]{:S(2)}, u32[]{:S(2)}) collective-permute-start(bf16[2,8,160,128]{3,2,1,0:T(8,128)(2,1)} %collective-permute-done.17.rest_12_), channel_id=1, source_target_pairs={{1,0},{0,1},{5,4},{4,5},{9,8},{8,9},{13,12},{12,13},{17,16},{16,17... | collective-permute-start | bytes 1966088 | tf_op jit(solution)/shard_map/ppermute | solution.py:37
  71.5 1.3 %collective-permute-done.19.rest_14_ = bf16[2,8,160,128]{3,2,1,0:T(8,128)(2,1)} collective-permute-done((bf16[2,8,160,128]{3,2,1,0:T(8,128)(2,1)}, bf16[2,8,160,128]{3,2,1,0:T(8,128)(2,1)}, u32[]{:S(2)}, u32[]{:S(2)}) %collective-permute-start.19) | collective-permute-done | bytes 655392 | tf_op jit(solution)/shard_map/ppermute | solution.py:37
  72.8 3.6 %collective-permute-start.20 = (bf16[2,8,160,128]{3,2,1,0:T(8,128)(2,1)}, bf16[2,8,160,128]{3,2,1,0:T(8,128)(2,1)}, u32[]{:S(2)}, u32[]{:S(2)}) collective-permute-start(bf16[2,8,160,128]{3,2,1,0:T(8,128)(2,1)} %collective-permute-done.19.rest_14_), channel_id=1, source_target_pairs={{1,0},{0,1},{5,4},{4,5},{9,8},{8,9},{13,12},{12,13},{17,16},{16,17... | collective-permute-start | bytes 1966088 | tf_op jit(solution)/shard_map/ppermute | solution.py:37
  76.5 2.0 %shard_map.56 = (bf16[160,4096]{1,0:T(8,128)(2,1)S(1)}, f32[160,128]{1,0:T(8,128)S(1)}, f32[5,1,256]{2,1,0:T(1,128)S(1)}) custom-call(s32[64]{0:T(128)S(1)} %copy-done.9, s32[2]{0:T(128)S(1)} %copy-done.8, f32[16]{0:T(128)S(1)} %copy-done.10, f32[1,2560]{1,0:T(1,128)S(1)} %broadcast_in_dim.6.eps_vir, bf16[8,8,80,128]{3,2,1,0:T(8,128)(2,1)S(1)} %all-to-all-done.1.packed), custom_call_target="tpu_custom_call" | custom-call | tf_op jit(solution)/shard_map/pallas_call | solution.py:131
  78.6 1.1 %copy-done.6 = bf16[2,8,160,128]{3,2,1,0:T(8,128)(2,1)S(1)} copy-done((bf16[2,8,160,128]{3,2,1,0:T(8,128)(2,1)S(1)}, bf16[2,8,160,128]{3,2,1,0:T(8,128)(2,1)}, u32[]{:S(2)}) %copy-start.6) | copy-done | bytes 655384
  79.7 8.9 %shard_map.57 = bf16[160,4096]{1,0:T(8,128)(2,1)} custom-call(bf16[160,4096]{1,0:T(8,128)(2,1)S(1)} %get-tuple-element.11.rows, f32[160,128]{1,0:T(8,128)S(1)} %get-tuple-element.12.left_gap, f32[5,1,256]{2,1,0:T(1,128)S(1)} %get-tuple-element.13.right_gap, bf16[2,8,160,128]{3,2,1,0:T(8,128)(2,1)S(1)} %pad_maximum_fusion.rest_0_, ...), custom_call_target="tpu_custom_call" | custom-call | tf_op jit(solution)/shard_map/pallas_call | solution.py:206
  (39 shorter events, 0.1 us)
Async XLA Ops:
  0.0 1.6 %copy-start = (bf16[64,160,64]{1,2,0:T(8,128)(2,1)S(1)}, bf16[64,160,64]{1,2,0:T(8,128)(2,1)}, u32[]{:S(2)}) copy-start(bf16[64,160,64]{1,2,0:T(8,128)(2,1)} %param.5) | copy-start | bytes 3932164
  1.6 0.7 copy-start.7
  4.4 29.1 %all-to-all-start = ((bf16[8,8,80,128]{3,2,1,0:T(8,128)(2,1)}), bf16[8,8,80,128]{3,2,1,0:T(8,128)(2,1)S(1)}, u32[]{:S(2)}, u32[]{:S(2)}) async-start(bf16[8,8,80,128]{3,2,1,0:T(8,128)(2,1)} %get-tuple-element.10), calls=%async_computation | async-start | bytes 2621440 | tf_op jit(solution)/shard_map/all_to_all | solution.py:91
  10.3 6.7 %collective-permute-start = (bf16[160,128]{1,0:T(8,128)(2,1)S(1)}, bf16[160,128]{1,0:T(8,128)(2,1)S(1)}, u32[]{:S(2)}, u32[]{:S(2)}) collective-permute-start(bf16[160,128]{1,0:T(8,128)(2,1)S(1)} %get-tuple-element.14), channel_id=1, source_target_pairs={{32,0},{33,1},{36,4},{37,5},{40,8},{41,9},{44,12},{45,13},{48,16},... | collective-permute-start | bytes 122888 | tf_op jit(solution)/shard_map/ppermute | solution.py:37
  17.0 12.4 %collective-permute-start.3 = (bf16[2,160,128]{2,1,0:T(8,128)(2,1)S(1)}, bf16[2,160,128]{2,1,0:T(8,128)(2,1)S(1)}, u32[]{:S(2)}, u32[]{:S(2)}) collective-permute-start(bf16[2,160,128]{2,1,0:T(8,128)(2,1)S(1)} %pad_maximum_fusion.2), channel_id=1, source_target_pairs={{192,0},{193,1},{196,4},{197,5},{200,8},{201,9},{204,12},{205,13},... | collective-permute-start | bytes 245768 | tf_op jit(solution)/shard_map/ppermute | solution.py:37
  17.1 12.3 %collective-permute-start.2 = (bf16[2,160,128]{2,1,0:T(8,128)(2,1)S(1)}, bf16[2,160,128]{2,1,0:T(8,128)(2,1)S(1)}, u32[]{:S(2)}, u32[]{:S(2)}) collective-permute-start(bf16[2,160,128]{2,1,0:T(8,128)(2,1)S(1)} %pad_maximum_fusion.2), channel_id=1, source_target_pairs={{128,0},{129,1},{132,4},{133,5},{136,8},{137,9},{140,12},{141,13},... | collective-permute-start | bytes 245768 | tf_op jit(solution)/shard_map/ppermute | solution.py:37
  21.4 8.0 %collective-permute-start.1 = (bf16[2,160,128]{2,1,0:T(8,128)(2,1)S(1)}, bf16[2,160,128]{2,1,0:T(8,128)(2,1)S(1)}, u32[]{:S(2)}, u32[]{:S(2)}) collective-permute-start(bf16[2,160,128]{2,1,0:T(8,128)(2,1)S(1)} %pad_maximum_fusion.2), channel_id=1, source_target_pairs={{64,0},{65,1},{68,4},{69,5},{72,8},{73,9},{76,12},{77,13},{80,16},... | collective-permute-start | bytes 245768 | tf_op jit(solution)/shard_map/ppermute | solution.py:37
  29.4 10.3 %collective-permute-start.4 = (bf16[8,160,128]{2,1,0:T(8,128)(2,1)S(1)}, bf16[8,160,128]{2,1,0:T(8,128)(2,1)S(1)}, u32[]{:S(2)}, u32[]{:S(2)}) collective-permute-start(bf16[8,160,128]{2,1,0:T(8,128)(2,1)S(1)} %constant_dynamic-update-slice_fusion), channel_id=1, source_target_pairs={{4,0},{17,1},{8,4},{21,5},{12,8},{25,9},{0,12},{29,13},{20,16},{3,... | collective-permute-start | bytes 983048 | tf_op jit(solution)/shard_map/ppermute | solution.py:37
  32.2 16.4 %collective-permute-start.7 = (bf16[8,160,128]{2,1,0:T(8,128)(2,1)S(1)}, bf16[8,160,128]{2,1,0:T(8,128)(2,1)S(1)}, u32[]{:S(2)}, u32[]{:S(2)}) collective-permute-start(bf16[8,160,128]{2,1,0:T(8,128)(2,1)S(1)} %constant_dynamic-update-slice_fusion), channel_id=1, source_target_pairs={{12,0},{19,1},{0,4},{23,5},{4,8},{27,9},{8,12},{31,13},{28,16},{1,... | collective-permute-start | bytes 983048 | tf_op jit(solution)/shard_map/ppermute | solution.py:37
  32.2 16.4 %collective-permute-start.6 = (bf16[8,160,128]{2,1,0:T(8,128)(2,1)S(1)}, bf16[8,160,128]{2,1,0:T(8,128)(2,1)}, u32[]{:S(2)}, u32[]{:S(2)}) collective-permute-start(bf16[8,160,128]{2,1,0:T(8,128)(2,1)S(1)} %constant_dynamic-update-slice_fusion), channel_id=1, source_target_pairs={{8,0},{3,1},{12,4},{7,5},{0,8},{11,9},{4,12},{15,13},{24,16},{19,1... | collective-permute-start | bytes 983048 | tf_op jit(solution)/shard_map/ppermute | solution.py:37
  34.7 41.8 %all-to-all-start.1 = ((bf16[8,8,80,128]{3,2,1,0:T(8,128)(2,1)}), bf16[8,8,80,128]{3,2,1,0:T(8,128)(2,1)S(1)}, u32[]{:S(2)}, u32[]{:S(2)}) async-start(bf16[8,8,80,128]{3,2,1,0:T(8,128)(2,1)} %bitcast.12), calls=%async_computation.1 | async-start | bytes 2621440 | tf_op jit(solution)/shard_map/all_to_all | solution.py:91
  39.8 0.7 copy-start.12
  40.5 35.9 %copy-start.13 = (f32[2560]{0:T(1024)S(1)}, f32[2560]{0:T(1024)}, u32[]{:S(2)}) copy-start(f32[2560]{0:T(1024)} %param.7) | copy-start | bytes 30724
  40.5 35.9 %copy-start.8 = (s32[2]{0:T(128)S(1)}, s32[2]{0:T(128)}, u32[]{:S(2)}) copy-start(s32[2]{0:T(128)} %order.3) | copy-start | bytes 28
  40.5 35.9 %copy-start.9 = (s32[64]{0:T(128)S(1)}, s32[64]{0:T(128)}, u32[]{:S(2)}) copy-start(s32[64]{0:T(128)} %owner.1) | copy-start | bytes 772
  40.5 36.0 %copy-start.10 = (f32[16]{0:T(128)S(1)}, f32[16]{0:T(128)}, u32[]{:S(2)}) copy-start(f32[16]{0:T(128)} %eps_occ.1) | copy-start | bytes 196
  41.6 11.6 %collective-permute-start.15 = (bf16[2,8,160,128]{3,2,1,0:T(8,128)(2,1)S(1)}, bf16[2,8,160,128]{3,2,1,0:T(8,128)(2,1)S(1)}, u32[]{:S(2)}, u32[]{:S(2)}) collective-permute-start(bf16[2,8,160,128]{3,2,1,0:T(8,128)(2,1)S(1)} %pad_maximum_fusion.rest_0_), channel_id=1, source_target_pairs={{18,0},{13,1},{22,4},{1,5},{26,8},{5,9},{30,12},{9,13},{0,16},{29,... | collective-permute-start | bytes 1966088 | tf_op jit(solution)/shard_map/ppermute | solution.py:37
  42.8 14.3 %collective-permute-start.9 = (bf16[2,8,160,128]{3,2,1,0:T(8,128)(2,1)S(1)}, bf16[2,8,160,128]{3,2,1,0:T(8,128)(2,1)}, u32[]{:S(2)}, u32[]{:S(2)}) collective-permute-start(bf16[2,8,160,128]{3,2,1,0:T(8,128)(2,1)S(1)} %pad_maximum_fusion.rest_0_), channel_id=1, source_target_pairs={{16,0},{5,1},{20,4},{9,5},{24,8},{13,9},{28,12},{1,13},{2,16},{21,... | collective-permute-start | bytes 1966088 | tf_op jit(solution)/shard_map/ppermute | solution.py:37
  44.3 13.1 %collective-permute-start.5 = (bf16[2,8,160,128]{3,2,1,0:T(8,128)(2,1)S(1)}, bf16[2,8,160,128]{3,2,1,0:T(8,128)(2,1)S(1)}, u32[]{:S(2)}, u32[]{:S(2)}) collective-permute-start(bf16[2,8,160,128]{3,2,1,0:T(8,128)(2,1)S(1)} %pad_maximum_fusion.rest_0_), channel_id=1, source_target_pairs={{1,0},{0,1},{5,4},{4,5},{9,8},{8,9},{13,12},{12,13},{17,16},{16,17... | collective-permute-start | bytes 1966088 | tf_op jit(solution)/shard_map/ppermute | solution.py:37
  48.6 0.7 copy-start.11
  50.5 11.1 %collective-permute-start.11 = (bf16[2,8,160,128]{3,2,1,0:T(8,128)(2,1)S(1)}, bf16[2,8,160,128]{3,2,1,0:T(8,128)(2,1)}, u32[]{:S(2)}, u32[]{:S(2)}) collective-permute-start(bf16[2,8,160,128]{3,2,1,0:T(8,128)(2,1)S(1)} %pad_maximum_fusion.1.rest_2_), channel_id=1, source_target_pairs={{18,0},{13,1},{22,4},{1,5},{26,8},{5,9},{30,12},{9,13},{0,16},{29,... | collective-permute-start | bytes 1966088 | tf_op jit(solution)/shard_map/ppermute | solution.py:37
  52.1 9.8 %collective-permute-start.13 = (bf16[2,8,160,128]{3,2,1,0:T(8,128)(2,1)S(1)}, bf16[2,8,160,128]{3,2,1,0:T(8,128)(2,1)}, u32[]{:S(2)}, u32[]{:S(2)}) collective-permute-start(bf16[2,8,160,128]{3,2,1,0:T(8,128)(2,1)S(1)} %pad_maximum_fusion.1.rest_2_), channel_id=1, source_target_pairs={{16,0},{5,1},{20,4},{9,5},{24,8},{13,9},{28,12},{1,13},{2,16},{21,... | collective-permute-start | bytes 1966088 | tf_op jit(solution)/shard_map/ppermute | solution.py:37
  53.2 11.3 %collective-permute-start.8 = (bf16[2,8,160,128]{3,2,1,0:T(8,128)(2,1)S(1)}, bf16[2,8,160,128]{3,2,1,0:T(8,128)(2,1)S(1)}, u32[]{:S(2)}, u32[]{:S(2)}) collective-permute-start(bf16[2,8,160,128]{3,2,1,0:T(8,128)(2,1)S(1)} %pad_maximum_fusion.1.rest_2_), channel_id=1, source_target_pairs={{1,0},{0,1},{5,4},{4,5},{9,8},{8,9},{13,12},{12,13},{17,16},{16,17... | collective-permute-start | bytes 1966088 | tf_op jit(solution)/shard_map/ppermute | solution.py:37
  57.2 8.2 %collective-permute-start.16 = (bf16[2,8,160,128]{3,2,1,0:T(8,128)(2,1)S(1)}, bf16[2,8,160,128]{3,2,1,0:T(8,128)(2,1)S(1)}, u32[]{:S(2)}, u32[]{:S(2)}) collective-permute-start(bf16[2,8,160,128]{3,2,1,0:T(8,128)(2,1)S(1)} %collective-permute-done.15.rest_10_), channel_id=1, source_target_pairs={{1,0},{0,1},{5,4},{4,5},{9,8},{8,9},{13,12},{12,13},{17,16},{16,17... | collective-permute-start | bytes 1966088 | tf_op jit(solution)/shard_map/ppermute | solution.py:37
  57.5 0.8 copy-start.1
  58.3 10.7 %collective-permute-start.17 = (bf16[2,8,160,128]{3,2,1,0:T(8,128)(2,1)}, bf16[2,8,160,128]{3,2,1,0:T(8,128)(2,1)}, u32[]{:S(2)}, u32[]{:S(2)}) collective-permute-start(bf16[2,8,160,128]{3,2,1,0:T(8,128)(2,1)} %collective-permute-done.9.rest_4_), channel_id=1, source_target_pairs={{16,0},{5,1},{20,4},{9,5},{24,8},{13,9},{28,12},{1,13},{2,16},{21,... | collective-permute-start | bytes 1966088 | tf_op jit(solution)/shard_map/ppermute | solution.py:37
  61.6 11.3 %collective-permute-start.19 = (bf16[2,8,160,128]{3,2,1,0:T(8,128)(2,1)}, bf16[2,8,160,128]{3,2,1,0:T(8,128)(2,1)}, u32[]{:S(2)}, u32[]{:S(2)}) collective-permute-start(bf16[2,8,160,128]{3,2,1,0:T(8,128)(2,1)} %collective-permute-done.11.rest_6_), channel_id=1, source_target_pairs={{18,0},{13,1},{22,4},{1,5},{26,8},{5,9},{30,12},{9,13},{0,16},{29,... | collective-permute-start | bytes 1966088 | tf_op jit(solution)/shard_map/ppermute | solution.py:37
  61.9 16.6 %collective-permute-start.10 = (bf16[2,8,160,128]{3,2,1,0:T(8,128)(2,1)}, bf16[2,8,160,128]{3,2,1,0:T(8,128)(2,1)}, u32[]{:S(2)}, u32[]{:S(2)}) collective-permute-start(bf16[2,8,160,128]{3,2,1,0:T(8,128)(2,1)} %collective-permute-done.9.rest_4_), channel_id=1, source_target_pairs={{1,0},{0,1},{5,4},{4,5},{9,8},{8,9},{13,12},{12,13},{17,16},{16,17... | collective-permute-start | bytes 1966088 | tf_op jit(solution)/shard_map/ppermute | solution.py:37
  64.5 0.9 %copy-start.3 = (bf16[2,8,160,128]{3,2,1,0:T(8,128)(2,1)}, bf16[2,8,160,128]{3,2,1,0:T(8,128)(2,1)S(1)}, u32[]{:S(2)}) copy-start(bf16[2,8,160,128]{3,2,1,0:T(8,128)(2,1)S(1)} %collective-permute-done.8.rest_3_) | copy-start | bytes 1966084
  65.4 13.2 %collective-permute-start.12 = (bf16[2,8,160,128]{3,2,1,0:T(8,128)(2,1)}, bf16[2,8,160,128]{3,2,1,0:T(8,128)(2,1)}, u32[]{:S(2)}, u32[]{:S(2)}) collective-permute-start(bf16[2,8,160,128]{3,2,1,0:T(8,128)(2,1)} %collective-permute-done.11.rest_6_), channel_id=1, source_target_pairs={{1,0},{0,1},{5,4},{4,5},{9,8},{8,9},{13,12},{12,13},{17,16},{16,17... | collective-permute-start | bytes 1966088 | tf_op jit(solution)/shard_map/ppermute | solution.py:37
  65.4 0.9 copy-start.5
  66.3 12.3 %collective-permute-start.14 = (bf16[2,8,160,128]{3,2,1,0:T(8,128)(2,1)}, bf16[2,8,160,128]{3,2,1,0:T(8,128)(2,1)}, u32[]{:S(2)}, u32[]{:S(2)}) collective-permute-start(bf16[2,8,160,128]{3,2,1,0:T(8,128)(2,1)} %collective-permute-done.13.rest_8_), channel_id=1, source_target_pairs={{1,0},{0,1},{5,4},{4,5},{9,8},{8,9},{13,12},{12,13},{17,16},{16,17... | collective-permute-start | bytes 1966088 | tf_op jit(solution)/shard_map/ppermute | solution.py:37
  69.0 9.6 %collective-permute-start.18 = (bf16[2,8,160,128]{3,2,1,0:T(8,128)(2,1)}, bf16[2,8,160,128]{3,2,1,0:T(8,128)(2,1)}, u32[]{:S(2)}, u32[]{:S(2)}) collective-permute-start(bf16[2,8,160,128]{3,2,1,0:T(8,128)(2,1)} %collective-permute-done.17.rest_12_), channel_id=1, source_target_pairs={{1,0},{0,1},{5,4},{4,5},{9,8},{8,9},{13,12},{12,13},{17,16},{16,17... | collective-permute-start | bytes 1966088 | tf_op jit(solution)/shard_map/ppermute | solution.py:37
  72.8 5.7 %collective-permute-start.20 = (bf16[2,8,160,128]{3,2,1,0:T(8,128)(2,1)}, bf16[2,8,160,128]{3,2,1,0:T(8,128)(2,1)}, u32[]{:S(2)}, u32[]{:S(2)}) collective-permute-start(bf16[2,8,160,128]{3,2,1,0:T(8,128)(2,1)} %collective-permute-done.19.rest_14_), channel_id=1, source_target_pairs={{1,0},{0,1},{5,4},{4,5},{9,8},{8,9},{13,12},{12,13},{17,16},{16,17... | collective-permute-start | bytes 1966088 | tf_op jit(solution)/shard_map/ppermute | solution.py:37
  76.5 2.1 %copy-start.2 = (bf16[2,8,160,128]{3,2,1,0:T(8,128)(2,1)S(1)}, bf16[2,8,160,128]{3,2,1,0:T(8,128)(2,1)}, u32[]{:S(2)}) copy-start(bf16[2,8,160,128]{3,2,1,0:T(8,128)(2,1)} %copy-done.1) | copy-start | bytes 1966084
  76.5 2.1 %copy-start.4 = (bf16[2,8,160,128]{3,2,1,0:T(8,128)(2,1)S(1)}, bf16[2,8,160,128]{3,2,1,0:T(8,128)(2,1)}, u32[]{:S(2)}) copy-start(bf16[2,8,160,128]{3,2,1,0:T(8,128)(2,1)} %copy-done.3) | copy-start | bytes 1966084
  78.6 1.1 %copy-start.6 = (bf16[2,8,160,128]{3,2,1,0:T(8,128)(2,1)S(1)}, bf16[2,8,160,128]{3,2,1,0:T(8,128)(2,1)}, u32[]{:S(2)}) copy-start(bf16[2,8,160,128]{3,2,1,0:T(8,128)(2,1)} %copy-done.5) | copy-start | bytes 1966084

commit v3 on v0

v3 whole, which is shorter than its diff:
```python
import functools

import jax
import jax.numpy as jnp
from jax import lax
from jax.experimental import pallas as pl
from jax.experimental.pallas import tpu as pltpu
from jax.sharding import PartitionSpec as P

ROUNDS = 2
NZ, NX, NY, NC = 8, 4, 4, 2
XY = 8
COLS = 64
ROWS = 160
TAIL = ROWS - 128
PACKED = COLS + COLS * TAIL // 128
GROUPS = 128 // TAIL
GROUP_COLS = COLS // GROUPS
BOTH = ("occ", "slab")
LINE = 2 * COLS + COLS // 2
VMEM_LIMIT = 20 * 1024 * 1024


def index(z, x, y, core):
    return ((z % NZ) * XY + (x % 2) * NY + y % NY) * 4 + (x % NX) // 2 * 2 + core


def fetch(block, dz=0, first=0, second=0, swap=0):
    pairs = []
    for z in range(NZ):
        for x in range(NX):
            for y in range(NY):
                for core in range(NC):
                    dx, dy = (first, second) if core else (second, first)
                    pairs.append((index(z + dz, x + dx, y + dy, core ^ swap), index(z, x, y, core)))
    return lax.ppermute(block, BOTH, pairs)


def position():
    occ, slab = lax.axis_index("occ"), lax.axis_index("slab")
    return lax.div(occ, XY), lax.div(slab, 2) * 2 + lax.rem(lax.div(occ, NY), 2), lax.rem(occ, NY), lax.rem(slab, 2)


def line_kernel(order, columns, out, rounds, sems):
    copies = [
        pltpu.make_async_copy(columns.at[order[k]], rounds.at[k], sems.at[k]) for k in range(ROUNDS)]
    for copy in copies:
        copy.start()
    for copy in copies:
        copy.wait()
    for k in range(ROUNDS):
        out[k * COLS:(k + 1) * COLS] = rounds[k, :, :128]
    half = COLS // 2
    tail = [rounds[k, h:h + half, 128:] for h in (0, half) for k in range(ROUNDS)]
    out[2 * COLS:] = jnp.concatenate(tail, axis=1)


def pack_line(columns, round_order):
    return pl.pallas_call(
        line_kernel,
        in_specs=[pl.BlockSpec(memory_space=pltpu.SMEM), pl.BlockSpec(memory_space=pltpu.HBM)],
        out_specs=pl.BlockSpec(memory_space=pltpu.VMEM),
        out_shape=jax.ShapeDtypeStruct((LINE, 128), jnp.bfloat16),
        scratch_shapes=[pltpu.VMEM((ROUNDS, COLS, ROWS), jnp.bfloat16), pltpu.SemaphoreType.DMA((ROUNDS,))],
    )(round_order, columns)


def pack_kernel(pieces, out):
    step = pieces.shape[0]
    for b in range(step):
        piece = pieces[b]
        z, spot = pl.program_id(0) * (step // XY) + b // XY, b % XY
        out[spot, z, :COLS] = piece[:, :128]
        tail = [piece[g * GROUP_COLS:(g + 1) * GROUP_COLS, 128:] for g in range(GROUPS)]
        out[spot, z, COLS:] = jnp.concatenate(tail, axis=1)


def pack(columns):
    blocks = columns.shape[0]
    step = 32
    return pl.pallas_call(
        pack_kernel,
        grid=(blocks // step,),
        in_specs=[pl.BlockSpec((step, COLS, ROWS), lambda i: (i, 0, 0))],
        out_specs=pl.BlockSpec((XY, NZ, PACKED, 128), lambda i: (0, 0, 0, 0)),
        out_shape=jax.ShapeDtypeStruct((XY, NZ, PACKED, 128), jnp.bfloat16),
        compiler_params=pltpu.CompilerParams(vmem_limit_bytes=VMEM_LIMIT),
    )(columns)


def exchange(packed, planes):
    groups = [[m * XY + o if planes else o * XY + m for m in range(8)] for o in range(8)]
    return lax.all_to_all(packed, "occ", split_axis=0, concat_axis=0, axis_index_groups=groups, tiled=True)


def gamma_kernel(layout, owner, order, eps_occ, eps_vir, packed, *refs):
    pieces, (out, weights, tails, block_ref, rows, right, amplitude, result, load_sems, store_sem) = (
        refs[:len(layout)], refs[len(layout):])
    my_z, my_x, my_y, my_core = position()
    fetch_block = pltpu.make_async_copy(packed, block_ref, load_sems.at[NC])
    fetch_block.start()
    copies = [[], []]
    for swap in range(NC):
        for piece, (second, swapped, first) in zip(pieces, layout):
            if swapped == swap:
                place = weights.at[swap, second, pl.ds(first, piece.shape[0])]
                copies[swap].append(pltpu.make_async_copy(piece, place, load_sems.at[swap]))
    for copy in copies[0] + copies[1]:
        copy.start()

    def line_of(swap, x_hi, spot):
        core = 1 - my_core if swap else my_core
        dx = lax.rem(x_hi * 2 + spot // NY + NX - my_x, NX)
        dy = lax.rem(spot % NY + NY - my_y, NY)
        return weights.at[swap, jnp.where(core == 0, dx, dy), jnp.where(core == 0, dy, dx)]

    span = 4 * ROWS
    vir_blocks = eps_vir.shape[1] // span

    def energies(slot):
        block = owner[slot]
        start = pl.multiple_of(lax.rem(block, vir_blocks) * span, 128)
        return eps_occ[lax.div(block, vir_blocks)] - eps_vir[:, pl.ds(start, span)]

    mine = energies(lax.axis_index("occ"))
    left = mine[:, :ROWS]
    for s in range(1, 4):
        left = jnp.where(lax.axis_index("slab") == s, mine[:, s * ROWS:(s + 1) * ROWS], left)
    left = jnp.concatenate([left, jnp.zeros((1, 256 - ROWS), jnp.float32)], axis=1)
    left = jnp.broadcast_to(left, (256, 256)).T[:ROWS]
    theirs = [energies(order[k]) for k in range(ROUNDS)]
    for s in range(4):
        right[s] = jnp.concatenate([t[:, s * ROWS:s * ROWS + 128] for t in theirs], axis=1)
    right[4] = jnp.concatenate(
        [t[:, s * ROWS + 128:(s + 1) * ROWS] for s in range(4) for t in theirs], axis=1)

    plane_cols = XY * COLS
    fetch_block.wait()
    for dz in range(NZ):
        cols = slice(dz * plane_cols, (dz + 1) * plane_cols)
        block = block_ref[lax.rem(my_z + dz, NZ)]
        rows[:128, cols] = block[:, :COLS].reshape(plane_cols, 128).T
        tail = block[:, COLS:].astype(jnp.float32).reshape(XY * GROUP_COLS, 128)
        groups = [tail if g == 0 else pltpu.roll(tail, 128 - TAIL * g, 1) for g in range(GROUPS)]
        groups = [v.reshape(XY, 1, GROUP_COLS, 128) for v in groups]
        tail = jnp.concatenate(groups, axis=1).reshape(plane_cols, 128)
        rows[128:, cols] = tail.T[:TAIL].astype(jnp.bfloat16)

    def contract(p, pair):
        part = jnp.dot(rows[...], jnp.concatenate(pair, axis=1), preferred_element_type=jnp.float32)
        amplitude[p] = (part / (left + right[p])).astype(jnp.bfloat16)

    def slab_cols(lines, k, planes):
        return jnp.concatenate([v[z, k * COLS:(k + 1) * COLS] for z in planes for v in lines], axis=0)

    for swap in range(NC):
        for copy in copies[swap]:
            copy.wait()
        for h in range(2):
            lines = [line_of(swap, h, spot) for spot in range(XY)]
            p = 2 * h + (1 - my_core if swap else my_core)
            contract(p, [slab_cols(lines, k, range(NZ)) for k in range(ROUNDS)])
    half = COLS // 2
    for h in range(2):
        for spot in range(XY):
            mine, other = line_of(0, h, spot), line_of(1, h, spot)
            for z in range(NZ):
                mine_tail, other_tail = mine[z, 2 * COLS:], other[z, 2 * COLS:]
                low = jnp.where(my_core == 0, mine_tail, other_tail)
                high = jnp.where(my_core == 0, other_tail, mine_tail)
                tails[h, z, spot, :half] = jnp.concatenate([low[:, :64], high[:, :64]], axis=1)
                tails[h, z, spot, half:] = jnp.concatenate([low[:, 64:], high[:, 64:]], axis=1)
    contract(4, [tails[h].reshape(NZ * plane_cols, 128) for h in range(2)])

    slabs = [2 * h + (1 - my_core if swap else my_core) for swap in range(NC) for h in range(2)] + [4]
    turned = jnp.concatenate([amplitude[p] for p in slabs], axis=1).T
    lines = [[line_of(swap, h, spot) for spot in range(XY)] for swap in range(NC) for h in range(2)]
    stores = []
    for dz in range(NZ):
        part = [slab_cols(slab, k, [dz]) for slab in lines for k in range(ROUNDS)]
        part += [tails[h, dz].reshape(plane_cols, 128) for h in range(2)]
        part = jnp.concatenate(part, axis=1)
        part = jnp.dot(part, turned, preferred_element_type=jnp.float32)
        result[dz] = part.astype(jnp.bfloat16).T
        start = pl.multiple_of(lax.rem(my_z + dz, NZ) * plane_cols, plane_cols)
        stores.append(pltpu.make_async_copy(result.at[dz], out.at[:, pl.ds(start, plane_cols)], store_sem))
        stores[-1].start()
    for store in stores:
        store.wait()


def gamma(block_owner, round_order, eps_occ, vir_row, packed, pieces, layout):
    smem = pl.BlockSpec(memory_space=pltpu.SMEM)
    vmem = pl.BlockSpec(memory_space=pltpu.VMEM)
    return pl.pallas_call(
        functools.partial(gamma_kernel, layout),
        in_specs=[smem] * 3 + [vmem] + [pl.BlockSpec(memory_space=pl.ANY)] * (1 + len(pieces)),
        out_specs=pl.BlockSpec(memory_space=pltpu.HBM),
        out_shape=jax.ShapeDtypeStruct((ROWS, NZ * XY * COLS), jnp.bfloat16),
        scratch_shapes=[
            pltpu.VMEM((NC, 4, 4, NZ, LINE, 128), jnp.bfloat16),
            pltpu.VMEM((2, NZ, XY, COLS, 128), jnp.bfloat16),
            pltpu.VMEM((NZ, XY, PACKED, 128), jnp.bfloat16),
            pltpu.VMEM((ROWS, NZ * XY * COLS), jnp.bfloat16),
            pltpu.VMEM((5, 1, 256), jnp.float32),
            pltpu.VMEM((5, ROWS, 256), jnp.bfloat16),
            pltpu.VMEM((NZ, ROWS, XY * COLS), jnp.bfloat16),
            pltpu.SemaphoreType.DMA((NC + 1,)),
            pltpu.SemaphoreType.DMA,
        ],
        compiler_params=pltpu.CompilerParams(vmem_limit_bytes=60 * 1024 * 1024),
    )(block_owner, round_order, eps_occ, vir_row, packed, *pieces)


def on_device(three_centre, eps_occ, eps_vir, block_owner, round_order):
    columns = jnp.swapaxes(three_centre, 1, 2)

    own = pack_line(columns, round_order)
    above = fetch(own, dz=1)
    packed = pack(columns)
    own, above, packed = lax.optimization_barrier((own, above, packed))
    pair = jnp.stack([own, above])
    far = [fetch(pair, dz=d) for d in (2, 4, 6)]
    line = jnp.concatenate([pair] + far)

    packed = exchange(packed, False)
    packed = exchange(jnp.swapaxes(packed, 0, 1), True)

    pieces, layout = [], []

    def keep(array, second, firsts):
        pieces.extend([array, fetch(array, swap=1)])
        layout.extend([(second, 0, firsts), (second, 1, firsts)])

    side = [fetch(line, first=d) for d in (1, 2, 3)]
    low, high = jnp.stack([line, side[0]]), jnp.stack(side[1:])
    keep(low, 0, 0)
    keep(high, 0, 2)
    ahead_low, behind_high = fetch(low, second=1), fetch(high, second=3)
    ahead_high, behind_low = fetch(high, second=1), fetch(low, second=3)
    ahead_low, vir_row = lax.optimization_barrier((ahead_low, eps_vir[None]))
    keep(ahead_low, 1, 0)
    keep(behind_high, 3, 2)
    keep(ahead_high, 1, 2)
    keep(behind_low, 3, 0)
    keep(fetch(ahead_low, second=1), 2, 0)
    keep(fetch(behind_high, second=3), 2, 2)

    return gamma(block_owner, round_order, eps_occ, vir_row, packed, pieces, tuple(layout))[None]


def solution(mesh):
    in_specs = (P(None, "slab", "occ"), P(), P(), P(), P())
    out_specs = P("occ", "slab", None)
    return jax.shard_map(
        on_device, mesh=mesh, in_specs=in_specs, out_specs=out_specs, check_vma=False
    )
```

time: 799 us -> 86.3 us (0.11)
  the two profiles are of different devices: /device:TPU:8 before, /device:TPU:1 now
where the time goes in v3:
time: 86.3 us; the launch traced here: 86 us
  starting transfers between devices  43.1 us (50%)
  waiting for transfers between devices  21.5 us (25%)
  Pallas kernels  14.1 us (16%)
  local copies, waits for them, and re-layouts  5.72 us (7%)
  other arithmetic  1.21 us (1%)
    ppermute x21, starting transfers between devices, fetch(): return lax.ppermute(block, BOTH, pairs)  34.3 us
    ppermute x21, waiting for transfers between devices, fetch(): return lax.ppermute(block, BOTH, pairs)  20 us
    pallas_call x1, Pallas kernels, gamma(): pl.pallas_call(functools.partial(gamma_kernel, layout), in_specs=[smem] *...  10.3 us
    all_to_all x2, starting transfers between devices, exchange(): lax.all_to_all(packed, 'occ', split_axis=0, concat_axis=0, axis_index_gro...  8.82 us
    unnamed x44, local copies, waits for them, and re-layouts  3.96 us
    pallas_call x1, Pallas kernels, pack_line(): pl.pallas_call(line_kernel, in_specs=[pl.BlockSpec(memory_space=pltpu.SME...  2.27 us
  transfers between devices with their start and end apart: 23, of which 7 were waited for; matrix products, arithmetic and copies ran while one was open for 4% of the time, Pallas kernels for 2%

profile of v3, /device:TPU:1, one launch (start us, length us, event | category | flops | bytes accessed | tf_op | source)
XLA Modules:
  0.0 86.0 jit_solution(18127425961850729913)
XLA Ops:
  0.0 2.3 %shard_map.55 = bf16[160,128]{1,0:T(8,128)(2,1)} custom-call(s32[2]{0:T(128)} %order.3, bf16[64,64,160]{2,1,0:T(8,128)(2,1)} %bitcast.13), custom_call_target="tpu_custom_call" | custom-call | tf_op jit(solution)/shard_map/pallas_call | solution.py:59
  2.3 6.5 %collective-permute-start = (bf16[160,128]{1,0:T(8,128)(2,1)}, bf16[160,128]{1,0:T(8,128)(2,1)S(1)}, u32[]{:S(2)}, u32[]{:S(2)}) collective-permute-start(bf16[160,128]{1,0:T(8,128)(2,1)} %shard_map.55), channel_id=1, source_target_pairs={{32,0},{33,1},{36,4},{37,5},{40,8},{41,9},{44,12},{45,13},{48,16},... | collective-permute-start | bytes 122888 | tf_op jit(solution)/shard_map/ppermute | solution.py:36
  8.8 1.5 %shard_map.56 = bf16[8,8,80,128]{3,2,1,0:T(8,128)(2,1)} custom-call(bf16[64,64,160]{2,1,0:T(8,128)(2,1)S(1)} %bitcast.14), custom_call_target="tpu_custom_call" | custom-call | tf_op jit(solution)/shard_map/pallas_call | solution.py:81
  10.3 5.3 %all-to-all-start = ((bf16[8,8,80,128]{3,2,1,0:T(8,128)(2,1)}), bf16[8,8,80,128]{3,2,1,0:T(8,128)(2,1)S(1)}, u32[]{:S(2)}, u32[]{:S(2)}) async-start(bf16[8,8,80,128]{3,2,1,0:T(8,128)(2,1)} %shard_map.56), calls=%async_computation | async-start | bytes 2621440 | tf_op jit(solution)/shard_map/all_to_all | solution.py:93
  15.5 0.1 collective-permute-start.3
  15.6 3.9 %collective-permute-start.2 = (bf16[2,160,128]{2,1,0:T(8,128)(2,1)S(1)}, bf16[2,160,128]{2,1,0:T(8,128)(2,1)S(1)}, u32[]{:S(2)}, u32[]{:S(2)}) collective-permute-start(bf16[2,160,128]{2,1,0:T(8,128)(2,1)S(1)} %pad_maximum_fusion.2), channel_id=1, source_target_pairs={{128,0},{129,1},{132,4},{133,5},{136,8},{137,9},{140,12},{141,13},... | collective-permute-start | bytes 245768 | tf_op jit(solution)/shard_map/ppermute | solution.py:36
  19.6 2.4 %collective-permute-start.1 = (bf16[2,160,128]{2,1,0:T(8,128)(2,1)S(1)}, bf16[2,160,128]{2,1,0:T(8,128)(2,1)S(1)}, u32[]{:S(2)}, u32[]{:S(2)}) collective-permute-start(bf16[2,160,128]{2,1,0:T(8,128)(2,1)S(1)} %pad_maximum_fusion.2), channel_id=1, source_target_pairs={{64,0},{65,1},{68,4},{69,5},{72,8},{73,9},{76,12},{77,13},{80,16},... | collective-permute-start | bytes 245768 | tf_op jit(solution)/shard_map/ppermute | solution.py:36
  22.0 5.7 %collective-permute-done.1 = bf16[2,160,128]{2,1,0:T(8,128)(2,1)S(1)} collective-permute-done((bf16[2,160,128]{2,1,0:T(8,128)(2,1)S(1)}, bf16[2,160,128]{2,1,0:T(8,128)(2,1)S(1)}, u32[]{:S(2)}, u32[]{:S(2)}) %collective-permute-start.1) | collective-permute-done | bytes 81952 | tf_op jit(solution)/shard_map/ppermute | solution.py:36
  27.8 2.6 %collective-permute-start.4 = (bf16[8,160,128]{2,1,0:T(8,128)(2,1)S(1)}, bf16[8,160,128]{2,1,0:T(8,128)(2,1)S(1)}, u32[]{:S(2)}, u32[]{:S(2)}) collective-permute-start(bf16[8,160,128]{2,1,0:T(8,128)(2,1)S(1)} %constant_dynamic-update-slice_fusion), channel_id=1, source_target_pairs={{4,0},{17,1},{8,4},{21,5},{12,8},{25,9},{0,12},{29,13},{20,16},{3,... | collective-permute-start | bytes 983048 | tf_op jit(solution)/shard_map/ppermute | solution.py:36
  30.4 0.0 collective-permute-start.8
  30.4 1.4 %collective-permute-start.7 = (bf16[8,160,128]{2,1,0:T(8,128)(2,1)S(1)}, bf16[8,160,128]{2,1,0:T(8,128)(2,1)}, u32[]{:S(2)}, u32[]{:S(2)}) collective-permute-start(bf16[8,160,128]{2,1,0:T(8,128)(2,1)S(1)} %constant_dynamic-update-slice_fusion), channel_id=1, source_target_pairs={{8,0},{3,1},{12,4},{7,5},{0,8},{11,9},{4,12},{15,13},{24,16},{19,1... | collective-permute-start | bytes 983048 | tf_op jit(solution)/shard_map/ppermute | solution.py:36
  31.8 1.5 %all-to-all-done = bf16[8,8,80,128]{3,2,1,0:T(8,128)(2,1)S(1)} async-done(((bf16[8,8,80,128]{3,2,1,0:T(8,128)(2,1)}), bf16[8,8,80,128]{3,2,1,0:T(8,128)(2,1)S(1)}, u32[]{:S(2)}, u32[]{:S(2)}) %all-to-all-start) | async-done | bytes 1310752 | tf_op jit(solution)/shard_map/all_to_all | solution.py:93
  33.2 1.1 %copy.9 = bf16[8,8,80,128]{3,2,0,1:T(8,128)(2,1)} copy(bf16[8,8,80,128]{3,2,1,0:T(8,128)(2,1)S(1)} %all-to-all-done) | data formatting | bytes 2621440 | tf_op jit(solution)/shard_map/all_to_all | solution.py:93
  34.4 3.6 %all-to-all-start.1 = ((bf16[8,8,80,128]{3,2,1,0:T(8,128)(2,1)}), bf16[8,8,80,128]{3,2,1,0:T(8,128)(2,1)S(1)}, u32[]{:S(2)}, u32[]{:S(2)}) async-start(bf16[8,8,80,128]{3,2,1,0:T(8,128)(2,1)} %bitcast.12), calls=%async_computation.1 | async-start | bytes 2621440 | tf_op jit(solution)/shard_map/all_to_all | solution.py:93
  38.0 0.0 copy-start.19
  38.0 0.1 pad_maximum_fusion.refs_0_
  38.1 0.6 collective-permute-start.15
  38.6 4.5 %collective-permute-start.6 = (bf16[2,8,160,128]{3,2,1,0:T(8,128)(2,1)S(1)}, bf16[2,8,160,128]{3,2,1,0:T(8,128)(2,1)S(1)}, u32[]{:S(2)}, u32[]{:S(2)}) collective-permute-start(bf16[2,8,160,128]{3,2,1,0:T(8,128)(2,1)S(1)} %pad_maximum_fusion.refs_0_), channel_id=1, source_target_pairs={{1,0},{0,1},{5,4},{4,5},{9,8},{8,9},{13,12},{12,13},{17,16},{16,17... | collective-permute-start | bytes 1966088 | tf_op jit(solution)/shard_map/ppermute | solution.py:36
  43.1 0.9 %collective-permute-start.5 = (bf16[2,8,160,128]{3,2,1,0:T(8,128)(2,1)S(1)}, bf16[2,8,160,128]{3,2,1,0:T(8,128)(2,1)S(1)}, u32[]{:S(2)}, u32[]{:S(2)}) collective-permute-start(bf16[2,8,160,128]{3,2,1,0:T(8,128)(2,1)S(1)} %pad_maximum_fusion.refs_0_), channel_id=1, source_target_pairs={{16,0},{5,1},{20,4},{9,5},{24,8},{13,9},{28,12},{1,13},{2,16},{21,... | collective-permute-start | bytes 1966088 | tf_op jit(solution)/shard_map/ppermute | solution.py:36
  44.0 0.0 collective-permute-done.8
  44.0 0.0 collective-permute-done.7
  44.0 0.7 copy-done.18
  44.7 1.1 %pad_maximum_fusion.1.refs_2_ = bf16[2,8,160,128]{3,2,1,0:T(8,128)(2,1)S(1)} fusion(bf16[1,8,160,128]{3,2,1,0:T(8,128)(2,1)} %bitcast.17, bf16[1,8,160,128]{3,2,1,0:T(8,128)(2,1)} %bitcast.6), kind=kLoop, calls=%fused_computation.2 | loop fusion | flops 327680 | bytes 1310720 | tf_op jit(solution)/shard_map/stack | solution.py:236
  45.8 0.7 collective-permute-start.11
  46.5 0.6 broadcast_in_dim.6.eps_vir
  47.1 2.1 %collective-permute-start.13 = (bf16[2,8,160,128]{3,2,1,0:T(8,128)(2,1)S(1)}, bf16[2,8,160,128]{3,2,1,0:T(8,128)(2,1)S(1)}, u32[]{:S(2)}, u32[]{:S(2)}) collective-permute-start(bf16[2,8,160,128]{3,2,1,0:T(8,128)(2,1)S(1)} %pad_maximum_fusion.1.refs_2_), channel_id=1, source_target_pairs={{16,0},{5,1},{20,4},{9,5},{24,8},{13,9},{28,12},{1,13},{2,16},{21,... | collective-permute-start | bytes 1966088 | tf_op jit(solution)/shard_map/ppermute | solution.py:36
  49.2 3.6 %collective-permute-done.5.refs_4_ = bf16[2,8,160,128]{3,2,1,0:T(8,128)(2,1)S(1)} collective-permute-done((bf16[2,8,160,128]{3,2,1,0:T(8,128)(2,1)S(1)}, bf16[2,8,160,128]{3,2,1,0:T(8,128)(2,1)S(1)}, u32[]{:S(2)}, u32[]{:S(2)}) %collective-permute-start.5) | collective-permute-done | bytes 655392 | tf_op jit(solution)/shard_map/ppermute | solution.py:36
  52.8 0.8 collective-permute-start.9
  53.7 0.0 collective-permute-done.15.refs_10_
  53.7 0.1 collective-permute-start.16
  53.8 0.0 collective-permute-done.6.refs_1_
  53.8 1.7 %collective-permute-start.17 = (bf16[2,8,160,128]{3,2,1,0:T(8,128)(2,1)S(1)}, bf16[2,8,160,128]{3,2,1,0:T(8,128)(2,1)S(1)}, u32[]{:S(2)}, u32[]{:S(2)}) collective-permute-start(bf16[2,8,160,128]{3,2,1,0:T(8,128)(2,1)S(1)} %collective-permute-done.5.refs_4_), channel_id=1, source_target_pairs={{16,0},{5,1},{20,4},{9,5},{24,8},{13,9},{28,12},{1,13},{2,16},{21,... | collective-permute-start | bytes 1966088 | tf_op jit(solution)/shard_map/ppermute | solution.py:36
  55.4 1.9 %collective-permute-done.11.refs_6_ = bf16[2,8,160,128]{3,2,1,0:T(8,128)(2,1)S(1)} collective-permute-done((bf16[2,8,160,128]{3,2,1,0:T(8,128)(2,1)S(1)}, bf16[2,8,160,128]{3,2,1,0:T(8,128)(2,1)S(1)}, u32[]{:S(2)}, u32[]{:S(2)}) %collective-permute-start.11) | collective-permute-done | bytes 655392 | tf_op jit(solution)/shard_map/ppermute | solution.py:36
  57.3 0.0 collective-permute-start.19
  57.3 2.5 %collective-permute-done.13.refs_8_ = bf16[2,8,160,128]{3,2,1,0:T(8,128)(2,1)S(1)} collective-permute-done((bf16[2,8,160,128]{3,2,1,0:T(8,128)(2,1)S(1)}, bf16[2,8,160,128]{3,2,1,0:T(8,128)(2,1)S(1)}, u32[]{:S(2)}, u32[]{:S(2)}) %collective-permute-start.13) | collective-permute-done | bytes 655392 | tf_op jit(solution)/shard_map/ppermute | solution.py:36
  59.9 0.9 collective-permute-start.10
  60.7 0.1 collective-permute-start.12
  60.9 0.4 collective-permute-start.14
  61.2 5.6 %collective-permute-done.17.refs_12_ = bf16[2,8,160,128]{3,2,1,0:T(8,128)(2,1)S(1)} collective-permute-done((bf16[2,8,160,128]{3,2,1,0:T(8,128)(2,1)S(1)}, bf16[2,8,160,128]{3,2,1,0:T(8,128)(2,1)S(1)}, u32[]{:S(2)}, u32[]{:S(2)}) %collective-permute-start.17) | collective-permute-done | bytes 655392 | tf_op jit(solution)/shard_map/ppermute | solution.py:36
  66.9 0.8 collective-permute-start.18
  67.7 0.6 collective-permute-done.19.refs_14_
  68.3 4.0 %collective-permute-start.20 = (bf16[2,8,160,128]{3,2,1,0:T(8,128)(2,1)S(1)}, bf16[2,8,160,128]{3,2,1,0:T(8,128)(2,1)}, u32[]{:S(2)}, u32[]{:S(2)}) collective-permute-start(bf16[2,8,160,128]{3,2,1,0:T(8,128)(2,1)S(1)} %collective-permute-done.19.refs_14_), channel_id=1, source_target_pairs={{1,0},{0,1},{5,4},{4,5},{9,8},{8,9},{13,12},{12,13},{17,16},{16,17... | collective-permute-start | bytes 1966088 | tf_op jit(solution)/shard_map/ppermute | solution.py:36
  72.4 0.8 copy-done.13
  73.1 0.2 copy-done.15
  73.4 0.2 copy-done.14
  73.6 0.9 copy-done.16
  74.5 1.1 %copy-done.1 = bf16[8,8,80,128]{3,2,1,0:T(8,128)(2,1)} copy-done((bf16[8,8,80,128]{3,2,1,0:T(8,128)(2,1)}, bf16[8,8,80,128]{3,2,1,0:T(8,128)(2,1)S(1)}, u32[]{:S(2)}) %copy-start.1) | copy-done | bytes 1310744
  75.5 10.3 %shard_map.57 = bf16[160,4096]{1,0:T(8,128)(2,1)} custom-call(s32[64]{0:T(128)} %owner.1, s32[2]{0:T(128)} %order.3, f32[16]{0:T(128)} %eps_occ.1, f32[1,2560]{1,0:T(1,128)} %broadcast_in_dim.6.eps_vir, bf16[8,8,80,128]{3,2,1,0:T(8,128)(2,1)} %copy-done.1, bf16[2,8,160,128]{3,2,1,0:T(8,128)(2,1)} %copy-done.2, bf16[2,8,160,128]{3,2,1,0:T(8,128)(2,1)} %copy-done.5, ...), custom_call_target="tpu_custom_call" | custom-call | tf_op jit(solution)/shard_map/pallas_call | solution.py:195
  (51 shorter events, 0.2 us)
Async XLA Ops:
  0.0 8.8 %copy-start = (bf16[64,160,64]{1,2,0:T(8,128)(2,1)S(1)}, bf16[64,160,64]{1,2,0:T(8,128)(2,1)}, u32[]{:S(2)}) copy-start(bf16[64,160,64]{1,2,0:T(8,128)(2,1)} %param.5) | copy-start | bytes 3932164
  2.3 8.0 %collective-permute-start = (bf16[160,128]{1,0:T(8,128)(2,1)}, bf16[160,128]{1,0:T(8,128)(2,1)S(1)}, u32[]{:S(2)}, u32[]{:S(2)}) collective-permute-start(bf16[160,128]{1,0:T(8,128)(2,1)} %shard_map.55), channel_id=1, source_target_pairs={{32,0},{33,1},{36,4},{37,5},{40,8},{41,9},{44,12},{45,13},{48,16},... | collective-permute-start | bytes 122888 | tf_op jit(solution)/shard_map/ppermute | solution.py:36
  10.3 5.3 %copy-start.17 = (bf16[160,128]{1,0:T(8,128)(2,1)S(1)}, bf16[160,128]{1,0:T(8,128)(2,1)}, u32[]{:S(2)}) copy-start(bf16[160,128]{1,0:T(8,128)(2,1)} %shard_map.55) | copy-start | bytes 122884
  10.3 23.0 %all-to-all-start = ((bf16[8,8,80,128]{3,2,1,0:T(8,128)(2,1)}), bf16[8,8,80,128]{3,2,1,0:T(8,128)(2,1)S(1)}, u32[]{:S(2)}, u32[]{:S(2)}) async-start(bf16[8,8,80,128]{3,2,1,0:T(8,128)(2,1)} %shard_map.56), calls=%async_computation | async-start | bytes 2621440 | tf_op jit(solution)/shard_map/all_to_all | solution.py:93
  15.5 12.2 %collective-permute-start.3 = (bf16[2,160,128]{2,1,0:T(8,128)(2,1)S(1)}, bf16[2,160,128]{2,1,0:T(8,128)(2,1)S(1)}, u32[]{:S(2)}, u32[]{:S(2)}) collective-permute-start(bf16[2,160,128]{2,1,0:T(8,128)(2,1)S(1)} %pad_maximum_fusion.2), channel_id=1, source_target_pairs={{192,0},{193,1},{196,4},{197,5},{200,8},{201,9},{204,12},{205,13},... | collective-permute-start | bytes 245768 | tf_op jit(solution)/shard_map/ppermute | solution.py:36
  15.6 12.1 %collective-permute-start.2 = (bf16[2,160,128]{2,1,0:T(8,128)(2,1)S(1)}, bf16[2,160,128]{2,1,0:T(8,128)(2,1)S(1)}, u32[]{:S(2)}, u32[]{:S(2)}) collective-permute-start(bf16[2,160,128]{2,1,0:T(8,128)(2,1)S(1)} %pad_maximum_fusion.2), channel_id=1, source_target_pairs={{128,0},{129,1},{132,4},{133,5},{136,8},{137,9},{140,12},{141,13},... | collective-permute-start | bytes 245768 | tf_op jit(solution)/shard_map/ppermute | solution.py:36
  19.6 8.1 %collective-permute-start.1 = (bf16[2,160,128]{2,1,0:T(8,128)(2,1)S(1)}, bf16[2,160,128]{2,1,0:T(8,128)(2,1)S(1)}, u32[]{:S(2)}, u32[]{:S(2)}) collective-permute-start(bf16[2,160,128]{2,1,0:T(8,128)(2,1)S(1)} %pad_maximum_fusion.2), channel_id=1, source_target_pairs={{64,0},{65,1},{68,4},{69,5},{72,8},{73,9},{76,12},{77,13},{80,16},... | collective-permute-start | bytes 245768 | tf_op jit(solution)/shard_map/ppermute | solution.py:36
  27.8 10.2 %collective-permute-start.4 = (bf16[8,160,128]{2,1,0:T(8,128)(2,1)S(1)}, bf16[8,160,128]{2,1,0:T(8,128)(2,1)S(1)}, u32[]{:S(2)}, u32[]{:S(2)}) collective-permute-start(bf16[8,160,128]{2,1,0:T(8,128)(2,1)S(1)} %constant_dynamic-update-slice_fusion), channel_id=1, source_target_pairs={{4,0},{17,1},{8,4},{21,5},{12,8},{25,9},{0,12},{29,13},{20,16},{3,... | collective-permute-start | bytes 983048 | tf_op jit(solution)/shard_map/ppermute | solution.py:36
  30.4 13.6 %collective-permute-start.8 = (bf16[8,160,128]{2,1,0:T(8,128)(2,1)S(1)}, bf16[8,160,128]{2,1,0:T(8,128)(2,1)S(1)}, u32[]{:S(2)}, u32[]{:S(2)}) collective-permute-start(bf16[8,160,128]{2,1,0:T(8,128)(2,1)S(1)} %constant_dynamic-update-slice_fusion), channel_id=1, source_target_pairs={{12,0},{19,1},{0,4},{23,5},{4,8},{27,9},{8,12},{31,13},{28,16},{1,... | collective-permute-start | bytes 983048 | tf_op jit(solution)/shard_map/ppermute | solution.py:36
  30.4 13.6 %collective-permute-start.7 = (bf16[8,160,128]{2,1,0:T(8,128)(2,1)S(1)}, bf16[8,160,128]{2,1,0:T(8,128)(2,1)}, u32[]{:S(2)}, u32[]{:S(2)}) collective-permute-start(bf16[8,160,128]{2,1,0:T(8,128)(2,1)S(1)} %constant_dynamic-update-slice_fusion), channel_id=1, source_target_pairs={{8,0},{3,1},{12,4},{7,5},{0,8},{11,9},{4,12},{15,13},{24,16},{19,1... | collective-permute-start | bytes 983048 | tf_op jit(solution)/shard_map/ppermute | solution.py:36
  34.4 40.1 %all-to-all-start.1 = ((bf16[8,8,80,128]{3,2,1,0:T(8,128)(2,1)}), bf16[8,8,80,128]{3,2,1,0:T(8,128)(2,1)S(1)}, u32[]{:S(2)}, u32[]{:S(2)}) async-start(bf16[8,8,80,128]{3,2,1,0:T(8,128)(2,1)} %bitcast.12), calls=%async_computation.1 | async-start | bytes 2621440 | tf_op jit(solution)/shard_map/all_to_all | solution.py:93
  38.0 8.6 %copy-start.19 = (f32[2560]{0:T(1024)S(1)}, f32[2560]{0:T(1024)}, u32[]{:S(2)}) copy-start(f32[2560]{0:T(1024)} %param.7) | copy-start | bytes 30724
  38.0 36.4 %copy-start.2 = (bf16[2,8,160,128]{3,2,1,0:T(8,128)(2,1)}, bf16[2,8,160,128]{3,2,1,0:T(8,128)(2,1)S(1)}, u32[]{:S(2)}) copy-start(bf16[2,8,160,128]{3,2,1,0:T(8,128)(2,1)S(1)} %pad_maximum_fusion.refs_0_) | copy-start | bytes 1966084
  38.1 15.6 %collective-permute-start.15 = (bf16[2,8,160,128]{3,2,1,0:T(8,128)(2,1)S(1)}, bf16[2,8,160,128]{3,2,1,0:T(8,128)(2,1)S(1)}, u32[]{:S(2)}, u32[]{:S(2)}) collective-permute-start(bf16[2,8,160,128]{3,2,1,0:T(8,128)(2,1)S(1)} %pad_maximum_fusion.refs_0_), channel_id=1, source_target_pairs={{18,0},{13,1},{22,4},{1,5},{26,8},{5,9},{30,12},{9,13},{0,16},{29,... | collective-permute-start | bytes 1966088 | tf_op jit(solution)/shard_map/ppermute | solution.py:36
  38.6 15.2 %collective-permute-start.6 = (bf16[2,8,160,128]{3,2,1,0:T(8,128)(2,1)S(1)}, bf16[2,8,160,128]{3,2,1,0:T(8,128)(2,1)S(1)}, u32[]{:S(2)}, u32[]{:S(2)}) collective-permute-start(bf16[2,8,160,128]{3,2,1,0:T(8,128)(2,1)S(1)} %pad_maximum_fusion.refs_0_), channel_id=1, source_target_pairs={{1,0},{0,1},{5,4},{4,5},{9,8},{8,9},{13,12},{12,13},{17,16},{16,17... | collective-permute-start | bytes 1966088 | tf_op jit(solution)/shard_map/ppermute | solution.py:36
  43.1 9.8 %collective-permute-start.5 = (bf16[2,8,160,128]{3,2,1,0:T(8,128)(2,1)S(1)}, bf16[2,8,160,128]{3,2,1,0:T(8,128)(2,1)S(1)}, u32[]{:S(2)}, u32[]{:S(2)}) collective-permute-start(bf16[2,8,160,128]{3,2,1,0:T(8,128)(2,1)S(1)} %pad_maximum_fusion.refs_0_), channel_id=1, source_target_pairs={{16,0},{5,1},{20,4},{9,5},{24,8},{13,9},{28,12},{1,13},{2,16},{21,... | collective-permute-start | bytes 1966088 | tf_op jit(solution)/shard_map/ppermute | solution.py:36
  44.0 0.7 copy-start.18
  45.8 28.6 %copy-start.3 = (bf16[2,8,160,128]{3,2,1,0:T(8,128)(2,1)}, bf16[2,8,160,128]{3,2,1,0:T(8,128)(2,1)S(1)}, u32[]{:S(2)}) copy-start(bf16[2,8,160,128]{3,2,1,0:T(8,128)(2,1)S(1)} %pad_maximum_fusion.1.refs_2_) | copy-start | bytes 1966084
  45.8 11.5 %collective-permute-start.11 = (bf16[2,8,160,128]{3,2,1,0:T(8,128)(2,1)S(1)}, bf16[2,8,160,128]{3,2,1,0:T(8,128)(2,1)S(1)}, u32[]{:S(2)}, u32[]{:S(2)}) collective-permute-start(bf16[2,8,160,128]{3,2,1,0:T(8,128)(2,1)S(1)} %pad_maximum_fusion.1.refs_2_), channel_id=1, source_target_pairs={{18,0},{13,1},{22,4},{1,5},{26,8},{5,9},{30,12},{9,13},{0,16},{29,... | collective-permute-start | bytes 1966088 | tf_op jit(solution)/shard_map/ppermute | solution.py:36
  47.1 12.7 %collective-permute-start.13 = (bf16[2,8,160,128]{3,2,1,0:T(8,128)(2,1)S(1)}, bf16[2,8,160,128]{3,2,1,0:T(8,128)(2,1)S(1)}, u32[]{:S(2)}, u32[]{:S(2)}) collective-permute-start(bf16[2,8,160,128]{3,2,1,0:T(8,128)(2,1)S(1)} %pad_maximum_fusion.1.refs_2_), channel_id=1, source_target_pairs={{16,0},{5,1},{20,4},{9,5},{24,8},{13,9},{28,12},{1,13},{2,16},{21,... | collective-permute-start | bytes 1966088 | tf_op jit(solution)/shard_map/ppermute | solution.py:36
  52.8 19.4 %copy-start.6 = (bf16[2,8,160,128]{3,2,1,0:T(8,128)(2,1)}, bf16[2,8,160,128]{3,2,1,0:T(8,128)(2,1)S(1)}, u32[]{:S(2)}) copy-start(bf16[2,8,160,128]{3,2,1,0:T(8,128)(2,1)S(1)} %collective-permute-done.5.refs_4_) | copy-start | bytes 1966084
  52.8 7.9 %collective-permute-start.9 = (bf16[2,8,160,128]{3,2,1,0:T(8,128)(2,1)S(1)}, bf16[2,8,160,128]{3,2,1,0:T(8,128)(2,1)S(1)}, u32[]{:S(2)}, u32[]{:S(2)}) collective-permute-start(bf16[2,8,160,128]{3,2,1,0:T(8,128)(2,1)S(1)} %pad_maximum_fusion.1.refs_2_), channel_id=1, source_target_pairs={{1,0},{0,1},{5,4},{4,5},{9,8},{8,9},{13,12},{12,13},{17,16},{16,17... | collective-permute-start | bytes 1966088 | tf_op jit(solution)/shard_map/ppermute | solution.py:36
  53.7 20.8 %copy-start.4 = (bf16[2,8,160,128]{3,2,1,0:T(8,128)(2,1)}, bf16[2,8,160,128]{3,2,1,0:T(8,128)(2,1)S(1)}, u32[]{:S(2)}) copy-start(bf16[2,8,160,128]{3,2,1,0:T(8,128)(2,1)S(1)} %collective-permute-done.15.refs_10_) | copy-start | bytes 1966084
  53.7 7.2 %collective-permute-start.16 = (bf16[2,8,160,128]{3,2,1,0:T(8,128)(2,1)S(1)}, bf16[2,8,160,128]{3,2,1,0:T(8,128)(2,1)S(1)}, u32[]{:S(2)}, u32[]{:S(2)}) collective-permute-start(bf16[2,8,160,128]{3,2,1,0:T(8,128)(2,1)S(1)} %collective-permute-done.15.refs_10_), channel_id=1, source_target_pairs={{1,0},{0,1},{5,4},{4,5},{9,8},{8,9},{13,12},{12,13},{17,16},{16,17... | collective-permute-start | bytes 1966088 | tf_op jit(solution)/shard_map/ppermute | solution.py:36
  53.8 18.5 %copy-start.5 = (bf16[2,8,160,128]{3,2,1,0:T(8,128)(2,1)}, bf16[2,8,160,128]{3,2,1,0:T(8,128)(2,1)S(1)}, u32[]{:S(2)}) copy-start(bf16[2,8,160,128]{3,2,1,0:T(8,128)(2,1)S(1)} %collective-permute-done.6.refs_1_) | copy-start | bytes 1966084
  53.8 13.1 %collective-permute-start.17 = (bf16[2,8,160,128]{3,2,1,0:T(8,128)(2,1)S(1)}, bf16[2,8,160,128]{3,2,1,0:T(8,128)(2,1)S(1)}, u32[]{:S(2)}, u32[]{:S(2)}) collective-permute-start(bf16[2,8,160,128]{3,2,1,0:T(8,128)(2,1)S(1)} %collective-permute-done.5.refs_4_), channel_id=1, source_target_pairs={{16,0},{5,1},{20,4},{9,5},{24,8},{13,9},{28,12},{1,13},{2,16},{21,... | collective-permute-start | bytes 1966088 | tf_op jit(solution)/shard_map/ppermute | solution.py:36
  57.3 15.0 %copy-start.7 = (bf16[2,8,160,128]{3,2,1,0:T(8,128)(2,1)}, bf16[2,8,160,128]{3,2,1,0:T(8,128)(2,1)S(1)}, u32[]{:S(2)}) copy-start(bf16[2,8,160,128]{3,2,1,0:T(8,128)(2,1)S(1)} %collective-permute-done.11.refs_6_) | copy-start | bytes 1966084
  57.3 10.9 %collective-permute-start.19 = (bf16[2,8,160,128]{3,2,1,0:T(8,128)(2,1)S(1)}, bf16[2,8,160,128]{3,2,1,0:T(8,128)(2,1)S(1)}, u32[]{:S(2)}, u32[]{:S(2)}) collective-permute-start(bf16[2,8,160,128]{3,2,1,0:T(8,128)(2,1)S(1)} %collective-permute-done.11.refs_6_), channel_id=1, source_target_pairs={{18,0},{13,1},{22,4},{1,5},{26,8},{5,9},{30,12},{9,13},{0,16},{29,... | collective-permute-start | bytes 1966088 | tf_op jit(solution)/shard_map/ppermute | solution.py:36
  59.9 12.5 %copy-start.8 = (bf16[2,8,160,128]{3,2,1,0:T(8,128)(2,1)}, bf16[2,8,160,128]{3,2,1,0:T(8,128)(2,1)S(1)}, u32[]{:S(2)}) copy-start(bf16[2,8,160,128]{3,2,1,0:T(8,128)(2,1)S(1)} %collective-permute-done.13.refs_8_) | copy-start | bytes 1966084
  59.9 12.4 %collective-permute-start.10 = (bf16[2,8,160,128]{3,2,1,0:T(8,128)(2,1)S(1)}, bf16[2,8,160,128]{3,2,1,0:T(8,128)(2,1)S(1)}, u32[]{:S(2)}, u32[]{:S(2)}) collective-permute-start(bf16[2,8,160,128]{3,2,1,0:T(8,128)(2,1)S(1)} %collective-permute-done.5.refs_4_), channel_id=1, source_target_pairs={{1,0},{0,1},{5,4},{4,5},{9,8},{8,9},{13,12},{12,13},{17,16},{16,17... | collective-permute-start | bytes 1966088 | tf_op jit(solution)/shard_map/ppermute | solution.py:36
  60.7 11.6 %copy-start.9 = (bf16[2,8,160,128]{3,2,1,0:T(8,128)(2,1)}, bf16[2,8,160,128]{3,2,1,0:T(8,128)(2,1)S(1)}, u32[]{:S(2)}) copy-start(bf16[2,8,160,128]{3,2,1,0:T(8,128)(2,1)S(1)} %collective-permute-done.9.refs_3_) | copy-start | bytes 1966084
  60.7 11.5 %collective-permute-start.12 = (bf16[2,8,160,128]{3,2,1,0:T(8,128)(2,1)S(1)}, bf16[2,8,160,128]{3,2,1,0:T(8,128)(2,1)S(1)}, u32[]{:S(2)}, u32[]{:S(2)}) collective-permute-start(bf16[2,8,160,128]{3,2,1,0:T(8,128)(2,1)S(1)} %collective-permute-done.11.refs_6_), channel_id=1, source_target_pairs={{1,0},{0,1},{5,4},{4,5},{9,8},{8,9},{13,12},{12,13},{17,16},{16,17... | collective-permute-start | bytes 1966088 | tf_op jit(solution)/shard_map/ppermute | solution.py:36
  60.8 11.5 %copy-start.10 = (bf16[2,8,160,128]{3,2,1,0:T(8,128)(2,1)}, bf16[2,8,160,128]{3,2,1,0:T(8,128)(2,1)S(1)}, u32[]{:S(2)}) copy-start(bf16[2,8,160,128]{3,2,1,0:T(8,128)(2,1)S(1)} %collective-permute-done.16.refs_11_) | copy-start | bytes 1966084
  60.9 11.4 %collective-permute-start.14 = (bf16[2,8,160,128]{3,2,1,0:T(8,128)(2,1)S(1)}, bf16[2,8,160,128]{3,2,1,0:T(8,128)(2,1)S(1)}, u32[]{:S(2)}, u32[]{:S(2)}) collective-permute-start(bf16[2,8,160,128]{3,2,1,0:T(8,128)(2,1)S(1)} %collective-permute-done.13.refs_8_), channel_id=1, source_target_pairs={{1,0},{0,1},{5,4},{4,5},{9,8},{8,9},{13,12},{12,13},{17,16},{16,17... | collective-permute-start | bytes 1966088 | tf_op jit(solution)/shard_map/ppermute | solution.py:36
  66.9 5.5 %copy-start.11 = (bf16[2,8,160,128]{3,2,1,0:T(8,128)(2,1)}, bf16[2,8,160,128]{3,2,1,0:T(8,128)(2,1)S(1)}, u32[]{:S(2)}) copy-start(bf16[2,8,160,128]{3,2,1,0:T(8,128)(2,1)S(1)} %collective-permute-done.17.refs_12_) | copy-start | bytes 1966084
  66.9 5.4 %collective-permute-start.18 = (bf16[2,8,160,128]{3,2,1,0:T(8,128)(2,1)S(1)}, bf16[2,8,160,128]{3,2,1,0:T(8,128)(2,1)S(1)}, u32[]{:S(2)}, u32[]{:S(2)}) collective-permute-start(bf16[2,8,160,128]{3,2,1,0:T(8,128)(2,1)S(1)} %collective-permute-done.17.refs_12_), channel_id=1, source_target_pairs={{1,0},{0,1},{5,4},{4,5},{9,8},{8,9},{13,12},{12,13},{17,16},{16,17... | collective-permute-start | bytes 1966088 | tf_op jit(solution)/shard_map/ppermute | solution.py:36
  68.3 4.1 %copy-start.12 = (bf16[2,8,160,128]{3,2,1,0:T(8,128)(2,1)}, bf16[2,8,160,128]{3,2,1,0:T(8,128)(2,1)S(1)}, u32[]{:S(2)}) copy-start(bf16[2,8,160,128]{3,2,1,0:T(8,128)(2,1)S(1)} %collective-permute-done.19.refs_14_) | copy-start | bytes 1966084
  68.3 6.1 %collective-permute-start.20 = (bf16[2,8,160,128]{3,2,1,0:T(8,128)(2,1)S(1)}, bf16[2,8,160,128]{3,2,1,0:T(8,128)(2,1)}, u32[]{:S(2)}, u32[]{:S(2)}) collective-permute-start(bf16[2,8,160,128]{3,2,1,0:T(8,128)(2,1)S(1)} %collective-permute-done.19.refs_14_), channel_id=1, source_target_pairs={{1,0},{0,1},{5,4},{4,5},{9,8},{8,9},{13,12},{12,13},{17,16},{16,17... | collective-permute-start | bytes 1966088 | tf_op jit(solution)/shard_map/ppermute | solution.py:36
  72.2 0.9 %copy-start.13 = (bf16[2,8,160,128]{3,2,1,0:T(8,128)(2,1)}, bf16[2,8,160,128]{3,2,1,0:T(8,128)(2,1)S(1)}, u32[]{:S(2)}) copy-start(bf16[2,8,160,128]{3,2,1,0:T(8,128)(2,1)S(1)} %collective-permute-done.10.refs_5_) | copy-start | bytes 1966084
  72.2 1.1 %copy-start.15 = (bf16[2,8,160,128]{3,2,1,0:T(8,128)(2,1)}, bf16[2,8,160,128]{3,2,1,0:T(8,128)(2,1)S(1)}, u32[]{:S(2)}) copy-start(bf16[2,8,160,128]{3,2,1,0:T(8,128)(2,1)S(1)} %collective-permute-done.14.refs_9_) | copy-start | bytes 1966084
  72.3 1.3 %copy-start.14 = (bf16[2,8,160,128]{3,2,1,0:T(8,128)(2,1)}, bf16[2,8,160,128]{3,2,1,0:T(8,128)(2,1)S(1)}, u32[]{:S(2)}) copy-start(bf16[2,8,160,128]{3,2,1,0:T(8,128)(2,1)S(1)} %collective-permute-done.12.refs_7_) | copy-start | bytes 1966084
  73.6 0.9 copy-start.16
  74.5 1.1 %copy-start.1 = (bf16[8,8,80,128]{3,2,1,0:T(8,128)(2,1)}, bf16[8,8,80,128]{3,2,1,0:T(8,128)(2,1)S(1)}, u32[]{:S(2)}) copy-start(bf16[8,8,80,128]{3,2,1,0:T(8,128)(2,1)S(1)} %all-to-all-done.1.packed) | copy-start | bytes 3932164

commit v4 on v3

--- a/solution.py
+++ b/solution.py
@@ -94,7 +94,7 @@
 
 
 def gamma_kernel(layout, owner, order, eps_occ, eps_vir, packed, *refs):
-    pieces, (out, weights, tails, block_ref, rows, right, amplitude, result, load_sems, store_sem) = (
+    pieces, (out, weights, tails, block_ref, rows, right, amplitude, partial, result, load_sems, store_sem) = (
         refs[:len(layout)], refs[len(layout):])
     my_z, my_x, my_y, my_core = position()
     fetch_block = pltpu.make_async_copy(packed, block_ref, load_sems.at[NC])
@@ -153,13 +153,27 @@
     def slab_cols(lines, k, planes):
         return jnp.concatenate([v[z, k * COLS:(k + 1) * COLS] for z in planes for v in lines], axis=0)
 
-    for swap in range(NC):
-        for copy in copies[swap]:
-            copy.wait()
-        for h in range(2):
-            lines = [line_of(swap, h, spot) for spot in range(XY)]
-            p = 2 * h + (1 - my_core if swap else my_core)
-            contract(p, [slab_cols(lines, k, range(NZ)) for k in range(ROUNDS)])
+    lines = [[line_of(swap, h, spot) for spot in range(XY)] for swap in range(NC) for h in range(2)]
+    slabs = [2 * h + (1 - my_core if swap else my_core) for swap in range(NC) for h in range(2)] + [4]
+
+    def turned(first, last):
+        return jnp.concatenate([amplitude[p] for p in slabs[first:last]], axis=1).T
+
+    for copy in copies[0]:
+        copy.wait()
+    for n in range(2):
+        contract(slabs[n], [slab_cols(lines[n], k, range(NZ)) for k in range(ROUNDS)])
+    by_slab = turned(0, 2)
+    for dz in range(0, NZ, 2):
+        planes = range(dz, dz + 2)
+        part = [slab_cols(lines[n], k, planes) for n in range(2) for k in range(ROUNDS)]
+        part = jnp.dot(jnp.concatenate(part, axis=1), by_slab, preferred_element_type=jnp.float32)
+        partial[dz:dz + 2] = part.reshape(2, plane_cols, ROWS)
+
+    for copy in copies[1]:
+        copy.wait()
+    for n in range(2, 4):
+        contract(slabs[n], [slab_cols(lines[n], k, range(NZ)) for k in range(ROUNDS)])
     half = COLS // 2
     for h in range(2):
         for spot in range(XY):
@@ -172,19 +186,19 @@
                 tails[h, z, spot, half:] = jnp.concatenate([low[:, 64:], high[:, 64:]], axis=1)
     contract(4, [tails[h].reshape(NZ * plane_cols, 128) for h in range(2)])
 
-    slabs = [2 * h + (1 - my_core if swap else my_core) for swap in range(NC) for h in range(2)] + [4]
-    turned = jnp.concatenate([amplitude[p] for p in slabs], axis=1).T
-    lines = [[line_of(swap, h, spot) for spot in range(XY)] for swap in range(NC) for h in range(2)]
+    by_slab = turned(2, 5)
     stores = []
-    for dz in range(NZ):
-        part = [slab_cols(slab, k, [dz]) for slab in lines for k in range(ROUNDS)]
-        part += [tails[h, dz].reshape(plane_cols, 128) for h in range(2)]
-        part = jnp.concatenate(part, axis=1)
-        part = jnp.dot(part, turned, preferred_element_type=jnp.float32)
-        result[dz] = part.astype(jnp.bfloat16).T
-        start = pl.multiple_of(lax.rem(my_z + dz, NZ) * plane_cols, plane_cols)
-        stores.append(pltpu.make_async_copy(result.at[dz], out.at[:, pl.ds(start, plane_cols)], store_sem))
-        stores[-1].start()
+    for dz in range(0, NZ, 2):
+        planes = range(dz, dz + 2)
+        part = [slab_cols(lines[n], k, planes) for n in range(2, 4) for k in range(ROUNDS)]
+        part += [tails[h, dz:dz + 2].reshape(2 * plane_cols, 128) for h in range(2)]
+        part = jnp.dot(jnp.concatenate(part, axis=1), by_slab, preferred_element_type=jnp.float32)
+        part = part.reshape(2, plane_cols, ROWS) + partial[dz:dz + 2]
+        for z in planes:
+            result[z] = part[z - dz].astype(jnp.bfloat16).T
+            start = pl.multiple_of(lax.rem(my_z + z, NZ) * plane_cols, plane_cols)
+            stores.append(pltpu.make_async_copy(result.at[z], out.at[:, pl.ds(start, plane_cols)], store_sem))
+            stores[-1].start()
     for store in stores:
         store.wait()
 
@@ -204,12 +218,13 @@
             pltpu.VMEM((ROWS, NZ * XY * COLS), jnp.bfloat16),
             pltpu.VMEM((5, 1, 256), jnp.float32),
             pltpu.VMEM((5, ROWS, 256), jnp.bfloat16),
+            pltpu.VMEM((NZ, XY * COLS, ROWS), jnp.float32),
             pltpu.VMEM((NZ, ROWS, XY * COLS), jnp.bfloat16),
             pltpu.SemaphoreType.DMA((NC + 1,)),
             pltpu.SemaphoreType.DMA,
         ],
-        compiler_params=pltpu.CompilerParams(vmem_limit_bytes=60 * 1024 * 1024),
-    )(block_owner, round_order, eps_occ, vir_row, packed, *pieces)
+        compiler_params=pltpu.CompilerParams(vmem_limit_bytes=32 * 1024 * 1024),
+    )(block_owner, round_order, eps_occ, vir_row, packed, *[pltpu.with_memory_space_constraint(v, pltpu.HBM) for v in pieces])
 
 
 def on_device(three_centre, eps_occ, eps_vir, block_owner, round_order):

time: 86.3 us -> 84.5 us (0.979)
  local copies, waits for them, and re-layouts: 5.72 us -> 4.02 us
    unnamed x44 -> x48, local copies, waits for them, and re-layouts: 3.96 us -> 2.85 us
  transfers between devices with their start and end apart: 23 -> 23, of which waited for: 7 -> 7; matrix products, arithmetic and copies ran while one was open for 4% -> 3% of each run, Pallas kernels for 2% -> 2%
where the time goes in v4:
time: 84.5 us; the launch traced here: 84.3 us
  starting transfers between devices  43.2 us (51%)
  waiting for transfers between devices  21.9 us (26%)
  Pallas kernels  13.4 us (16%)
  local copies, waits for them, and re-layouts  4.02 us (5%)
  other arithmetic  1.21 us (1%)
    ppermute x21, starting transfers between devices, fetch(): return lax.ppermute(block, BOTH, pairs)  34.4 us
    ppermute x21, waiting for transfers between devices, fetch(): return lax.ppermute(block, BOTH, pairs)  20.5 us
    pallas_call x1, Pallas kernels, gamma(): pl.pallas_call(functools.partial(gamma_kernel, layout), in_specs=[smem] *...  9.64 us
    all_to_all x2, starting transfers between devices, exchange(): lax.all_to_all(packed, 'occ', split_axis=0, concat_axis=0, axis_index_gro...  8.82 us
    unnamed x48, local copies, waits for them, and re-layouts  2.85 us
    pallas_call x1, Pallas kernels, pack_line(): pl.pallas_call(line_kernel, in_specs=[pl.BlockSpec(memory_space=pltpu.SME...  2.27 us
  transfers between devices with their start and end apart: 23, of which 7 were waited for; matrix products, arithmetic and copies ran while one was open for 3% of the time, Pallas kernels for 2%

profile of v4, /device:TPU:1, one launch (start us, length us, event | category | flops | bytes accessed | tf_op | source)
XLA Modules:
  0.0 84.3 jit_solution(14140602919966890206)
XLA Ops:
  0.0 2.3 %shard_map.55 = bf16[160,128]{1,0:T(8,128)(2,1)} custom-call(s32[2]{0:T(128)} %order.3, bf16[64,64,160]{2,1,0:T(8,128)(2,1)} %bitcast.13), custom_call_target="tpu_custom_call" | custom-call | tf_op jit(solution)/shard_map/pallas_call | solution.py:59
  2.3 6.5 %collective-permute-start = (bf16[160,128]{1,0:T(8,128)(2,1)}, bf16[160,128]{1,0:T(8,128)(2,1)S(1)}, u32[]{:S(2)}, u32[]{:S(2)}) collective-permute-start(bf16[160,128]{1,0:T(8,128)(2,1)} %shard_map.55), channel_id=1, source_target_pairs={{32,0},{33,1},{36,4},{37,5},{40,8},{41,9},{44,12},{45,13},{48,16},... | collective-permute-start | bytes 122888 | tf_op jit(solution)/shard_map/ppermute | solution.py:36
  8.8 1.5 %shard_map.56 = bf16[8,8,80,128]{3,2,1,0:T(8,128)(2,1)} custom-call(bf16[64,64,160]{2,1,0:T(8,128)(2,1)S(1)} %bitcast.14), custom_call_target="tpu_custom_call" | custom-call | tf_op jit(solution)/shard_map/pallas_call | solution.py:81
  10.3 0.0 collective-permute-done
  10.3 5.3 %all-to-all-start = ((bf16[8,8,80,128]{3,2,1,0:T(8,128)(2,1)}), bf16[8,8,80,128]{3,2,1,0:T(8,128)(2,1)S(1)}, u32[]{:S(2)}, u32[]{:S(2)}) async-start(bf16[8,8,80,128]{3,2,1,0:T(8,128)(2,1)} %shard_map.56), calls=%async_computation | async-start | bytes 2621440 | tf_op jit(solution)/shard_map/all_to_all | solution.py:93
  15.5 0.1 collective-permute-start.3
  15.6 3.9 %collective-permute-start.2 = (bf16[2,160,128]{2,1,0:T(8,128)(2,1)S(1)}, bf16[2,160,128]{2,1,0:T(8,128)(2,1)S(1)}, u32[]{:S(2)}, u32[]{:S(2)}) collective-permute-start(bf16[2,160,128]{2,1,0:T(8,128)(2,1)S(1)} %pad_maximum_fusion.2), channel_id=1, source_target_pairs={{128,0},{129,1},{132,4},{133,5},{136,8},{137,9},{140,12},{141,13},... | collective-permute-start | bytes 245768 | tf_op jit(solution)/shard_map/ppermute | solution.py:36
  19.6 2.4 %collective-permute-start.1 = (bf16[2,160,128]{2,1,0:T(8,128)(2,1)S(1)}, bf16[2,160,128]{2,1,0:T(8,128)(2,1)S(1)}, u32[]{:S(2)}, u32[]{:S(2)}) collective-permute-start(bf16[2,160,128]{2,1,0:T(8,128)(2,1)S(1)} %pad_maximum_fusion.2), channel_id=1, source_target_pairs={{64,0},{65,1},{68,4},{69,5},{72,8},{73,9},{76,12},{77,13},{80,16},... | collective-permute-start | bytes 245768 | tf_op jit(solution)/shard_map/ppermute | solution.py:36
  22.0 5.7 %collective-permute-done.1 = bf16[2,160,128]{2,1,0:T(8,128)(2,1)S(1)} collective-permute-done((bf16[2,160,128]{2,1,0:T(8,128)(2,1)S(1)}, bf16[2,160,128]{2,1,0:T(8,128)(2,1)S(1)}, u32[]{:S(2)}, u32[]{:S(2)}) %collective-permute-start.1) | collective-permute-done | bytes 81952 | tf_op jit(solution)/shard_map/ppermute | solution.py:36
  27.8 2.6 %collective-permute-start.4 = (bf16[8,160,128]{2,1,0:T(8,128)(2,1)S(1)}, bf16[8,160,128]{2,1,0:T(8,128)(2,1)S(1)}, u32[]{:S(2)}, u32[]{:S(2)}) collective-permute-start(bf16[8,160,128]{2,1,0:T(8,128)(2,1)S(1)} %constant_dynamic-update-slice_fusion), channel_id=1, source_target_pairs={{4,0},{17,1},{8,4},{21,5},{12,8},{25,9},{0,12},{29,13},{20,16},{3,... | collective-permute-start | bytes 983048 | tf_op jit(solution)/shard_map/ppermute | solution.py:36
  30.4 0.0 collective-permute-start.8
  30.4 1.4 %collective-permute-start.7 = (bf16[8,160,128]{2,1,0:T(8,128)(2,1)S(1)}, bf16[8,160,128]{2,1,0:T(8,128)(2,1)}, u32[]{:S(2)}, u32[]{:S(2)}) collective-permute-start(bf16[8,160,128]{2,1,0:T(8,128)(2,1)S(1)} %constant_dynamic-update-slice_fusion), channel_id=1, source_target_pairs={{8,0},{3,1},{12,4},{7,5},{0,8},{11,9},{4,12},{15,13},{24,16},{19,1... | collective-permute-start | bytes 983048 | tf_op jit(solution)/shard_map/ppermute | solution.py:36
  31.8 1.5 %all-to-all-done = bf16[8,8,80,128]{3,2,1,0:T(8,128)(2,1)S(1)} async-done(((bf16[8,8,80,128]{3,2,1,0:T(8,128)(2,1)}), bf16[8,8,80,128]{3,2,1,0:T(8,128)(2,1)S(1)}, u32[]{:S(2)}, u32[]{:S(2)}) %all-to-all-start) | async-done | bytes 1310752 | tf_op jit(solution)/shard_map/all_to_all | solution.py:93
  33.2 1.1 %copy.9 = bf16[8,8,80,128]{3,2,0,1:T(8,128)(2,1)} copy(bf16[8,8,80,128]{3,2,1,0:T(8,128)(2,1)S(1)} %all-to-all-done) | data formatting | bytes 2621440 | tf_op jit(solution)/shard_map/all_to_all | solution.py:93
  34.4 3.6 %all-to-all-start.1 = ((bf16[8,8,80,128]{3,2,1,0:T(8,128)(2,1)}), bf16[8,8,80,128]{3,2,1,0:T(8,128)(2,1)S(1)}, u32[]{:S(2)}, u32[]{:S(2)}) async-start(bf16[8,8,80,128]{3,2,1,0:T(8,128)(2,1)} %bitcast.12), calls=%async_computation.1 | async-start | bytes 2621440 | tf_op jit(solution)/shard_map/all_to_all | solution.py:93
  37.9 0.0 collective-permute-done.4
  38.0 0.0 copy-start.21
  38.0 0.0 copy-start.1
  38.0 0.0 copy-start.2
  38.0 0.0 copy-start.3
  38.0 0.1 pad_maximum_fusion.refs_0_
  38.1 0.6 collective-permute-start.15
  38.7 4.5 %collective-permute-start.6 = (bf16[2,8,160,128]{3,2,1,0:T(8,128)(2,1)S(1)}, bf16[2,8,160,128]{3,2,1,0:T(8,128)(2,1)S(1)}, u32[]{:S(2)}, u32[]{:S(2)}) collective-permute-start(bf16[2,8,160,128]{3,2,1,0:T(8,128)(2,1)S(1)} %pad_maximum_fusion.refs_0_), channel_id=1, source_target_pairs={{1,0},{0,1},{5,4},{4,5},{9,8},{8,9},{13,12},{12,13},{17,16},{16,17... | collective-permute-start | bytes 1966088 | tf_op jit(solution)/shard_map/ppermute | solution.py:36
  43.1 0.9 %collective-permute-start.5 = (bf16[2,8,160,128]{3,2,1,0:T(8,128)(2,1)S(1)}, bf16[2,8,160,128]{3,2,1,0:T(8,128)(2,1)S(1)}, u32[]{:S(2)}, u32[]{:S(2)}) collective-permute-start(bf16[2,8,160,128]{3,2,1,0:T(8,128)(2,1)S(1)} %pad_maximum_fusion.refs_0_), channel_id=1, source_target_pairs={{16,0},{5,1},{20,4},{9,5},{24,8},{13,9},{28,12},{1,13},{2,16},{21,... | collective-permute-start | bytes 1966088 | tf_op jit(solution)/shard_map/ppermute | solution.py:36
  44.0 0.0 collective-permute-done.7
  44.0 0.7 copy-done.20
  44.7 1.1 %pad_maximum_fusion.1.refs_2_ = bf16[2,8,160,128]{3,2,1,0:T(8,128)(2,1)S(1)} fusion(bf16[1,8,160,128]{3,2,1,0:T(8,128)(2,1)} %bitcast.17, bf16[1,8,160,128]{3,2,1,0:T(8,128)(2,1)} %bitcast.6), kind=kLoop, calls=%fused_computation.2 | loop fusion | flops 327680 | bytes 1310720 | tf_op jit(solution)/shard_map/stack | solution.py:251
  45.9 0.7 collective-permute-start.11
  46.6 2.1 %collective-permute-start.13 = (bf16[2,8,160,128]{3,2,1,0:T(8,128)(2,1)S(1)}, bf16[2,8,160,128]{3,2,1,0:T(8,128)(2,1)S(1)}, u32[]{:S(2)}, u32[]{:S(2)}) collective-permute-start(bf16[2,8,160,128]{3,2,1,0:T(8,128)(2,1)S(1)} %pad_maximum_fusion.1.refs_2_), channel_id=1, source_target_pairs={{16,0},{5,1},{20,4},{9,5},{24,8},{13,9},{28,12},{1,13},{2,16},{21,... | collective-permute-start | bytes 1966088 | tf_op jit(solution)/shard_map/ppermute | solution.py:36
  48.7 4.1 %collective-permute-done.5.refs_4_ = bf16[2,8,160,128]{3,2,1,0:T(8,128)(2,1)S(1)} collective-permute-done((bf16[2,8,160,128]{3,2,1,0:T(8,128)(2,1)S(1)}, bf16[2,8,160,128]{3,2,1,0:T(8,128)(2,1)S(1)}, u32[]{:S(2)}, u32[]{:S(2)}) %collective-permute-start.5) | collective-permute-done | bytes 655392 | tf_op jit(solution)/shard_map/ppermute | solution.py:36
  52.9 0.8 collective-permute-start.9
  53.7 0.0 collective-permute-done.15.refs_10_
  53.7 0.1 collective-permute-start.16
  53.8 1.7 %collective-permute-start.17 = (bf16[2,8,160,128]{3,2,1,0:T(8,128)(2,1)S(1)}, bf16[2,8,160,128]{3,2,1,0:T(8,128)(2,1)S(1)}, u32[]{:S(2)}, u32[]{:S(2)}) collective-permute-start(bf16[2,8,160,128]{3,2,1,0:T(8,128)(2,1)S(1)} %collective-permute-done.5.refs_4_), channel_id=1, source_target_pairs={{16,0},{5,1},{20,4},{9,5},{24,8},{13,9},{28,12},{1,13},{2,16},{21,... | collective-permute-start | bytes 1966088 | tf_op jit(solution)/shard_map/ppermute | solution.py:36
  55.5 1.9 %collective-permute-done.11.refs_6_ = bf16[2,8,160,128]{3,2,1,0:T(8,128)(2,1)S(1)} collective-permute-done((bf16[2,8,160,128]{3,2,1,0:T(8,128)(2,1)S(1)}, bf16[2,8,160,128]{3,2,1,0:T(8,128)(2,1)S(1)}, u32[]{:S(2)}, u32[]{:S(2)}) %collective-permute-start.11) | collective-permute-done | bytes 655392 | tf_op jit(solution)/shard_map/ppermute | solution.py:36
  57.3 2.6 %collective-permute-done.13.refs_8_ = bf16[2,8,160,128]{3,2,1,0:T(8,128)(2,1)S(1)} collective-permute-done((bf16[2,8,160,128]{3,2,1,0:T(8,128)(2,1)S(1)}, bf16[2,8,160,128]{3,2,1,0:T(8,128)(2,1)S(1)}, u32[]{:S(2)}, u32[]{:S(2)}) %collective-permute-start.13) | collective-permute-done | bytes 655392 | tf_op jit(solution)/shard_map/ppermute | solution.py:36
  59.9 0.9 %collective-permute-start.10 = (bf16[2,8,160,128]{3,2,1,0:T(8,128)(2,1)S(1)}, bf16[2,8,160,128]{3,2,1,0:T(8,128)(2,1)S(1)}, u32[]{:S(2)}, u32[]{:S(2)}) collective-permute-start(bf16[2,8,160,128]{3,2,1,0:T(8,128)(2,1)S(1)} %collective-permute-done.5.refs_4_), channel_id=1, source_target_pairs={{1,0},{0,1},{5,4},{4,5},{9,8},{8,9},{13,12},{12,13},{17,16},{16,17... | collective-permute-start | bytes 1966088 | tf_op jit(solution)/shard_map/ppermute | solution.py:36
  60.8 0.1 collective-permute-start.12
  60.9 0.4 collective-permute-start.14
  61.3 5.6 %collective-permute-done.17.refs_12_ = bf16[2,8,160,128]{3,2,1,0:T(8,128)(2,1)S(1)} collective-permute-done((bf16[2,8,160,128]{3,2,1,0:T(8,128)(2,1)S(1)}, bf16[2,8,160,128]{3,2,1,0:T(8,128)(2,1)S(1)}, u32[]{:S(2)}, u32[]{:S(2)}) %collective-permute-start.17) | collective-permute-done | bytes 655392 | tf_op jit(solution)/shard_map/ppermute | solution.py:36
  66.9 0.8 collective-permute-start.18
  67.7 0.5 collective-permute-done.19.refs_14_
  68.3 4.0 %collective-permute-start.20 = (bf16[2,8,160,128]{3,2,1,0:T(8,128)(2,1)S(1)}, bf16[2,8,160,128]{3,2,1,0:T(8,128)(2,1)}, u32[]{:S(2)}, u32[]{:S(2)}) collective-permute-start(bf16[2,8,160,128]{3,2,1,0:T(8,128)(2,1)S(1)} %collective-permute-done.19.refs_14_), channel_id=1, source_target_pairs={{1,0},{0,1},{5,4},{4,5},{9,8},{8,9},{13,12},{12,13},{17,16},{16,17... | collective-permute-start | bytes 1966088 | tf_op jit(solution)/shard_map/ppermute | solution.py:36
  72.4 0.7 copy-done.15
  73.1 0.2 copy-done.17
  73.3 0.2 copy-done.16
  73.6 0.8 copy-done.18
  74.5 9.6 %shard_map.57 = bf16[160,4096]{1,0:T(8,128)(2,1)} custom-call(s32[64]{0:T(128)S(1)} %copy-done.2, s32[2]{0:T(128)S(1)} %copy-done.1, f32[16]{0:T(128)S(1)} %copy-done.3, f32[1,2560]{1,0:T(1,128)S(1)} %broadcast_in_dim.6.eps_vir, bf16[8,8,80,128]{3,2,1,0:T(8,128)(2,1)S(1)} %all-to-all-done.1.packed, bf16[2,8,160,128]{3,2,1,0:T(8,128)(2,1)} %copy-done.4, ...), custom_call_target="tpu_custom_call" | custom-call | tf_op jit(solution)/shard_map/pallas_call | solution.py:209
  (55 shorter events, 0.2 us)
Async XLA Ops:
  0.0 8.8 %copy-start = (bf16[64,160,64]{1,2,0:T(8,128)(2,1)S(1)}, bf16[64,160,64]{1,2,0:T(8,128)(2,1)}, u32[]{:S(2)}) copy-start(bf16[64,160,64]{1,2,0:T(8,128)(2,1)} %param.5) | copy-start | bytes 3932164
  2.3 8.0 %collective-permute-start = (bf16[160,128]{1,0:T(8,128)(2,1)}, bf16[160,128]{1,0:T(8,128)(2,1)S(1)}, u32[]{:S(2)}, u32[]{:S(2)}) collective-permute-start(bf16[160,128]{1,0:T(8,128)(2,1)} %shard_map.55), channel_id=1, source_target_pairs={{32,0},{33,1},{36,4},{37,5},{40,8},{41,9},{44,12},{45,13},{48,16},... | collective-permute-start | bytes 122888 | tf_op jit(solution)/shard_map/ppermute | solution.py:36
  10.3 5.3 %copy-start.19 = (bf16[160,128]{1,0:T(8,128)(2,1)S(1)}, bf16[160,128]{1,0:T(8,128)(2,1)}, u32[]{:S(2)}) copy-start(bf16[160,128]{1,0:T(8,128)(2,1)} %shard_map.55) | copy-start | bytes 122884
  10.3 23.0 %all-to-all-start = ((bf16[8,8,80,128]{3,2,1,0:T(8,128)(2,1)}), bf16[8,8,80,128]{3,2,1,0:T(8,128)(2,1)S(1)}, u32[]{:S(2)}, u32[]{:S(2)}) async-start(bf16[8,8,80,128]{3,2,1,0:T(8,128)(2,1)} %shard_map.56), calls=%async_computation | async-start | bytes 2621440 | tf_op jit(solution)/shard_map/all_to_all | solution.py:93
  15.5 12.2 %collective-permute-start.3 = (bf16[2,160,128]{2,1,0:T(8,128)(2,1)S(1)}, bf16[2,160,128]{2,1,0:T(8,128)(2,1)S(1)}, u32[]{:S(2)}, u32[]{:S(2)}) collective-permute-start(bf16[2,160,128]{2,1,0:T(8,128)(2,1)S(1)} %pad_maximum_fusion.2), channel_id=1, source_target_pairs={{192,0},{193,1},{196,4},{197,5},{200,8},{201,9},{204,12},{205,13},... | collective-permute-start | bytes 245768 | tf_op jit(solution)/shard_map/ppermute | solution.py:36
  15.6 12.1 %collective-permute-start.2 = (bf16[2,160,128]{2,1,0:T(8,128)(2,1)S(1)}, bf16[2,160,128]{2,1,0:T(8,128)(2,1)S(1)}, u32[]{:S(2)}, u32[]{:S(2)}) collective-permute-start(bf16[2,160,128]{2,1,0:T(8,128)(2,1)S(1)} %pad_maximum_fusion.2), channel_id=1, source_target_pairs={{128,0},{129,1},{132,4},{133,5},{136,8},{137,9},{140,12},{141,13},... | collective-permute-start | bytes 245768 | tf_op jit(solution)/shard_map/ppermute | solution.py:36
  19.6 8.1 %collective-permute-start.1 = (bf16[2,160,128]{2,1,0:T(8,128)(2,1)S(1)}, bf16[2,160,128]{2,1,0:T(8,128)(2,1)S(1)}, u32[]{:S(2)}, u32[]{:S(2)}) collective-permute-start(bf16[2,160,128]{2,1,0:T(8,128)(2,1)S(1)} %pad_maximum_fusion.2), channel_id=1, source_target_pairs={{64,0},{65,1},{68,4},{69,5},{72,8},{73,9},{76,12},{77,13},{80,16},... | collective-permute-start | bytes 245768 | tf_op jit(solution)/shard_map/ppermute | solution.py:36
  27.8 10.2 %collective-permute-start.4 = (bf16[8,160,128]{2,1,0:T(8,128)(2,1)S(1)}, bf16[8,160,128]{2,1,0:T(8,128)(2,1)S(1)}, u32[]{:S(2)}, u32[]{:S(2)}) collective-permute-start(bf16[8,160,128]{2,1,0:T(8,128)(2,1)S(1)} %constant_dynamic-update-slice_fusion), channel_id=1, source_target_pairs={{4,0},{17,1},{8,4},{21,5},{12,8},{25,9},{0,12},{29,13},{20,16},{3,... | collective-permute-start | bytes 983048 | tf_op jit(solution)/shard_map/ppermute | solution.py:36
  30.4 13.6 %collective-permute-start.8 = (bf16[8,160,128]{2,1,0:T(8,128)(2,1)S(1)}, bf16[8,160,128]{2,1,0:T(8,128)(2,1)S(1)}, u32[]{:S(2)}, u32[]{:S(2)}) collective-permute-start(bf16[8,160,128]{2,1,0:T(8,128)(2,1)S(1)} %constant_dynamic-update-slice_fusion), channel_id=1, source_target_pairs={{12,0},{19,1},{0,4},{23,5},{4,8},{27,9},{8,12},{31,13},{28,16},{1,... | collective-permute-start | bytes 983048 | tf_op jit(solution)/shard_map/ppermute | solution.py:36
  30.4 13.6 %collective-permute-start.7 = (bf16[8,160,128]{2,1,0:T(8,128)(2,1)S(1)}, bf16[8,160,128]{2,1,0:T(8,128)(2,1)}, u32[]{:S(2)}, u32[]{:S(2)}) collective-permute-start(bf16[8,160,128]{2,1,0:T(8,128)(2,1)S(1)} %constant_dynamic-update-slice_fusion), channel_id=1, source_target_pairs={{8,0},{3,1},{12,4},{7,5},{0,8},{11,9},{4,12},{15,13},{24,16},{19,1... | collective-permute-start | bytes 983048 | tf_op jit(solution)/shard_map/ppermute | solution.py:36
  34.4 40.0 %all-to-all-start.1 = ((bf16[8,8,80,128]{3,2,1,0:T(8,128)(2,1)}), bf16[8,8,80,128]{3,2,1,0:T(8,128)(2,1)S(1)}, u32[]{:S(2)}, u32[]{:S(2)}) async-start(bf16[8,8,80,128]{3,2,1,0:T(8,128)(2,1)} %bitcast.12), calls=%async_computation.1 | async-start | bytes 2621440 | tf_op jit(solution)/shard_map/all_to_all | solution.py:93
  38.0 8.6 %copy-start.21 = (f32[2560]{0:T(1024)S(1)}, f32[2560]{0:T(1024)}, u32[]{:S(2)}) copy-start(f32[2560]{0:T(1024)} %param.7) | copy-start | bytes 30724
  38.0 36.5 %copy-start.1 = (s32[2]{0:T(128)S(1)}, s32[2]{0:T(128)}, u32[]{:S(2)}) copy-start(s32[2]{0:T(128)} %order.3) | copy-start | bytes 28
  38.0 36.5 %copy-start.2 = (s32[64]{0:T(128)S(1)}, s32[64]{0:T(128)}, u32[]{:S(2)}) copy-start(s32[64]{0:T(128)} %owner.1) | copy-start | bytes 772
  38.0 36.5 %copy-start.3 = (f32[16]{0:T(128)S(1)}, f32[16]{0:T(128)}, u32[]{:S(2)}) copy-start(f32[16]{0:T(128)} %eps_occ.1) | copy-start | bytes 196
  38.1 36.3 %copy-start.4 = (bf16[2,8,160,128]{3,2,1,0:T(8,128)(2,1)}, bf16[2,8,160,128]{3,2,1,0:T(8,128)(2,1)S(1)}, u32[]{:S(2)}) copy-start(bf16[2,8,160,128]{3,2,1,0:T(8,128)(2,1)S(1)} %pad_maximum_fusion.refs_0_) | copy-start | bytes 1966084
  38.1 15.6 %collective-permute-start.15 = (bf16[2,8,160,128]{3,2,1,0:T(8,128)(2,1)S(1)}, bf16[2,8,160,128]{3,2,1,0:T(8,128)(2,1)S(1)}, u32[]{:S(2)}, u32[]{:S(2)}) collective-permute-start(bf16[2,8,160,128]{3,2,1,0:T(8,128)(2,1)S(1)} %pad_maximum_fusion.refs_0_), channel_id=1, source_target_pairs={{18,0},{13,1},{22,4},{1,5},{26,8},{5,9},{30,12},{9,13},{0,16},{29,... | collective-permute-start | bytes 1966088 | tf_op jit(solution)/shard_map/ppermute | solution.py:36
  38.7 15.2 %collective-permute-start.6 = (bf16[2,8,160,128]{3,2,1,0:T(8,128)(2,1)S(1)}, bf16[2,8,160,128]{3,2,1,0:T(8,128)(2,1)S(1)}, u32[]{:S(2)}, u32[]{:S(2)}) collective-permute-start(bf16[2,8,160,128]{3,2,1,0:T(8,128)(2,1)S(1)} %pad_maximum_fusion.refs_0_), channel_id=1, source_target_pairs={{1,0},{0,1},{5,4},{4,5},{9,8},{8,9},{13,12},{12,13},{17,16},{16,17... | collective-permute-start | bytes 1966088 | tf_op jit(solution)/shard_map/ppermute | solution.py:36
  43.1 9.8 %collective-permute-start.5 = (bf16[2,8,160,128]{3,2,1,0:T(8,128)(2,1)S(1)}, bf16[2,8,160,128]{3,2,1,0:T(8,128)(2,1)S(1)}, u32[]{:S(2)}, u32[]{:S(2)}) collective-permute-start(bf16[2,8,160,128]{3,2,1,0:T(8,128)(2,1)S(1)} %pad_maximum_fusion.refs_0_), channel_id=1, source_target_pairs={{16,0},{5,1},{20,4},{9,5},{24,8},{13,9},{28,12},{1,13},{2,16},{21,... | collective-permute-start | bytes 1966088 | tf_op jit(solution)/shard_map/ppermute | solution.py:36
  44.0 0.7 copy-start.20
  45.9 28.5 %copy-start.5 = (bf16[2,8,160,128]{3,2,1,0:T(8,128)(2,1)}, bf16[2,8,160,128]{3,2,1,0:T(8,128)(2,1)S(1)}, u32[]{:S(2)}) copy-start(bf16[2,8,160,128]{3,2,1,0:T(8,128)(2,1)S(1)} %pad_maximum_fusion.1.refs_2_) | copy-start | bytes 1966084
  45.9 11.4 %collective-permute-start.11 = (bf16[2,8,160,128]{3,2,1,0:T(8,128)(2,1)S(1)}, bf16[2,8,160,128]{3,2,1,0:T(8,128)(2,1)S(1)}, u32[]{:S(2)}, u32[]{:S(2)}) collective-permute-start(bf16[2,8,160,128]{3,2,1,0:T(8,128)(2,1)S(1)} %pad_maximum_fusion.1.refs_2_), channel_id=1, source_target_pairs={{18,0},{13,1},{22,4},{1,5},{26,8},{5,9},{30,12},{9,13},{0,16},{29,... | collective-permute-start | bytes 1966088 | tf_op jit(solution)/shard_map/ppermute | solution.py:36
  46.6 13.3 %collective-permute-start.13 = (bf16[2,8,160,128]{3,2,1,0:T(8,128)(2,1)S(1)}, bf16[2,8,160,128]{3,2,1,0:T(8,128)(2,1)S(1)}, u32[]{:S(2)}, u32[]{:S(2)}) collective-permute-start(bf16[2,8,160,128]{3,2,1,0:T(8,128)(2,1)S(1)} %pad_maximum_fusion.1.refs_2_), channel_id=1, source_target_pairs={{16,0},{5,1},{20,4},{9,5},{24,8},{13,9},{28,12},{1,13},{2,16},{21,... | collective-permute-start | bytes 1966088 | tf_op jit(solution)/shard_map/ppermute | solution.py:36
  52.9 19.4 %copy-start.8 = (bf16[2,8,160,128]{3,2,1,0:T(8,128)(2,1)}, bf16[2,8,160,128]{3,2,1,0:T(8,128)(2,1)S(1)}, u32[]{:S(2)}) copy-start(bf16[2,8,160,128]{3,2,1,0:T(8,128)(2,1)S(1)} %collective-permute-done.5.refs_4_) | copy-start | bytes 1966084
  52.9 7.9 %collective-permute-start.9 = (bf16[2,8,160,128]{3,2,1,0:T(8,128)(2,1)S(1)}, bf16[2,8,160,128]{3,2,1,0:T(8,128)(2,1)S(1)}, u32[]{:S(2)}, u32[]{:S(2)}) collective-permute-start(bf16[2,8,160,128]{3,2,1,0:T(8,128)(2,1)S(1)} %pad_maximum_fusion.1.refs_2_), channel_id=1, source_target_pairs={{1,0},{0,1},{5,4},{4,5},{9,8},{8,9},{13,12},{12,13},{17,16},{16,17... | collective-permute-start | bytes 1966088 | tf_op jit(solution)/shard_map/ppermute | solution.py:36
  53.7 20.7 %copy-start.6 = (bf16[2,8,160,128]{3,2,1,0:T(8,128)(2,1)}, bf16[2,8,160,128]{3,2,1,0:T(8,128)(2,1)S(1)}, u32[]{:S(2)}) copy-start(bf16[2,8,160,128]{3,2,1,0:T(8,128)(2,1)S(1)} %collective-permute-done.15.refs_10_) | copy-start | bytes 1966084
  53.7 7.2 %collective-permute-start.16 = (bf16[2,8,160,128]{3,2,1,0:T(8,128)(2,1)S(1)}, bf16[2,8,160,128]{3,2,1,0:T(8,128)(2,1)S(1)}, u32[]{:S(2)}, u32[]{:S(2)}) collective-permute-start(bf16[2,8,160,128]{3,2,1,0:T(8,128)(2,1)S(1)} %collective-permute-done.15.refs_10_), channel_id=1, source_target_pairs={{1,0},{0,1},{5,4},{4,5},{9,8},{8,9},{13,12},{12,13},{17,16},{16,17... | collective-permute-start | bytes 1966088 | tf_op jit(solution)/shard_map/ppermute | solution.py:36
  53.8 18.5 %copy-start.7 = (bf16[2,8,160,128]{3,2,1,0:T(8,128)(2,1)}, bf16[2,8,160,128]{3,2,1,0:T(8,128)(2,1)S(1)}, u32[]{:S(2)}) copy-start(bf16[2,8,160,128]{3,2,1,0:T(8,128)(2,1)S(1)} %collective-permute-done.6.refs_1_) | copy-start | bytes 1966084
  53.8 13.1 %collective-permute-start.17 = (bf16[2,8,160,128]{3,2,1,0:T(8,128)(2,1)S(1)}, bf16[2,8,160,128]{3,2,1,0:T(8,128)(2,1)S(1)}, u32[]{:S(2)}, u32[]{:S(2)}) collective-permute-start(bf16[2,8,160,128]{3,2,1,0:T(8,128)(2,1)S(1)} %collective-permute-done.5.refs_4_), channel_id=1, source_target_pairs={{16,0},{5,1},{20,4},{9,5},{24,8},{13,9},{28,12},{1,13},{2,16},{21,... | collective-permute-start | bytes 1966088 | tf_op jit(solution)/shard_map/ppermute | solution.py:36
  57.3 15.0 %copy-start.9 = (bf16[2,8,160,128]{3,2,1,0:T(8,128)(2,1)}, bf16[2,8,160,128]{3,2,1,0:T(8,128)(2,1)S(1)}, u32[]{:S(2)}) copy-start(bf16[2,8,160,128]{3,2,1,0:T(8,128)(2,1)S(1)} %collective-permute-done.11.refs_6_) | copy-start | bytes 1966084
  57.3 10.9 %collective-permute-start.19 = (bf16[2,8,160,128]{3,2,1,0:T(8,128)(2,1)S(1)}, bf16[2,8,160,128]{3,2,1,0:T(8,128)(2,1)S(1)}, u32[]{:S(2)}, u32[]{:S(2)}) collective-permute-start(bf16[2,8,160,128]{3,2,1,0:T(8,128)(2,1)S(1)} %collective-permute-done.11.refs_6_), channel_id=1, source_target_pairs={{18,0},{13,1},{22,4},{1,5},{26,8},{5,9},{30,12},{9,13},{0,16},{29,... | collective-permute-start | bytes 1966088 | tf_op jit(solution)/shard_map/ppermute | solution.py:36
  59.9 12.5 %copy-start.10 = (bf16[2,8,160,128]{3,2,1,0:T(8,128)(2,1)}, bf16[2,8,160,128]{3,2,1,0:T(8,128)(2,1)S(1)}, u32[]{:S(2)}) copy-start(bf16[2,8,160,128]{3,2,1,0:T(8,128)(2,1)S(1)} %collective-permute-done.13.refs_8_) | copy-start | bytes 1966084
  59.9 12.4 %collective-permute-start.10 = (bf16[2,8,160,128]{3,2,1,0:T(8,128)(2,1)S(1)}, bf16[2,8,160,128]{3,2,1,0:T(8,128)(2,1)S(1)}, u32[]{:S(2)}, u32[]{:S(2)}) collective-permute-start(bf16[2,8,160,128]{3,2,1,0:T(8,128)(2,1)S(1)} %collective-permute-done.5.refs_4_), channel_id=1, source_target_pairs={{1,0},{0,1},{5,4},{4,5},{9,8},{8,9},{13,12},{12,13},{17,16},{16,17... | collective-permute-start | bytes 1966088 | tf_op jit(solution)/shard_map/ppermute | solution.py:36
  60.8 11.6 %copy-start.11 = (bf16[2,8,160,128]{3,2,1,0:T(8,128)(2,1)}, bf16[2,8,160,128]{3,2,1,0:T(8,128)(2,1)S(1)}, u32[]{:S(2)}) copy-start(bf16[2,8,160,128]{3,2,1,0:T(8,128)(2,1)S(1)} %collective-permute-done.9.refs_3_) | copy-start | bytes 1966084
  60.8 11.5 %collective-permute-start.12 = (bf16[2,8,160,128]{3,2,1,0:T(8,128)(2,1)S(1)}, bf16[2,8,160,128]{3,2,1,0:T(8,128)(2,1)S(1)}, u32[]{:S(2)}, u32[]{:S(2)}) collective-permute-start(bf16[2,8,160,128]{3,2,1,0:T(8,128)(2,1)S(1)} %collective-permute-done.11.refs_6_), channel_id=1, source_target_pairs={{1,0},{0,1},{5,4},{4,5},{9,8},{8,9},{13,12},{12,13},{17,16},{16,17... | collective-permute-start | bytes 1966088 | tf_op jit(solution)/shard_map/ppermute | solution.py:36
  60.9 11.5 %copy-start.12 = (bf16[2,8,160,128]{3,2,1,0:T(8,128)(2,1)}, bf16[2,8,160,128]{3,2,1,0:T(8,128)(2,1)S(1)}, u32[]{:S(2)}) copy-start(bf16[2,8,160,128]{3,2,1,0:T(8,128)(2,1)S(1)} %collective-permute-done.16.refs_11_) | copy-start | bytes 1966084
  60.9 11.4 %collective-permute-start.14 = (bf16[2,8,160,128]{3,2,1,0:T(8,128)(2,1)S(1)}, bf16[2,8,160,128]{3,2,1,0:T(8,128)(2,1)S(1)}, u32[]{:S(2)}, u32[]{:S(2)}) collective-permute-start(bf16[2,8,160,128]{3,2,1,0:T(8,128)(2,1)S(1)} %collective-permute-done.13.refs_8_), channel_id=1, source_target_pairs={{1,0},{0,1},{5,4},{4,5},{9,8},{8,9},{13,12},{12,13},{17,16},{16,17... | collective-permute-start | bytes 1966088 | tf_op jit(solution)/shard_map/ppermute | solution.py:36
  66.9 5.5 %copy-start.13 = (bf16[2,8,160,128]{3,2,1,0:T(8,128)(2,1)}, bf16[2,8,160,128]{3,2,1,0:T(8,128)(2,1)S(1)}, u32[]{:S(2)}) copy-start(bf16[2,8,160,128]{3,2,1,0:T(8,128)(2,1)S(1)} %collective-permute-done.17.refs_12_) | copy-start | bytes 1966084
  66.9 5.4 %collective-permute-start.18 = (bf16[2,8,160,128]{3,2,1,0:T(8,128)(2,1)S(1)}, bf16[2,8,160,128]{3,2,1,0:T(8,128)(2,1)S(1)}, u32[]{:S(2)}, u32[]{:S(2)}) collective-permute-start(bf16[2,8,160,128]{3,2,1,0:T(8,128)(2,1)S(1)} %collective-permute-done.17.refs_12_), channel_id=1, source_target_pairs={{1,0},{0,1},{5,4},{4,5},{9,8},{8,9},{13,12},{12,13},{17,16},{16,17... | collective-permute-start | bytes 1966088 | tf_op jit(solution)/shard_map/ppermute | solution.py:36
  68.3 4.1 %copy-start.14 = (bf16[2,8,160,128]{3,2,1,0:T(8,128)(2,1)}, bf16[2,8,160,128]{3,2,1,0:T(8,128)(2,1)S(1)}, u32[]{:S(2)}) copy-start(bf16[2,8,160,128]{3,2,1,0:T(8,128)(2,1)S(1)} %collective-permute-done.19.refs_14_) | copy-start | bytes 1966084
  68.3 6.1 %collective-permute-start.20 = (bf16[2,8,160,128]{3,2,1,0:T(8,128)(2,1)S(1)}, bf16[2,8,160,128]{3,2,1,0:T(8,128)(2,1)}, u32[]{:S(2)}, u32[]{:S(2)}) collective-permute-start(bf16[2,8,160,128]{3,2,1,0:T(8,128)(2,1)S(1)} %collective-permute-done.19.refs_14_), channel_id=1, source_target_pairs={{1,0},{0,1},{5,4},{4,5},{9,8},{8,9},{13,12},{12,13},{17,16},{16,17... | collective-permute-start | bytes 1966088 | tf_op jit(solution)/shard_map/ppermute | solution.py:36
  72.3 0.8 %copy-start.15 = (bf16[2,8,160,128]{3,2,1,0:T(8,128)(2,1)}, bf16[2,8,160,128]{3,2,1,0:T(8,128)(2,1)S(1)}, u32[]{:S(2)}) copy-start(bf16[2,8,160,128]{3,2,1,0:T(8,128)(2,1)S(1)} %collective-permute-done.10.refs_5_) | copy-start | bytes 1966084
  72.3 1.1 %copy-start.17 = (bf16[2,8,160,128]{3,2,1,0:T(8,128)(2,1)}, bf16[2,8,160,128]{3,2,1,0:T(8,128)(2,1)S(1)}, u32[]{:S(2)}) copy-start(bf16[2,8,160,128]{3,2,1,0:T(8,128)(2,1)S(1)} %collective-permute-done.14.refs_9_) | copy-start | bytes 1966084
  72.3 1.3 %copy-start.16 = (bf16[2,8,160,128]{3,2,1,0:T(8,128)(2,1)}, bf16[2,8,160,128]{3,2,1,0:T(8,128)(2,1)S(1)}, u32[]{:S(2)}) copy-start(bf16[2,8,160,128]{3,2,1,0:T(8,128)(2,1)S(1)} %collective-permute-done.12.refs_7_) | copy-start | bytes 1966084
  73.6 0.8 copy-start.18

commit v5 on v4

--- a/solution.py
+++ b/solution.py
@@ -62,7 +62,8 @@
         out_specs=pl.BlockSpec(memory_space=pltpu.VMEM),
         out_shape=jax.ShapeDtypeStruct((LINE, 128), jnp.bfloat16),
         scratch_shapes=[pltpu.VMEM((ROUNDS, COLS, ROWS), jnp.bfloat16), pltpu.SemaphoreType.DMA((ROUNDS,))],
-    )(round_order, columns)
+        compiler_params=pltpu.CompilerParams(vmem_limit_bytes=4 * 1024 * 1024),
+    )(*[pltpu.with_memory_space_constraint(v, pltpu.HBM) for v in (round_order, columns)])
 
 
 def pack_kernel(pieces, out):

time: 84.5 us -> 83.7 us (level)
    unnamed x48 -> x46, local copies, waits for them, and re-layouts: 2.85 us -> 2.85 us
where the time goes in v5:
time: 83.7 us; the launch traced here: 83.5 us
  starting transfers between devices  42.9 us (51%)
  waiting for transfers between devices  22 us (26%)
  Pallas kernels  12.8 us (15%)
  local copies, waits for them, and re-layouts  4.02 us (5%)
  other arithmetic  1.2 us (1%)
    ppermute x21, starting transfers between devices, fetch(): return lax.ppermute(block, BOTH, pairs)  34.2 us
    ppermute x21, waiting for transfers between devices, fetch(): return lax.ppermute(block, BOTH, pairs)  20.5 us
    pallas_call x1, Pallas kernels, gamma(): pl.pallas_call(functools.partial(gamma_kernel, layout), in_specs=[smem] *...  9.64 us
    all_to_all x2, starting transfers between devices, exchange(): lax.all_to_all(packed, 'occ', split_axis=0, concat_axis=0, axis_index_gro...  8.69 us
    unnamed x46, local copies, waits for them, and re-layouts  2.85 us
  transfers between devices with their start and end apart: 23, of which 7 were waited for; matrix products, arithmetic and copies ran while one was open for 3% of the time, Pallas kernels for 2%

profile of v5, /device:TPU:1, one launch (start us, length us, event | category | flops | bytes accessed | tf_op | source)
XLA Modules:
  0.0 83.5 jit_solution(7402461094099213284)
XLA Ops:
  0.0 1.7 %shard_map.55 = bf16[160,128]{1,0:T(8,128)(2,1)S(1)} custom-call(s32[2]{0:T(128)} %order.3, bf16[64,64,160]{2,1,0:T(8,128)(2,1)} %bitcast.13), custom_call_target="tpu_custom_call" | custom-call | tf_op jit(solution)/shard_map/pallas_call | solution.py:59
  1.7 6.5 %collective-permute-start = (bf16[160,128]{1,0:T(8,128)(2,1)S(1)}, bf16[160,128]{1,0:T(8,128)(2,1)S(1)}, u32[]{:S(2)}, u32[]{:S(2)}) collective-permute-start(bf16[160,128]{1,0:T(8,128)(2,1)S(1)} %shard_map.55), channel_id=1, source_target_pairs={{32,0},{33,1},{36,4},{37,5},{40,8},{41,9},{44,12},{45,13},{48,16},... | collective-permute-start | bytes 122888 | tf_op jit(solution)/shard_map/ppermute | solution.py:36
  8.2 1.5 %shard_map.56 = bf16[8,8,80,128]{3,2,1,0:T(8,128)(2,1)} custom-call(bf16[64,64,160]{2,1,0:T(8,128)(2,1)S(1)} %bitcast.14), custom_call_target="tpu_custom_call" | custom-call | tf_op jit(solution)/shard_map/pallas_call | solution.py:82
  9.7 5.1 %all-to-all-start = ((bf16[8,8,80,128]{3,2,1,0:T(8,128)(2,1)}), bf16[8,8,80,128]{3,2,1,0:T(8,128)(2,1)S(1)}, u32[]{:S(2)}, u32[]{:S(2)}) async-start(bf16[8,8,80,128]{3,2,1,0:T(8,128)(2,1)} %shard_map.56), calls=%async_computation | async-start | bytes 2621440 | tf_op jit(solution)/shard_map/all_to_all | solution.py:94
  14.8 0.1 collective-permute-start.3
  14.9 3.9 %collective-permute-start.2 = (bf16[2,160,128]{2,1,0:T(8,128)(2,1)S(1)}, bf16[2,160,128]{2,1,0:T(8,128)(2,1)S(1)}, u32[]{:S(2)}, u32[]{:S(2)}) collective-permute-start(bf16[2,160,128]{2,1,0:T(8,128)(2,1)S(1)} %pad_maximum_fusion.2), channel_id=1, source_target_pairs={{128,0},{129,1},{132,4},{133,5},{136,8},{137,9},{140,12},{141,13},... | collective-permute-start | bytes 245768 | tf_op jit(solution)/shard_map/ppermute | solution.py:36
  18.7 2.4 %collective-permute-start.1 = (bf16[2,160,128]{2,1,0:T(8,128)(2,1)S(1)}, bf16[2,160,128]{2,1,0:T(8,128)(2,1)S(1)}, u32[]{:S(2)}, u32[]{:S(2)}) collective-permute-start(bf16[2,160,128]{2,1,0:T(8,128)(2,1)S(1)} %pad_maximum_fusion.2), channel_id=1, source_target_pairs={{64,0},{65,1},{68,4},{69,5},{72,8},{73,9},{76,12},{77,13},{80,16},... | collective-permute-start | bytes 245768 | tf_op jit(solution)/shard_map/ppermute | solution.py:36
  21.1 5.7 %collective-permute-done.1 = bf16[2,160,128]{2,1,0:T(8,128)(2,1)S(1)} collective-permute-done((bf16[2,160,128]{2,1,0:T(8,128)(2,1)S(1)}, bf16[2,160,128]{2,1,0:T(8,128)(2,1)S(1)}, u32[]{:S(2)}, u32[]{:S(2)}) %collective-permute-start.1) | collective-permute-done | bytes 81952 | tf_op jit(solution)/shard_map/ppermute | solution.py:36
  26.9 0.0 collective-permute-done.2
  26.9 0.0 collective-permute-done.3
  26.9 2.6 %collective-permute-start.4 = (bf16[8,160,128]{2,1,0:T(8,128)(2,1)S(1)}, bf16[8,160,128]{2,1,0:T(8,128)(2,1)S(1)}, u32[]{:S(2)}, u32[]{:S(2)}) collective-permute-start(bf16[8,160,128]{2,1,0:T(8,128)(2,1)S(1)} %constant_dynamic-update-slice_fusion), channel_id=1, source_target_pairs={{4,0},{17,1},{8,4},{21,5},{12,8},{25,9},{0,12},{29,13},{20,16},{3,... | collective-permute-start | bytes 983048 | tf_op jit(solution)/shard_map/ppermute | solution.py:36
  29.6 0.0 collective-permute-start.8
  29.6 1.3 %collective-permute-start.7 = (bf16[8,160,128]{2,1,0:T(8,128)(2,1)S(1)}, bf16[8,160,128]{2,1,0:T(8,128)(2,1)}, u32[]{:S(2)}, u32[]{:S(2)}) collective-permute-start(bf16[8,160,128]{2,1,0:T(8,128)(2,1)S(1)} %constant_dynamic-update-slice_fusion), channel_id=1, source_target_pairs={{8,0},{3,1},{12,4},{7,5},{0,8},{11,9},{4,12},{15,13},{24,16},{19,1... | collective-permute-start | bytes 983048 | tf_op jit(solution)/shard_map/ppermute | solution.py:36
  30.9 1.5 %all-to-all-done = bf16[8,8,80,128]{3,2,1,0:T(8,128)(2,1)S(1)} async-done(((bf16[8,8,80,128]{3,2,1,0:T(8,128)(2,1)}), bf16[8,8,80,128]{3,2,1,0:T(8,128)(2,1)S(1)}, u32[]{:S(2)}, u32[]{:S(2)}) %all-to-all-start) | async-done | bytes 1310752 | tf_op jit(solution)/shard_map/all_to_all | solution.py:94
  32.5 1.1 %copy.9 = bf16[8,8,80,128]{3,2,0,1:T(8,128)(2,1)} copy(bf16[8,8,80,128]{3,2,1,0:T(8,128)(2,1)S(1)} %all-to-all-done) | data formatting | bytes 2621440 | tf_op jit(solution)/shard_map/all_to_all | solution.py:94
  33.6 3.6 %all-to-all-start.1 = ((bf16[8,8,80,128]{3,2,1,0:T(8,128)(2,1)}), bf16[8,8,80,128]{3,2,1,0:T(8,128)(2,1)S(1)}, u32[]{:S(2)}, u32[]{:S(2)}) async-start(bf16[8,8,80,128]{3,2,1,0:T(8,128)(2,1)} %bitcast.12), calls=%async_computation.1 | async-start | bytes 2621440 | tf_op jit(solution)/shard_map/all_to_all | solution.py:94
  37.2 0.0 copy-start.20
  37.2 0.0 copy-start.1
  37.2 0.0 copy-start.2
  37.3 0.0 copy-start.3
  37.3 0.1 pad_maximum_fusion.refs_0_
  37.3 0.5 collective-permute-start.15
  37.8 4.5 %collective-permute-start.6 = (bf16[2,8,160,128]{3,2,1,0:T(8,128)(2,1)S(1)}, bf16[2,8,160,128]{3,2,1,0:T(8,128)(2,1)S(1)}, u32[]{:S(2)}, u32[]{:S(2)}) collective-permute-start(bf16[2,8,160,128]{3,2,1,0:T(8,128)(2,1)S(1)} %pad_maximum_fusion.refs_0_), channel_id=1, source_target_pairs={{1,0},{0,1},{5,4},{4,5},{9,8},{8,9},{13,12},{12,13},{17,16},{16,17... | collective-permute-start | bytes 1966088 | tf_op jit(solution)/shard_map/ppermute | solution.py:36
  42.3 0.9 %collective-permute-start.5 = (bf16[2,8,160,128]{3,2,1,0:T(8,128)(2,1)S(1)}, bf16[2,8,160,128]{3,2,1,0:T(8,128)(2,1)S(1)}, u32[]{:S(2)}, u32[]{:S(2)}) collective-permute-start(bf16[2,8,160,128]{3,2,1,0:T(8,128)(2,1)S(1)} %pad_maximum_fusion.refs_0_), channel_id=1, source_target_pairs={{16,0},{5,1},{20,4},{9,5},{24,8},{13,9},{28,12},{1,13},{2,16},{21,... | collective-permute-start | bytes 1966088 | tf_op jit(solution)/shard_map/ppermute | solution.py:36
  43.2 0.0 collective-permute-done.8
  43.2 0.0 collective-permute-done.7
  43.2 0.7 copy-done.19
  43.9 1.1 %pad_maximum_fusion.1.refs_2_ = bf16[2,8,160,128]{3,2,1,0:T(8,128)(2,1)S(1)} fusion(bf16[1,8,160,128]{3,2,1,0:T(8,128)(2,1)} %bitcast.17, bf16[1,8,160,128]{3,2,1,0:T(8,128)(2,1)} %bitcast.6), kind=kLoop, calls=%fused_computation.2 | loop fusion | flops 327680 | bytes 1310720 | tf_op jit(solution)/shard_map/stack | solution.py:252
  45.1 0.7 collective-permute-start.11
  45.8 2.1 %collective-permute-start.13 = (bf16[2,8,160,128]{3,2,1,0:T(8,128)(2,1)S(1)}, bf16[2,8,160,128]{3,2,1,0:T(8,128)(2,1)S(1)}, u32[]{:S(2)}, u32[]{:S(2)}) collective-permute-start(bf16[2,8,160,128]{3,2,1,0:T(8,128)(2,1)S(1)} %pad_maximum_fusion.1.refs_2_), channel_id=1, source_target_pairs={{16,0},{5,1},{20,4},{9,5},{24,8},{13,9},{28,12},{1,13},{2,16},{21,... | collective-permute-start | bytes 1966088 | tf_op jit(solution)/shard_map/ppermute | solution.py:36
  47.9 4.1 %collective-permute-done.5.refs_4_ = bf16[2,8,160,128]{3,2,1,0:T(8,128)(2,1)S(1)} collective-permute-done((bf16[2,8,160,128]{3,2,1,0:T(8,128)(2,1)S(1)}, bf16[2,8,160,128]{3,2,1,0:T(8,128)(2,1)S(1)}, u32[]{:S(2)}, u32[]{:S(2)}) %collective-permute-start.5) | collective-permute-done | bytes 655392 | tf_op jit(solution)/shard_map/ppermute | solution.py:36
  52.1 0.8 collective-permute-start.9
  52.9 0.1 collective-permute-start.16
  53.0 1.7 %collective-permute-start.17 = (bf16[2,8,160,128]{3,2,1,0:T(8,128)(2,1)S(1)}, bf16[2,8,160,128]{3,2,1,0:T(8,128)(2,1)S(1)}, u32[]{:S(2)}, u32[]{:S(2)}) collective-permute-start(bf16[2,8,160,128]{3,2,1,0:T(8,128)(2,1)S(1)} %collective-permute-done.5.refs_4_), channel_id=1, source_target_pairs={{16,0},{5,1},{20,4},{9,5},{24,8},{13,9},{28,12},{1,13},{2,16},{21,... | collective-permute-start | bytes 1966088 | tf_op jit(solution)/shard_map/ppermute | solution.py:36
  54.7 1.9 %collective-permute-done.11.refs_6_ = bf16[2,8,160,128]{3,2,1,0:T(8,128)(2,1)S(1)} collective-permute-done((bf16[2,8,160,128]{3,2,1,0:T(8,128)(2,1)S(1)}, bf16[2,8,160,128]{3,2,1,0:T(8,128)(2,1)S(1)}, u32[]{:S(2)}, u32[]{:S(2)}) %collective-permute-start.11) | collective-permute-done | bytes 655392 | tf_op jit(solution)/shard_map/ppermute | solution.py:36
  56.5 2.6 %collective-permute-done.13.refs_8_ = bf16[2,8,160,128]{3,2,1,0:T(8,128)(2,1)S(1)} collective-permute-done((bf16[2,8,160,128]{3,2,1,0:T(8,128)(2,1)S(1)}, bf16[2,8,160,128]{3,2,1,0:T(8,128)(2,1)S(1)}, u32[]{:S(2)}, u32[]{:S(2)}) %collective-permute-start.13) | collective-permute-done | bytes 655392 | tf_op jit(solution)/shard_map/ppermute | solution.py:36
  59.1 0.9 %collective-permute-start.10 = (bf16[2,8,160,128]{3,2,1,0:T(8,128)(2,1)S(1)}, bf16[2,8,160,128]{3,2,1,0:T(8,128)(2,1)S(1)}, u32[]{:S(2)}, u32[]{:S(2)}) collective-permute-start(bf16[2,8,160,128]{3,2,1,0:T(8,128)(2,1)S(1)} %collective-permute-done.5.refs_4_), channel_id=1, source_target_pairs={{1,0},{0,1},{5,4},{4,5},{9,8},{8,9},{13,12},{12,13},{17,16},{16,17... | collective-permute-start | bytes 1966088 | tf_op jit(solution)/shard_map/ppermute | solution.py:36
  59.9 0.1 collective-permute-start.12
  60.1 0.4 collective-permute-start.14
  60.5 5.6 %collective-permute-done.17.refs_12_ = bf16[2,8,160,128]{3,2,1,0:T(8,128)(2,1)S(1)} collective-permute-done((bf16[2,8,160,128]{3,2,1,0:T(8,128)(2,1)S(1)}, bf16[2,8,160,128]{3,2,1,0:T(8,128)(2,1)S(1)}, u32[]{:S(2)}, u32[]{:S(2)}) %collective-permute-start.17) | collective-permute-done | bytes 655392 | tf_op jit(solution)/shard_map/ppermute | solution.py:36
  66.1 0.8 collective-permute-start.18
  66.9 0.5 collective-permute-done.19.refs_14_
  67.5 4.0 %collective-permute-start.20 = (bf16[2,8,160,128]{3,2,1,0:T(8,128)(2,1)S(1)}, bf16[2,8,160,128]{3,2,1,0:T(8,128)(2,1)}, u32[]{:S(2)}, u32[]{:S(2)}) collective-permute-start(bf16[2,8,160,128]{3,2,1,0:T(8,128)(2,1)S(1)} %collective-permute-done.19.refs_14_), channel_id=1, source_target_pairs={{1,0},{0,1},{5,4},{4,5},{9,8},{8,9},{13,12},{12,13},{17,16},{16,17... | collective-permute-start | bytes 1966088 | tf_op jit(solution)/shard_map/ppermute | solution.py:36
  71.6 0.7 copy-done.15
  72.3 0.2 copy-done.17
  72.5 0.3 copy-done.16
  72.8 0.8 %copy-done.18 = bf16[2,8,160,128]{3,2,1,0:T(8,128)(2,1)} copy-done((bf16[2,8,160,128]{3,2,1,0:T(8,128)(2,1)}, bf16[2,8,160,128]{3,2,1,0:T(8,128)(2,1)S(1)}, u32[]{:S(2)}) %copy-start.18) | copy-done | bytes 655384
  73.7 9.6 %shard_map.57 = bf16[160,4096]{1,0:T(8,128)(2,1)} custom-call(s32[64]{0:T(128)S(1)} %copy-done.2, s32[2]{0:T(128)S(1)} %copy-done.1, f32[16]{0:T(128)S(1)} %copy-done.3, f32[1,2560]{1,0:T(1,128)S(1)} %broadcast_in_dim.6.eps_vir, bf16[8,8,80,128]{3,2,1,0:T(8,128)(2,1)S(1)} %all-to-all-done.1.packed, bf16[2,8,160,128]{3,2,1,0:T(8,128)(2,1)} %copy-done.4, ...), custom_call_target="tpu_custom_call" | custom-call | tf_op jit(solution)/shard_map/pallas_call | solution.py:210
  (53 shorter events, 0.2 us)
Async XLA Ops:
  0.0 8.2 %copy-start = (bf16[64,160,64]{1,2,0:T(8,128)(2,1)S(1)}, bf16[64,160,64]{1,2,0:T(8,128)(2,1)}, u32[]{:S(2)}) copy-start(bf16[64,160,64]{1,2,0:T(8,128)(2,1)} %param.5) | copy-start | bytes 3932164
  1.7 8.0 %collective-permute-start = (bf16[160,128]{1,0:T(8,128)(2,1)S(1)}, bf16[160,128]{1,0:T(8,128)(2,1)S(1)}, u32[]{:S(2)}, u32[]{:S(2)}) collective-permute-start(bf16[160,128]{1,0:T(8,128)(2,1)S(1)} %shard_map.55), channel_id=1, source_target_pairs={{32,0},{33,1},{36,4},{37,5},{40,8},{41,9},{44,12},{45,13},{48,16},... | collective-permute-start | bytes 122888 | tf_op jit(solution)/shard_map/ppermute | solution.py:36
  9.7 22.8 %all-to-all-start = ((bf16[8,8,80,128]{3,2,1,0:T(8,128)(2,1)}), bf16[8,8,80,128]{3,2,1,0:T(8,128)(2,1)S(1)}, u32[]{:S(2)}, u32[]{:S(2)}) async-start(bf16[8,8,80,128]{3,2,1,0:T(8,128)(2,1)} %shard_map.56), calls=%async_computation | async-start | bytes 2621440 | tf_op jit(solution)/shard_map/all_to_all | solution.py:94
  14.8 12.1 %collective-permute-start.3 = (bf16[2,160,128]{2,1,0:T(8,128)(2,1)S(1)}, bf16[2,160,128]{2,1,0:T(8,128)(2,1)S(1)}, u32[]{:S(2)}, u32[]{:S(2)}) collective-permute-start(bf16[2,160,128]{2,1,0:T(8,128)(2,1)S(1)} %pad_maximum_fusion.2), channel_id=1, source_target_pairs={{192,0},{193,1},{196,4},{197,5},{200,8},{201,9},{204,12},{205,13},... | collective-permute-start | bytes 245768 | tf_op jit(solution)/shard_map/ppermute | solution.py:36
  14.9 12.0 %collective-permute-start.2 = (bf16[2,160,128]{2,1,0:T(8,128)(2,1)S(1)}, bf16[2,160,128]{2,1,0:T(8,128)(2,1)S(1)}, u32[]{:S(2)}, u32[]{:S(2)}) collective-permute-start(bf16[2,160,128]{2,1,0:T(8,128)(2,1)S(1)} %pad_maximum_fusion.2), channel_id=1, source_target_pairs={{128,0},{129,1},{132,4},{133,5},{136,8},{137,9},{140,12},{141,13},... | collective-permute-start | bytes 245768 | tf_op jit(solution)/shard_map/ppermute | solution.py:36
  18.7 8.1 %collective-permute-start.1 = (bf16[2,160,128]{2,1,0:T(8,128)(2,1)S(1)}, bf16[2,160,128]{2,1,0:T(8,128)(2,1)S(1)}, u32[]{:S(2)}, u32[]{:S(2)}) collective-permute-start(bf16[2,160,128]{2,1,0:T(8,128)(2,1)S(1)} %pad_maximum_fusion.2), channel_id=1, source_target_pairs={{64,0},{65,1},{68,4},{69,5},{72,8},{73,9},{76,12},{77,13},{80,16},... | collective-permute-start | bytes 245768 | tf_op jit(solution)/shard_map/ppermute | solution.py:36
  26.9 10.3 %collective-permute-start.4 = (bf16[8,160,128]{2,1,0:T(8,128)(2,1)S(1)}, bf16[8,160,128]{2,1,0:T(8,128)(2,1)S(1)}, u32[]{:S(2)}, u32[]{:S(2)}) collective-permute-start(bf16[8,160,128]{2,1,0:T(8,128)(2,1)S(1)} %constant_dynamic-update-slice_fusion), channel_id=1, source_target_pairs={{4,0},{17,1},{8,4},{21,5},{12,8},{25,9},{0,12},{29,13},{20,16},{3,... | collective-permute-start | bytes 983048 | tf_op jit(solution)/shard_map/ppermute | solution.py:36
  29.6 13.6 %collective-permute-start.8 = (bf16[8,160,128]{2,1,0:T(8,128)(2,1)S(1)}, bf16[8,160,128]{2,1,0:T(8,128)(2,1)S(1)}, u32[]{:S(2)}, u32[]{:S(2)}) collective-permute-start(bf16[8,160,128]{2,1,0:T(8,128)(2,1)S(1)} %constant_dynamic-update-slice_fusion), channel_id=1, source_target_pairs={{12,0},{19,1},{0,4},{23,5},{4,8},{27,9},{8,12},{31,13},{28,16},{1,... | collective-permute-start | bytes 983048 | tf_op jit(solution)/shard_map/ppermute | solution.py:36
  29.6 13.6 %collective-permute-start.7 = (bf16[8,160,128]{2,1,0:T(8,128)(2,1)S(1)}, bf16[8,160,128]{2,1,0:T(8,128)(2,1)}, u32[]{:S(2)}, u32[]{:S(2)}) collective-permute-start(bf16[8,160,128]{2,1,0:T(8,128)(2,1)S(1)} %constant_dynamic-update-slice_fusion), channel_id=1, source_target_pairs={{8,0},{3,1},{12,4},{7,5},{0,8},{11,9},{4,12},{15,13},{24,16},{19,1... | collective-permute-start | bytes 983048 | tf_op jit(solution)/shard_map/ppermute | solution.py:36
  33.6 40.0 %all-to-all-start.1 = ((bf16[8,8,80,128]{3,2,1,0:T(8,128)(2,1)}), bf16[8,8,80,128]{3,2,1,0:T(8,128)(2,1)S(1)}, u32[]{:S(2)}, u32[]{:S(2)}) async-start(bf16[8,8,80,128]{3,2,1,0:T(8,128)(2,1)} %bitcast.12), calls=%async_computation.1 | async-start | bytes 2621440 | tf_op jit(solution)/shard_map/all_to_all | solution.py:94
  37.2 8.5 %copy-start.20 = (f32[2560]{0:T(1024)S(1)}, f32[2560]{0:T(1024)}, u32[]{:S(2)}) copy-start(f32[2560]{0:T(1024)} %param.7) | copy-start | bytes 30724
  37.2 36.4 %copy-start.1 = (s32[2]{0:T(128)S(1)}, s32[2]{0:T(128)}, u32[]{:S(2)}) copy-start(s32[2]{0:T(128)} %order.3) | copy-start | bytes 28
  37.2 36.4 %copy-start.2 = (s32[64]{0:T(128)S(1)}, s32[64]{0:T(128)}, u32[]{:S(2)}) copy-start(s32[64]{0:T(128)} %owner.1) | copy-start | bytes 772
  37.3 36.4 %copy-start.3 = (f32[16]{0:T(128)S(1)}, f32[16]{0:T(128)}, u32[]{:S(2)}) copy-start(f32[16]{0:T(128)} %eps_occ.1) | copy-start | bytes 196
  37.3 36.3 %copy-start.4 = (bf16[2,8,160,128]{3,2,1,0:T(8,128)(2,1)}, bf16[2,8,160,128]{3,2,1,0:T(8,128)(2,1)S(1)}, u32[]{:S(2)}) copy-start(bf16[2,8,160,128]{3,2,1,0:T(8,128)(2,1)S(1)} %pad_maximum_fusion.refs_0_) | copy-start | bytes 1966084
  37.3 15.5 %collective-permute-start.15 = (bf16[2,8,160,128]{3,2,1,0:T(8,128)(2,1)S(1)}, bf16[2,8,160,128]{3,2,1,0:T(8,128)(2,1)S(1)}, u32[]{:S(2)}, u32[]{:S(2)}) collective-permute-start(bf16[2,8,160,128]{3,2,1,0:T(8,128)(2,1)S(1)} %pad_maximum_fusion.refs_0_), channel_id=1, source_target_pairs={{18,0},{13,1},{22,4},{1,5},{26,8},{5,9},{30,12},{9,13},{0,16},{29,... | collective-permute-start | bytes 1966088 | tf_op jit(solution)/shard_map/ppermute | solution.py:36
  37.8 15.2 %collective-permute-start.6 = (bf16[2,8,160,128]{3,2,1,0:T(8,128)(2,1)S(1)}, bf16[2,8,160,128]{3,2,1,0:T(8,128)(2,1)S(1)}, u32[]{:S(2)}, u32[]{:S(2)}) collective-permute-start(bf16[2,8,160,128]{3,2,1,0:T(8,128)(2,1)S(1)} %pad_maximum_fusion.refs_0_), channel_id=1, source_target_pairs={{1,0},{0,1},{5,4},{4,5},{9,8},{8,9},{13,12},{12,13},{17,16},{16,17... | collective-permute-start | bytes 1966088 | tf_op jit(solution)/shard_map/ppermute | solution.py:36
  42.3 9.8 %collective-permute-start.5 = (bf16[2,8,160,128]{3,2,1,0:T(8,128)(2,1)S(1)}, bf16[2,8,160,128]{3,2,1,0:T(8,128)(2,1)S(1)}, u32[]{:S(2)}, u32[]{:S(2)}) collective-permute-start(bf16[2,8,160,128]{3,2,1,0:T(8,128)(2,1)S(1)} %pad_maximum_fusion.refs_0_), channel_id=1, source_target_pairs={{16,0},{5,1},{20,4},{9,5},{24,8},{13,9},{28,12},{1,13},{2,16},{21,... | collective-permute-start | bytes 1966088 | tf_op jit(solution)/shard_map/ppermute | solution.py:36
  43.2 0.7 copy-start.19
  45.1 28.6 %copy-start.5 = (bf16[2,8,160,128]{3,2,1,0:T(8,128)(2,1)}, bf16[2,8,160,128]{3,2,1,0:T(8,128)(2,1)S(1)}, u32[]{:S(2)}) copy-start(bf16[2,8,160,128]{3,2,1,0:T(8,128)(2,1)S(1)} %pad_maximum_fusion.1.refs_2_) | copy-start | bytes 1966084
  45.1 11.4 %collective-permute-start.11 = (bf16[2,8,160,128]{3,2,1,0:T(8,128)(2,1)S(1)}, bf16[2,8,160,128]{3,2,1,0:T(8,128)(2,1)S(1)}, u32[]{:S(2)}, u32[]{:S(2)}) collective-permute-start(bf16[2,8,160,128]{3,2,1,0:T(8,128)(2,1)S(1)} %pad_maximum_fusion.1.refs_2_), channel_id=1, source_target_pairs={{18,0},{13,1},{22,4},{1,5},{26,8},{5,9},{30,12},{9,13},{0,16},{29,... | collective-permute-start | bytes 1966088 | tf_op jit(solution)/shard_map/ppermute | solution.py:36
  45.8 13.3 %collective-permute-start.13 = (bf16[2,8,160,128]{3,2,1,0:T(8,128)(2,1)S(1)}, bf16[2,8,160,128]{3,2,1,0:T(8,128)(2,1)S(1)}, u32[]{:S(2)}, u32[]{:S(2)}) collective-permute-start(bf16[2,8,160,128]{3,2,1,0:T(8,128)(2,1)S(1)} %pad_maximum_fusion.1.refs_2_), channel_id=1, source_target_pairs={{16,0},{5,1},{20,4},{9,5},{24,8},{13,9},{28,12},{1,13},{2,16},{21,... | collective-permute-start | bytes 1966088 | tf_op jit(solution)/shard_map/ppermute | solution.py:36
  52.1 19.4 %copy-start.8 = (bf16[2,8,160,128]{3,2,1,0:T(8,128)(2,1)}, bf16[2,8,160,128]{3,2,1,0:T(8,128)(2,1)S(1)}, u32[]{:S(2)}) copy-start(bf16[2,8,160,128]{3,2,1,0:T(8,128)(2,1)S(1)} %collective-permute-done.5.refs_4_) | copy-start | bytes 1966084
  52.1 7.9 %collective-permute-start.9 = (bf16[2,8,160,128]{3,2,1,0:T(8,128)(2,1)S(1)}, bf16[2,8,160,128]{3,2,1,0:T(8,128)(2,1)S(1)}, u32[]{:S(2)}, u32[]{:S(2)}) collective-permute-start(bf16[2,8,160,128]{3,2,1,0:T(8,128)(2,1)S(1)} %pad_maximum_fusion.1.refs_2_), channel_id=1, source_target_pairs={{1,0},{0,1},{5,4},{4,5},{9,8},{8,9},{13,12},{12,13},{17,16},{16,17... | collective-permute-start | bytes 1966088 | tf_op jit(solution)/shard_map/ppermute | solution.py:36
  52.9 20.7 %copy-start.6 = (bf16[2,8,160,128]{3,2,1,0:T(8,128)(2,1)}, bf16[2,8,160,128]{3,2,1,0:T(8,128)(2,1)S(1)}, u32[]{:S(2)}) copy-start(bf16[2,8,160,128]{3,2,1,0:T(8,128)(2,1)S(1)} %collective-permute-done.15.refs_10_) | copy-start | bytes 1966084
  52.9 7.2 %collective-permute-start.16 = (bf16[2,8,160,128]{3,2,1,0:T(8,128)(2,1)S(1)}, bf16[2,8,160,128]{3,2,1,0:T(8,128)(2,1)S(1)}, u32[]{:S(2)}, u32[]{:S(2)}) collective-permute-start(bf16[2,8,160,128]{3,2,1,0:T(8,128)(2,1)S(1)} %collective-permute-done.15.refs_10_), channel_id=1, source_target_pairs={{1,0},{0,1},{5,4},{4,5},{9,8},{8,9},{13,12},{12,13},{17,16},{16,17... | collective-permute-start | bytes 1966088 | tf_op jit(solution)/shard_map/ppermute | solution.py:36
  53.0 18.5 %copy-start.7 = (bf16[2,8,160,128]{3,2,1,0:T(8,128)(2,1)}, bf16[2,8,160,128]{3,2,1,0:T(8,128)(2,1)S(1)}, u32[]{:S(2)}) copy-start(bf16[2,8,160,128]{3,2,1,0:T(8,128)(2,1)S(1)} %collective-permute-done.6.refs_1_) | copy-start | bytes 1966084
  53.0 13.1 %collective-permute-start.17 = (bf16[2,8,160,128]{3,2,1,0:T(8,128)(2,1)S(1)}, bf16[2,8,160,128]{3,2,1,0:T(8,128)(2,1)S(1)}, u32[]{:S(2)}, u32[]{:S(2)}) collective-permute-start(bf16[2,8,160,128]{3,2,1,0:T(8,128)(2,1)S(1)} %collective-permute-done.5.refs_4_), channel_id=1, source_target_pairs={{16,0},{5,1},{20,4},{9,5},{24,8},{13,9},{28,12},{1,13},{2,16},{21,... | collective-permute-start | bytes 1966088 | tf_op jit(solution)/shard_map/ppermute | solution.py:36
  56.5 15.0 %copy-start.9 = (bf16[2,8,160,128]{3,2,1,0:T(8,128)(2,1)}, bf16[2,8,160,128]{3,2,1,0:T(8,128)(2,1)S(1)}, u32[]{:S(2)}) copy-start(bf16[2,8,160,128]{3,2,1,0:T(8,128)(2,1)S(1)} %collective-permute-done.11.refs_6_) | copy-start | bytes 1966084
  56.5 10.9 %collective-permute-start.19 = (bf16[2,8,160,128]{3,2,1,0:T(8,128)(2,1)S(1)}, bf16[2,8,160,128]{3,2,1,0:T(8,128)(2,1)S(1)}, u32[]{:S(2)}, u32[]{:S(2)}) collective-permute-start(bf16[2,8,160,128]{3,2,1,0:T(8,128)(2,1)S(1)} %collective-permute-done.11.refs_6_), channel_id=1, source_target_pairs={{18,0},{13,1},{22,4},{1,5},{26,8},{5,9},{30,12},{9,13},{0,16},{29,... | collective-permute-start | bytes 1966088 | tf_op jit(solution)/shard_map/ppermute | solution.py:36
  59.1 12.5 %copy-start.10 = (bf16[2,8,160,128]{3,2,1,0:T(8,128)(2,1)}, bf16[2,8,160,128]{3,2,1,0:T(8,128)(2,1)S(1)}, u32[]{:S(2)}) copy-start(bf16[2,8,160,128]{3,2,1,0:T(8,128)(2,1)S(1)} %collective-permute-done.13.refs_8_) | copy-start | bytes 1966084
  59.1 12.4 %collective-permute-start.10 = (bf16[2,8,160,128]{3,2,1,0:T(8,128)(2,1)S(1)}, bf16[2,8,160,128]{3,2,1,0:T(8,128)(2,1)S(1)}, u32[]{:S(2)}, u32[]{:S(2)}) collective-permute-start(bf16[2,8,160,128]{3,2,1,0:T(8,128)(2,1)S(1)} %collective-permute-done.5.refs_4_), channel_id=1, source_target_pairs={{1,0},{0,1},{5,4},{4,5},{9,8},{8,9},{13,12},{12,13},{17,16},{16,17... | collective-permute-start | bytes 1966088 | tf_op jit(solution)/shard_map/ppermute | solution.py:36
  59.9 11.6 %copy-start.11 = (bf16[2,8,160,128]{3,2,1,0:T(8,128)(2,1)}, bf16[2,8,160,128]{3,2,1,0:T(8,128)(2,1)S(1)}, u32[]{:S(2)}) copy-start(bf16[2,8,160,128]{3,2,1,0:T(8,128)(2,1)S(1)} %collective-permute-done.9.refs_3_) | copy-start | bytes 1966084
  59.9 11.5 %collective-permute-start.12 = (bf16[2,8,160,128]{3,2,1,0:T(8,128)(2,1)S(1)}, bf16[2,8,160,128]{3,2,1,0:T(8,128)(2,1)S(1)}, u32[]{:S(2)}, u32[]{:S(2)}) collective-permute-start(bf16[2,8,160,128]{3,2,1,0:T(8,128)(2,1)S(1)} %collective-permute-done.11.refs_6_), channel_id=1, source_target_pairs={{1,0},{0,1},{5,4},{4,5},{9,8},{8,9},{13,12},{12,13},{17,16},{16,17... | collective-permute-start | bytes 1966088 | tf_op jit(solution)/shard_map/ppermute | solution.py:36
  60.1 11.5 %copy-start.12 = (bf16[2,8,160,128]{3,2,1,0:T(8,128)(2,1)}, bf16[2,8,160,128]{3,2,1,0:T(8,128)(2,1)S(1)}, u32[]{:S(2)}) copy-start(bf16[2,8,160,128]{3,2,1,0:T(8,128)(2,1)S(1)} %collective-permute-done.16.refs_11_) | copy-start | bytes 1966084
  60.1 11.4 %collective-permute-start.14 = (bf16[2,8,160,128]{3,2,1,0:T(8,128)(2,1)S(1)}, bf16[2,8,160,128]{3,2,1,0:T(8,128)(2,1)S(1)}, u32[]{:S(2)}, u32[]{:S(2)}) collective-permute-start(bf16[2,8,160,128]{3,2,1,0:T(8,128)(2,1)S(1)} %collective-permute-done.13.refs_8_), channel_id=1, source_target_pairs={{1,0},{0,1},{5,4},{4,5},{9,8},{8,9},{13,12},{12,13},{17,16},{16,17... | collective-permute-start | bytes 1966088 | tf_op jit(solution)/shard_map/ppermute | solution.py:36
  66.1 5.5 %copy-start.13 = (bf16[2,8,160,128]{3,2,1,0:T(8,128)(2,1)}, bf16[2,8,160,128]{3,2,1,0:T(8,128)(2,1)S(1)}, u32[]{:S(2)}) copy-start(bf16[2,8,160,128]{3,2,1,0:T(8,128)(2,1)S(1)} %collective-permute-done.17.refs_12_) | copy-start | bytes 1966084
  66.1 5.4 %collective-permute-start.18 = (bf16[2,8,160,128]{3,2,1,0:T(8,128)(2,1)S(1)}, bf16[2,8,160,128]{3,2,1,0:T(8,128)(2,1)S(1)}, u32[]{:S(2)}, u32[]{:S(2)}) collective-permute-start(bf16[2,8,160,128]{3,2,1,0:T(8,128)(2,1)S(1)} %collective-permute-done.17.refs_12_), channel_id=1, source_target_pairs={{1,0},{0,1},{5,4},{4,5},{9,8},{8,9},{13,12},{12,13},{17,16},{16,17... | collective-permute-start | bytes 1966088 | tf_op jit(solution)/shard_map/ppermute | solution.py:36
  67.5 4.1 %copy-start.14 = (bf16[2,8,160,128]{3,2,1,0:T(8,128)(2,1)}, bf16[2,8,160,128]{3,2,1,0:T(8,128)(2,1)S(1)}, u32[]{:S(2)}) copy-start(bf16[2,8,160,128]{3,2,1,0:T(8,128)(2,1)S(1)} %collective-permute-done.19.refs_14_) | copy-start | bytes 1966084
  67.5 6.1 %collective-permute-start.20 = (bf16[2,8,160,128]{3,2,1,0:T(8,128)(2,1)S(1)}, bf16[2,8,160,128]{3,2,1,0:T(8,128)(2,1)}, u32[]{:S(2)}, u32[]{:S(2)}) collective-permute-start(bf16[2,8,160,128]{3,2,1,0:T(8,128)(2,1)S(1)} %collective-permute-done.19.refs_14_), channel_id=1, source_target_pairs={{1,0},{0,1},{5,4},{4,5},{9,8},{8,9},{13,12},{12,13},{17,16},{16,17... | collective-permute-start | bytes 1966088 | tf_op jit(solution)/shard_map/ppermute | solution.py:36
  71.5 0.8 copy-start.15
  71.5 1.0 %copy-start.17 = (bf16[2,8,160,128]{3,2,1,0:T(8,128)(2,1)}, bf16[2,8,160,128]{3,2,1,0:T(8,128)(2,1)S(1)}, u32[]{:S(2)}) copy-start(bf16[2,8,160,128]{3,2,1,0:T(8,128)(2,1)S(1)} %collective-permute-done.14.refs_9_) | copy-start | bytes 1966084
  71.5 1.3 %copy-start.16 = (bf16[2,8,160,128]{3,2,1,0:T(8,128)(2,1)}, bf16[2,8,160,128]{3,2,1,0:T(8,128)(2,1)S(1)}, u32[]{:S(2)}) copy-start(bf16[2,8,160,128]{3,2,1,0:T(8,128)(2,1)S(1)} %collective-permute-done.12.refs_7_) | copy-start | bytes 1966084
  72.8 0.8 %copy-start.18 = (bf16[2,8,160,128]{3,2,1,0:T(8,128)(2,1)}, bf16[2,8,160,128]{3,2,1,0:T(8,128)(2,1)S(1)}, u32[]{:S(2)}) copy-start(bf16[2,8,160,128]{3,2,1,0:T(8,128)(2,1)S(1)} %collective-permute-done.18.refs_13_) | copy-start | bytes 1966084

commit v6 on v5

--- a/solution.py
+++ b/solution.py
@@ -254,12 +254,12 @@
     keep(high, 0, 2)
     ahead_low, behind_high = fetch(low, second=1), fetch(high, second=3)
     ahead_high, behind_low = fetch(high, second=1), fetch(low, second=3)
-    ahead_low, vir_row = lax.optimization_barrier((ahead_low, eps_vir[None]))
     keep(ahead_low, 1, 0)
     keep(behind_high, 3, 2)
     keep(ahead_high, 1, 2)
     keep(behind_low, 3, 0)
-    keep(fetch(ahead_low, second=1), 2, 0)
+    opposite, vir_row = lax.optimization_barrier((fetch(ahead_low, second=1), eps_vir[None]))
+    keep(opposite, 2, 0)
     keep(fetch(behind_high, second=3), 2, 2)
 
     return gamma(block_owner, round_order, eps_occ, vir_row, packed, pieces, tuple(layout))[None]

time: 83.7 us -> 96.4 us (1.15)
  waiting for transfers between devices: 22 us -> 34.1 us
    ppermute x21, waiting for transfers between devices: 20.5 us -> 33.8 us  [fetch(): return lax.ppermute(block, BOTH, pairs)]
    all_to_all x2, waiting for transfers between devices: 1.55 us -> 0.28 us  [exchange(): lax.all_to_all(packed, 'occ', split_axis=0, concat_axis=0, axis_index_gro...]
  transfers between devices with their start and end apart: 23 -> 23, of which waited for: 7 -> 8; matrix products, arithmetic and copies ran while one was open for 3% -> 3% of each run, Pallas kernels for 2% -> 2%
where the time goes in v6:
time: 96.4 us; the launch traced here: 96.2 us
  starting transfers between devices  43.7 us (45%)
  waiting for transfers between devices  34.1 us (35%)
  Pallas kernels  12.8 us (13%)
  local copies, waits for them, and re-layouts  3.86 us (4%)
  other arithmetic  1.2 us (1%)
    ppermute x21, starting transfers between devices, fetch(): return lax.ppermute(block, BOTH, pairs)  34.8 us
    ppermute x21, waiting for transfers between devices, fetch(): return lax.ppermute(block, BOTH, pairs)  33.8 us
    pallas_call x1, Pallas kernels, gamma(): pl.pallas_call(functools.partial(gamma_kernel, layout), in_specs=[smem] *...  9.63 us
    all_to_all x2, starting transfers between devices, exchange(): lax.all_to_all(packed, 'occ', split_axis=0, concat_axis=0, axis_index_gro...  8.92 us
    unnamed x46, local copies, waits for them, and re-layouts  2.69 us
  transfers between devices with their start and end apart: 23, of which 8 were waited for; matrix products, arithmetic and copies ran while one was open for 3% of the time, Pallas kernels for 2%

profile of v6, /device:TPU:1, one launch (start us, length us, event | category | flops | bytes accessed | tf_op | source)
XLA Modules:
  0.0 96.2 jit_solution(8227743020840176414)
XLA Ops:
  0.0 1.7 %shard_map.55 = bf16[160,128]{1,0:T(8,128)(2,1)S(1)} custom-call(s32[2]{0:T(128)} %order.3, bf16[64,64,160]{2,1,0:T(8,128)(2,1)} %bitcast.13), custom_call_target="tpu_custom_call" | custom-call | tf_op jit(solution)/shard_map/pallas_call | solution.py:59
  1.7 6.5 %collective-permute-start = (bf16[160,128]{1,0:T(8,128)(2,1)S(1)}, bf16[160,128]{1,0:T(8,128)(2,1)S(1)}, u32[]{:S(2)}, u32[]{:S(2)}) collective-permute-start(bf16[160,128]{1,0:T(8,128)(2,1)S(1)} %shard_map.55), channel_id=1, source_target_pairs={{32,0},{33,1},{36,4},{37,5},{40,8},{41,9},{44,12},{45,13},{48,16},... | collective-permute-start | bytes 122888 | tf_op jit(solution)/shard_map/ppermute | solution.py:36
  8.2 1.5 %shard_map.56 = bf16[8,8,80,128]{3,2,1,0:T(8,128)(2,1)} custom-call(bf16[64,64,160]{2,1,0:T(8,128)(2,1)S(1)} %bitcast.14), custom_call_target="tpu_custom_call" | custom-call | tf_op jit(solution)/shard_map/pallas_call | solution.py:82
  9.7 0.0 collective-permute-done
  9.7 0.1 collective-permute-start.3
  9.8 3.9 %collective-permute-start.2 = (bf16[2,160,128]{2,1,0:T(8,128)(2,1)S(1)}, bf16[2,160,128]{2,1,0:T(8,128)(2,1)S(1)}, u32[]{:S(2)}, u32[]{:S(2)}) collective-permute-start(bf16[2,160,128]{2,1,0:T(8,128)(2,1)S(1)} %pad_maximum_fusion.2), channel_id=1, source_target_pairs={{128,0},{129,1},{132,4},{133,5},{136,8},{137,9},{140,12},{141,13},... | collective-permute-start | bytes 245768 | tf_op jit(solution)/shard_map/ppermute | solution.py:36
  13.6 2.4 %collective-permute-start.1 = (bf16[2,160,128]{2,1,0:T(8,128)(2,1)S(1)}, bf16[2,160,128]{2,1,0:T(8,128)(2,1)S(1)}, u32[]{:S(2)}, u32[]{:S(2)}) collective-permute-start(bf16[2,160,128]{2,1,0:T(8,128)(2,1)S(1)} %pad_maximum_fusion.2), channel_id=1, source_target_pairs={{64,0},{65,1},{68,4},{69,5},{72,8},{73,9},{76,12},{77,13},{80,16},... | collective-permute-start | bytes 245768 | tf_op jit(solution)/shard_map/ppermute | solution.py:36
  16.0 5.1 %all-to-all-start = ((bf16[8,8,80,128]{3,2,1,0:T(8,128)(2,1)}), bf16[8,8,80,128]{3,2,1,0:T(8,128)(2,1)S(1)}, u32[]{:S(2)}, u32[]{:S(2)}) async-start(bf16[8,8,80,128]{3,2,1,0:T(8,128)(2,1)} %shard_map.56), calls=%async_computation | async-start | bytes 2621440 | tf_op jit(solution)/shard_map/all_to_all | solution.py:94
  21.1 0.6 collective-permute-done.1
  21.8 0.0 collective-permute-done.2
  21.8 0.0 collective-permute-done.3
  21.9 2.6 %collective-permute-start.4 = (bf16[8,160,128]{2,1,0:T(8,128)(2,1)S(1)}, bf16[8,160,128]{2,1,0:T(8,128)(2,1)S(1)}, u32[]{:S(2)}, u32[]{:S(2)}) collective-permute-start(bf16[8,160,128]{2,1,0:T(8,128)(2,1)S(1)} %constant_dynamic-update-slice_fusion), channel_id=1, source_target_pairs={{4,0},{17,1},{8,4},{21,5},{12,8},{25,9},{0,12},{29,13},{20,16},{3,... | collective-permute-start | bytes 983048 | tf_op jit(solution)/shard_map/ppermute | solution.py:36
  24.4 17.2 %collective-permute-done.4 = bf16[8,160,128]{2,1,0:T(8,128)(2,1)S(1)} collective-permute-done((bf16[8,160,128]{2,1,0:T(8,128)(2,1)S(1)}, bf16[8,160,128]{2,1,0:T(8,128)(2,1)S(1)}, u32[]{:S(2)}, u32[]{:S(2)}) %collective-permute-start.4) | collective-permute-done | bytes 327712 | tf_op jit(solution)/shard_map/ppermute | solution.py:36
  41.6 0.1 pad_maximum_fusion.refs_0_
  41.7 2.4 %collective-permute-start.5 = (bf16[2,8,160,128]{3,2,1,0:T(8,128)(2,1)S(1)}, bf16[2,8,160,128]{3,2,1,0:T(8,128)(2,1)S(1)}, u32[]{:S(2)}, u32[]{:S(2)}) collective-permute-start(bf16[2,8,160,128]{3,2,1,0:T(8,128)(2,1)S(1)} %pad_maximum_fusion.refs_0_), channel_id=1, source_target_pairs={{16,0},{5,1},{20,4},{9,5},{24,8},{13,9},{28,12},{1,13},{2,16},{21,... | collective-permute-start | bytes 1966088 | tf_op jit(solution)/shard_map/ppermute | solution.py:36
  44.1 0.0 collective-permute-start.9
  44.1 2.5 %collective-permute-start.8 = (bf16[8,160,128]{2,1,0:T(8,128)(2,1)S(1)}, bf16[8,160,128]{2,1,0:T(8,128)(2,1)}, u32[]{:S(2)}, u32[]{:S(2)}) collective-permute-start(bf16[8,160,128]{2,1,0:T(8,128)(2,1)S(1)} %constant_dynamic-update-slice_fusion), channel_id=1, source_target_pairs={{8,0},{3,1},{12,4},{7,5},{0,8},{11,9},{4,12},{15,13},{24,16},{19,1... | collective-permute-start | bytes 983048 | tf_op jit(solution)/shard_map/ppermute | solution.py:36
  46.6 0.0 all-to-all-done
  46.6 1.1 %copy.9 = bf16[8,8,80,128]{3,2,0,1:T(8,128)(2,1)} copy(bf16[8,8,80,128]{3,2,1,0:T(8,128)(2,1)S(1)} %all-to-all-done) | data formatting | bytes 2621440 | tf_op jit(solution)/shard_map/all_to_all | solution.py:94
  47.7 3.8 %all-to-all-start.1 = ((bf16[8,8,80,128]{3,2,1,0:T(8,128)(2,1)}), bf16[8,8,80,128]{3,2,1,0:T(8,128)(2,1)S(1)}, u32[]{:S(2)}, u32[]{:S(2)}) async-start(bf16[8,8,80,128]{3,2,1,0:T(8,128)(2,1)} %bitcast.12), calls=%async_computation.1 | async-start | bytes 2621440 | tf_op jit(solution)/shard_map/all_to_all | solution.py:94
  51.5 0.0 copy-start.1
  51.5 0.0 copy-start.2
  51.5 0.0 copy-start.3
  51.6 0.1 collective-permute-start.16
  51.6 3.5 %collective-permute-done.9 = bf16[8,160,128]{2,1,0:T(8,128)(2,1)S(1)} collective-permute-done((bf16[8,160,128]{2,1,0:T(8,128)(2,1)S(1)}, bf16[8,160,128]{2,1,0:T(8,128)(2,1)S(1)}, u32[]{:S(2)}, u32[]{:S(2)}) %collective-permute-start.9) | collective-permute-done | bytes 327712 | tf_op jit(solution)/shard_map/ppermute | solution.py:36
  55.2 0.7 copy-done.19
  55.9 1.1 %pad_maximum_fusion.1.refs_2_ = bf16[2,8,160,128]{3,2,1,0:T(8,128)(2,1)S(1)} fusion(bf16[1,8,160,128]{3,2,1,0:T(8,128)(2,1)} %bitcast.17, bf16[1,8,160,128]{3,2,1,0:T(8,128)(2,1)} %bitcast.6), kind=kLoop, calls=%fused_computation.2 | loop fusion | flops 327680 | bytes 1310720 | tf_op jit(solution)/shard_map/stack | solution.py:252
  57.0 0.1 collective-permute-start.12
  57.1 2.6 %collective-permute-start.6 = (bf16[2,8,160,128]{3,2,1,0:T(8,128)(2,1)S(1)}, bf16[2,8,160,128]{3,2,1,0:T(8,128)(2,1)S(1)}, u32[]{:S(2)}, u32[]{:S(2)}) collective-permute-start(bf16[2,8,160,128]{3,2,1,0:T(8,128)(2,1)S(1)} %collective-permute-done.5.refs_4_), channel_id=1, source_target_pairs={{16,0},{5,1},{20,4},{9,5},{24,8},{13,9},{28,12},{1,13},{2,16},{21,... | collective-permute-start | bytes 1966088 | tf_op jit(solution)/shard_map/ppermute | solution.py:36
  59.8 2.6 %collective-permute-start.7 = (bf16[2,8,160,128]{3,2,1,0:T(8,128)(2,1)S(1)}, bf16[2,8,160,128]{3,2,1,0:T(8,128)(2,1)S(1)}, u32[]{:S(2)}, u32[]{:S(2)}) collective-permute-start(bf16[2,8,160,128]{3,2,1,0:T(8,128)(2,1)S(1)} %pad_maximum_fusion.refs_0_), channel_id=1, source_target_pairs={{1,0},{0,1},{5,4},{4,5},{9,8},{8,9},{13,12},{12,13},{17,16},{16,17... | collective-permute-start | bytes 1966088 | tf_op jit(solution)/shard_map/ppermute | solution.py:36
  62.4 0.1 collective-permute-start.14
  62.5 1.0 %collective-permute-done.16.refs_10_ = bf16[2,8,160,128]{3,2,1,0:T(8,128)(2,1)S(1)} collective-permute-done((bf16[2,8,160,128]{3,2,1,0:T(8,128)(2,1)S(1)}, bf16[2,8,160,128]{3,2,1,0:T(8,128)(2,1)S(1)}, u32[]{:S(2)}, u32[]{:S(2)}) %collective-permute-start.16) | collective-permute-done | bytes 655392 | tf_op jit(solution)/shard_map/ppermute | solution.py:36
  63.5 1.6 %collective-permute-start.10 = (bf16[2,8,160,128]{3,2,1,0:T(8,128)(2,1)S(1)}, bf16[2,8,160,128]{3,2,1,0:T(8,128)(2,1)S(1)}, u32[]{:S(2)}, u32[]{:S(2)}) collective-permute-start(bf16[2,8,160,128]{3,2,1,0:T(8,128)(2,1)S(1)} %pad_maximum_fusion.1.refs_2_), channel_id=1, source_target_pairs={{1,0},{0,1},{5,4},{4,5},{9,8},{8,9},{13,12},{12,13},{17,16},{16,17... | collective-permute-start | bytes 1966088 | tf_op jit(solution)/shard_map/ppermute | solution.py:36
  65.1 5.4 %collective-permute-done.12.refs_6_ = bf16[2,8,160,128]{3,2,1,0:T(8,128)(2,1)S(1)} collective-permute-done((bf16[2,8,160,128]{3,2,1,0:T(8,128)(2,1)S(1)}, bf16[2,8,160,128]{3,2,1,0:T(8,128)(2,1)S(1)}, u32[]{:S(2)}, u32[]{:S(2)}) %collective-permute-start.12) | collective-permute-done | bytes 655392 | tf_op jit(solution)/shard_map/ppermute | solution.py:36
  70.5 1.6 %collective-permute-start.17 = (bf16[2,8,160,128]{3,2,1,0:T(8,128)(2,1)S(1)}, bf16[2,8,160,128]{3,2,1,0:T(8,128)(2,1)S(1)}, u32[]{:S(2)}, u32[]{:S(2)}) collective-permute-start(bf16[2,8,160,128]{3,2,1,0:T(8,128)(2,1)S(1)} %collective-permute-done.16.refs_10_), channel_id=1, source_target_pairs={{1,0},{0,1},{5,4},{4,5},{9,8},{8,9},{13,12},{12,13},{17,16},{16,17... | collective-permute-start | bytes 1966088 | tf_op jit(solution)/shard_map/ppermute | solution.py:36
  72.2 0.9 collective-permute-start.19
  73.1 0.3 collective-permute-start.11
  73.4 1.0 collective-permute-done.14.refs_8_
  74.3 3.2 %collective-permute-start.13 = (bf16[2,8,160,128]{3,2,1,0:T(8,128)(2,1)S(1)}, bf16[2,8,160,128]{3,2,1,0:T(8,128)(2,1)S(1)}, u32[]{:S(2)}, u32[]{:S(2)}) collective-permute-start(bf16[2,8,160,128]{3,2,1,0:T(8,128)(2,1)S(1)} %collective-permute-done.12.refs_6_), channel_id=1, source_target_pairs={{1,0},{0,1},{5,4},{4,5},{9,8},{8,9},{13,12},{12,13},{17,16},{16,17... | collective-permute-start | bytes 1966088 | tf_op jit(solution)/shard_map/ppermute | solution.py:36
  77.5 0.1 collective-permute-start.15
  77.6 0.4 collective-permute-start.18
  78.0 5.1 %collective-permute-done.19.refs_14_ = bf16[2,8,160,128]{3,2,1,0:T(8,128)(2,1)S(1)} collective-permute-done((bf16[2,8,160,128]{3,2,1,0:T(8,128)(2,1)S(1)}, bf16[2,8,160,128]{3,2,1,0:T(8,128)(2,1)S(1)}, u32[]{:S(2)}, u32[]{:S(2)}) %collective-permute-start.19) | collective-permute-done | bytes 655392 | tf_op jit(solution)/shard_map/ppermute | solution.py:36
  83.1 0.9 collective-permute-start.20
  84.2 0.8 copy-done.17
  85.0 0.2 copy-done.16
  85.2 0.8 copy-done.18
  86.0 0.3 all-to-all-done.1.packed
  86.4 9.6 %shard_map.57 = bf16[160,4096]{1,0:T(8,128)(2,1)} custom-call(s32[64]{0:T(128)S(1)} %copy-done.2, s32[2]{0:T(128)S(1)} %copy-done.1, f32[16]{0:T(128)S(1)} %copy-done.3, f32[1,2560]{1,0:T(1,128)S(1)} %broadcast_in_dim.6.eps_vir, bf16[8,8,80,128]{3,2,1,0:T(8,128)(2,1)S(1)} %all-to-all-done.1.packed, bf16[2,8,160,128]{3,2,1,0:T(8,128)(2,1)} %copy-done.4, ...), custom_call_target="tpu_custom_call" | custom-call | tf_op jit(solution)/shard_map/pallas_call | solution.py:210
  (53 shorter events, 0.2 us)
Async XLA Ops:
  0.0 8.2 %copy-start = (bf16[64,160,64]{1,2,0:T(8,128)(2,1)S(1)}, bf16[64,160,64]{1,2,0:T(8,128)(2,1)}, u32[]{:S(2)}) copy-start(bf16[64,160,64]{1,2,0:T(8,128)(2,1)} %param.5) | copy-start | bytes 3932164
  1.7 8.0 %collective-permute-start = (bf16[160,128]{1,0:T(8,128)(2,1)S(1)}, bf16[160,128]{1,0:T(8,128)(2,1)S(1)}, u32[]{:S(2)}, u32[]{:S(2)}) collective-permute-start(bf16[160,128]{1,0:T(8,128)(2,1)S(1)} %shard_map.55), channel_id=1, source_target_pairs={{32,0},{33,1},{36,4},{37,5},{40,8},{41,9},{44,12},{45,13},{48,16},... | collective-permute-start | bytes 122888 | tf_op jit(solution)/shard_map/ppermute | solution.py:36
  9.7 12.2 %collective-permute-start.3 = (bf16[2,160,128]{2,1,0:T(8,128)(2,1)S(1)}, bf16[2,160,128]{2,1,0:T(8,128)(2,1)S(1)}, u32[]{:S(2)}, u32[]{:S(2)}) collective-permute-start(bf16[2,160,128]{2,1,0:T(8,128)(2,1)S(1)} %pad_maximum_fusion.2), channel_id=1, source_target_pairs={{192,0},{193,1},{196,4},{197,5},{200,8},{201,9},{204,12},{205,13},... | collective-permute-start | bytes 245768 | tf_op jit(solution)/shard_map/ppermute | solution.py:36
  9.8 12.0 %collective-permute-start.2 = (bf16[2,160,128]{2,1,0:T(8,128)(2,1)S(1)}, bf16[2,160,128]{2,1,0:T(8,128)(2,1)S(1)}, u32[]{:S(2)}, u32[]{:S(2)}) collective-permute-start(bf16[2,160,128]{2,1,0:T(8,128)(2,1)S(1)} %pad_maximum_fusion.2), channel_id=1, source_target_pairs={{128,0},{129,1},{132,4},{133,5},{136,8},{137,9},{140,12},{141,13},... | collective-permute-start | bytes 245768 | tf_op jit(solution)/shard_map/ppermute | solution.py:36
  13.6 8.2 %collective-permute-start.1 = (bf16[2,160,128]{2,1,0:T(8,128)(2,1)S(1)}, bf16[2,160,128]{2,1,0:T(8,128)(2,1)S(1)}, u32[]{:S(2)}, u32[]{:S(2)}) collective-permute-start(bf16[2,160,128]{2,1,0:T(8,128)(2,1)S(1)} %pad_maximum_fusion.2), channel_id=1, source_target_pairs={{64,0},{65,1},{68,4},{69,5},{72,8},{73,9},{76,12},{77,13},{80,16},... | collective-permute-start | bytes 245768 | tf_op jit(solution)/shard_map/ppermute | solution.py:36
  16.0 30.5 %all-to-all-start = ((bf16[8,8,80,128]{3,2,1,0:T(8,128)(2,1)}), bf16[8,8,80,128]{3,2,1,0:T(8,128)(2,1)S(1)}, u32[]{:S(2)}, u32[]{:S(2)}) async-start(bf16[8,8,80,128]{3,2,1,0:T(8,128)(2,1)} %shard_map.56), calls=%async_computation | async-start | bytes 2621440 | tf_op jit(solution)/shard_map/all_to_all | solution.py:94
  21.9 19.7 %collective-permute-start.4 = (bf16[8,160,128]{2,1,0:T(8,128)(2,1)S(1)}, bf16[8,160,128]{2,1,0:T(8,128)(2,1)S(1)}, u32[]{:S(2)}, u32[]{:S(2)}) collective-permute-start(bf16[8,160,128]{2,1,0:T(8,128)(2,1)S(1)} %constant_dynamic-update-slice_fusion), channel_id=1, source_target_pairs={{4,0},{17,1},{8,4},{21,5},{12,8},{25,9},{0,12},{29,13},{20,16},{3,... | collective-permute-start | bytes 983048 | tf_op jit(solution)/shard_map/ppermute | solution.py:36
  41.7 18.1 %copy-start.4 = (bf16[2,8,160,128]{3,2,1,0:T(8,128)(2,1)}, bf16[2,8,160,128]{3,2,1,0:T(8,128)(2,1)S(1)}, u32[]{:S(2)}) copy-start(bf16[2,8,160,128]{3,2,1,0:T(8,128)(2,1)S(1)} %pad_maximum_fusion.refs_0_) | copy-start | bytes 1966084
  41.7 15.4 %collective-permute-start.5 = (bf16[2,8,160,128]{3,2,1,0:T(8,128)(2,1)S(1)}, bf16[2,8,160,128]{3,2,1,0:T(8,128)(2,1)S(1)}, u32[]{:S(2)}, u32[]{:S(2)}) collective-permute-start(bf16[2,8,160,128]{3,2,1,0:T(8,128)(2,1)S(1)} %pad_maximum_fusion.refs_0_), channel_id=1, source_target_pairs={{16,0},{5,1},{20,4},{9,5},{24,8},{13,9},{28,12},{1,13},{2,16},{21,... | collective-permute-start | bytes 1966088 | tf_op jit(solution)/shard_map/ppermute | solution.py:36
  44.1 11.0 %collective-permute-start.9 = (bf16[8,160,128]{2,1,0:T(8,128)(2,1)S(1)}, bf16[8,160,128]{2,1,0:T(8,128)(2,1)S(1)}, u32[]{:S(2)}, u32[]{:S(2)}) collective-permute-start(bf16[8,160,128]{2,1,0:T(8,128)(2,1)S(1)} %constant_dynamic-update-slice_fusion), channel_id=1, source_target_pairs={{12,0},{19,1},{0,4},{23,5},{4,8},{27,9},{8,12},{31,13},{28,16},{1,... | collective-permute-start | bytes 983048 | tf_op jit(solution)/shard_map/ppermute | solution.py:36
  44.1 11.0 %collective-permute-start.8 = (bf16[8,160,128]{2,1,0:T(8,128)(2,1)S(1)}, bf16[8,160,128]{2,1,0:T(8,128)(2,1)}, u32[]{:S(2)}, u32[]{:S(2)}) collective-permute-start(bf16[8,160,128]{2,1,0:T(8,128)(2,1)S(1)} %constant_dynamic-update-slice_fusion), channel_id=1, source_target_pairs={{8,0},{3,1},{12,4},{7,5},{0,8},{11,9},{4,12},{15,13},{24,16},{19,1... | collective-permute-start | bytes 983048 | tf_op jit(solution)/shard_map/ppermute | solution.py:36
  47.7 38.6 %all-to-all-start.1 = ((bf16[8,8,80,128]{3,2,1,0:T(8,128)(2,1)}), bf16[8,8,80,128]{3,2,1,0:T(8,128)(2,1)S(1)}, u32[]{:S(2)}, u32[]{:S(2)}) async-start(bf16[8,8,80,128]{3,2,1,0:T(8,128)(2,1)} %bitcast.12), calls=%async_computation.1 | async-start | bytes 2621440 | tf_op jit(solution)/shard_map/all_to_all | solution.py:94
  51.5 21.6 %copy-start.20 = (f32[2560]{0:T(1024)S(1)}, f32[2560]{0:T(1024)}, u32[]{:S(2)}) copy-start(f32[2560]{0:T(1024)} %param.7) | copy-start | bytes 30724
  51.5 34.8 %copy-start.1 = (s32[2]{0:T(128)S(1)}, s32[2]{0:T(128)}, u32[]{:S(2)}) copy-start(s32[2]{0:T(128)} %order.3) | copy-start | bytes 28
  51.5 34.8 %copy-start.2 = (s32[64]{0:T(128)S(1)}, s32[64]{0:T(128)}, u32[]{:S(2)}) copy-start(s32[64]{0:T(128)} %owner.1) | copy-start | bytes 772
  51.5 34.8 %copy-start.3 = (f32[16]{0:T(128)S(1)}, f32[16]{0:T(128)}, u32[]{:S(2)}) copy-start(f32[16]{0:T(128)} %eps_occ.1) | copy-start | bytes 196
  51.6 11.9 %collective-permute-start.16 = (bf16[2,8,160,128]{3,2,1,0:T(8,128)(2,1)S(1)}, bf16[2,8,160,128]{3,2,1,0:T(8,128)(2,1)S(1)}, u32[]{:S(2)}, u32[]{:S(2)}) collective-permute-start(bf16[2,8,160,128]{3,2,1,0:T(8,128)(2,1)S(1)} %pad_maximum_fusion.refs_0_), channel_id=1, source_target_pairs={{18,0},{13,1},{22,4},{1,5},{26,8},{5,9},{30,12},{9,13},{0,16},{29,... | collective-permute-start | bytes 1966088 | tf_op jit(solution)/shard_map/ppermute | solution.py:36
  55.2 0.7 copy-start.19
  57.0 29.3 %copy-start.5 = (bf16[2,8,160,128]{3,2,1,0:T(8,128)(2,1)}, bf16[2,8,160,128]{3,2,1,0:T(8,128)(2,1)S(1)}, u32[]{:S(2)}) copy-start(bf16[2,8,160,128]{3,2,1,0:T(8,128)(2,1)S(1)} %pad_maximum_fusion.1.refs_2_) | copy-start | bytes 1966084
  57.0 13.5 %collective-permute-start.12 = (bf16[2,8,160,128]{3,2,1,0:T(8,128)(2,1)S(1)}, bf16[2,8,160,128]{3,2,1,0:T(8,128)(2,1)S(1)}, u32[]{:S(2)}, u32[]{:S(2)}) collective-permute-start(bf16[2,8,160,128]{3,2,1,0:T(8,128)(2,1)S(1)} %pad_maximum_fusion.1.refs_2_), channel_id=1, source_target_pairs={{18,0},{13,1},{22,4},{1,5},{26,8},{5,9},{30,12},{9,13},{0,16},{29,... | collective-permute-start | bytes 1966088 | tf_op jit(solution)/shard_map/ppermute | solution.py:36
  57.1 29.2 %copy-start.6 = (bf16[2,8,160,128]{3,2,1,0:T(8,128)(2,1)}, bf16[2,8,160,128]{3,2,1,0:T(8,128)(2,1)S(1)}, u32[]{:S(2)}) copy-start(bf16[2,8,160,128]{3,2,1,0:T(8,128)(2,1)S(1)} %collective-permute-done.5.refs_4_) | copy-start | bytes 1966084
  57.1 15.0 %collective-permute-start.6 = (bf16[2,8,160,128]{3,2,1,0:T(8,128)(2,1)S(1)}, bf16[2,8,160,128]{3,2,1,0:T(8,128)(2,1)S(1)}, u32[]{:S(2)}, u32[]{:S(2)}) collective-permute-start(bf16[2,8,160,128]{3,2,1,0:T(8,128)(2,1)S(1)} %collective-permute-done.5.refs_4_), channel_id=1, source_target_pairs={{16,0},{5,1},{20,4},{9,5},{24,8},{13,9},{28,12},{1,13},{2,16},{21,... | collective-permute-start | bytes 1966088 | tf_op jit(solution)/shard_map/ppermute | solution.py:36
  59.8 13.3 %collective-permute-start.7 = (bf16[2,8,160,128]{3,2,1,0:T(8,128)(2,1)S(1)}, bf16[2,8,160,128]{3,2,1,0:T(8,128)(2,1)S(1)}, u32[]{:S(2)}, u32[]{:S(2)}) collective-permute-start(bf16[2,8,160,128]{3,2,1,0:T(8,128)(2,1)S(1)} %pad_maximum_fusion.refs_0_), channel_id=1, source_target_pairs={{1,0},{0,1},{5,4},{4,5},{9,8},{8,9},{13,12},{12,13},{17,16},{16,17... | collective-permute-start | bytes 1966088 | tf_op jit(solution)/shard_map/ppermute | solution.py:36
  62.4 12.0 %collective-permute-start.14 = (bf16[2,8,160,128]{3,2,1,0:T(8,128)(2,1)S(1)}, bf16[2,8,160,128]{3,2,1,0:T(8,128)(2,1)S(1)}, u32[]{:S(2)}, u32[]{:S(2)}) collective-permute-start(bf16[2,8,160,128]{3,2,1,0:T(8,128)(2,1)S(1)} %pad_maximum_fusion.1.refs_2_), channel_id=1, source_target_pairs={{16,0},{5,1},{20,4},{9,5},{24,8},{13,9},{28,12},{1,13},{2,16},{21,... | collective-permute-start | bytes 1966088 | tf_op jit(solution)/shard_map/ppermute | solution.py:36
  63.5 20.6 %copy-start.7 = (bf16[2,8,160,128]{3,2,1,0:T(8,128)(2,1)}, bf16[2,8,160,128]{3,2,1,0:T(8,128)(2,1)S(1)}, u32[]{:S(2)}) copy-start(bf16[2,8,160,128]{3,2,1,0:T(8,128)(2,1)S(1)} %collective-permute-done.16.refs_10_) | copy-start | bytes 1966084
  63.5 14.0 %collective-permute-start.10 = (bf16[2,8,160,128]{3,2,1,0:T(8,128)(2,1)S(1)}, bf16[2,8,160,128]{3,2,1,0:T(8,128)(2,1)S(1)}, u32[]{:S(2)}, u32[]{:S(2)}) collective-permute-start(bf16[2,8,160,128]{3,2,1,0:T(8,128)(2,1)S(1)} %pad_maximum_fusion.1.refs_2_), channel_id=1, source_target_pairs={{1,0},{0,1},{5,4},{4,5},{9,8},{8,9},{13,12},{12,13},{17,16},{16,17... | collective-permute-start | bytes 1966088 | tf_op jit(solution)/shard_map/ppermute | solution.py:36
  70.5 13.6 %copy-start.8 = (bf16[2,8,160,128]{3,2,1,0:T(8,128)(2,1)}, bf16[2,8,160,128]{3,2,1,0:T(8,128)(2,1)S(1)}, u32[]{:S(2)}) copy-start(bf16[2,8,160,128]{3,2,1,0:T(8,128)(2,1)S(1)} %collective-permute-done.12.refs_6_) | copy-start | bytes 1966084
  70.5 7.1 %collective-permute-start.17 = (bf16[2,8,160,128]{3,2,1,0:T(8,128)(2,1)S(1)}, bf16[2,8,160,128]{3,2,1,0:T(8,128)(2,1)S(1)}, u32[]{:S(2)}, u32[]{:S(2)}) collective-permute-start(bf16[2,8,160,128]{3,2,1,0:T(8,128)(2,1)S(1)} %collective-permute-done.16.refs_10_), channel_id=1, source_target_pairs={{1,0},{0,1},{5,4},{4,5},{9,8},{8,9},{13,12},{12,13},{17,16},{16,17... | collective-permute-start | bytes 1966088 | tf_op jit(solution)/shard_map/ppermute | solution.py:36
  72.2 12.0 %copy-start.9 = (bf16[2,8,160,128]{3,2,1,0:T(8,128)(2,1)}, bf16[2,8,160,128]{3,2,1,0:T(8,128)(2,1)S(1)}, u32[]{:S(2)}) copy-start(bf16[2,8,160,128]{3,2,1,0:T(8,128)(2,1)S(1)} %collective-permute-done.6.refs_12_) | copy-start | bytes 1966084
  72.2 10.9 %collective-permute-start.19 = (bf16[2,8,160,128]{3,2,1,0:T(8,128)(2,1)S(1)}, bf16[2,8,160,128]{3,2,1,0:T(8,128)(2,1)S(1)}, u32[]{:S(2)}, u32[]{:S(2)}) collective-permute-start(bf16[2,8,160,128]{3,2,1,0:T(8,128)(2,1)S(1)} %collective-permute-done.12.refs_6_), channel_id=1, source_target_pairs={{18,0},{13,1},{22,4},{1,5},{26,8},{5,9},{30,12},{9,13},{0,16},{29,... | collective-permute-start | bytes 1966088 | tf_op jit(solution)/shard_map/ppermute | solution.py:36
  73.1 11.0 %copy-start.10 = (bf16[2,8,160,128]{3,2,1,0:T(8,128)(2,1)}, bf16[2,8,160,128]{3,2,1,0:T(8,128)(2,1)S(1)}, u32[]{:S(2)}) copy-start(bf16[2,8,160,128]{3,2,1,0:T(8,128)(2,1)S(1)} %collective-permute-done.7.refs_1_) | copy-start | bytes 1966084
  73.1 11.0 %collective-permute-start.11 = (bf16[2,8,160,128]{3,2,1,0:T(8,128)(2,1)S(1)}, bf16[2,8,160,128]{3,2,1,0:T(8,128)(2,1)S(1)}, u32[]{:S(2)}, u32[]{:S(2)}) collective-permute-start(bf16[2,8,160,128]{3,2,1,0:T(8,128)(2,1)S(1)} %collective-permute-done.5.refs_4_), channel_id=1, source_target_pairs={{1,0},{0,1},{5,4},{4,5},{9,8},{8,9},{13,12},{12,13},{17,16},{16,17... | collective-permute-start | bytes 1966088 | tf_op jit(solution)/shard_map/ppermute | solution.py:36
  74.3 9.8 %copy-start.11 = (bf16[2,8,160,128]{3,2,1,0:T(8,128)(2,1)}, bf16[2,8,160,128]{3,2,1,0:T(8,128)(2,1)S(1)}, u32[]{:S(2)}) copy-start(bf16[2,8,160,128]{3,2,1,0:T(8,128)(2,1)S(1)} %collective-permute-done.14.refs_8_) | copy-start | bytes 1966084
  74.3 9.7 %collective-permute-start.13 = (bf16[2,8,160,128]{3,2,1,0:T(8,128)(2,1)S(1)}, bf16[2,8,160,128]{3,2,1,0:T(8,128)(2,1)S(1)}, u32[]{:S(2)}, u32[]{:S(2)}) collective-permute-start(bf16[2,8,160,128]{3,2,1,0:T(8,128)(2,1)S(1)} %collective-permute-done.12.refs_6_), channel_id=1, source_target_pairs={{1,0},{0,1},{5,4},{4,5},{9,8},{8,9},{13,12},{12,13},{17,16},{16,17... | collective-permute-start | bytes 1966088 | tf_op jit(solution)/shard_map/ppermute | solution.py:36
  77.5 6.7 %copy-start.12 = (bf16[2,8,160,128]{3,2,1,0:T(8,128)(2,1)}, bf16[2,8,160,128]{3,2,1,0:T(8,128)(2,1)S(1)}, u32[]{:S(2)}) copy-start(bf16[2,8,160,128]{3,2,1,0:T(8,128)(2,1)S(1)} %collective-permute-done.10.refs_3_) | copy-start | bytes 1966084
  77.5 6.6 %collective-permute-start.15 = (bf16[2,8,160,128]{3,2,1,0:T(8,128)(2,1)S(1)}, bf16[2,8,160,128]{3,2,1,0:T(8,128)(2,1)S(1)}, u32[]{:S(2)}, u32[]{:S(2)}) collective-permute-start(bf16[2,8,160,128]{3,2,1,0:T(8,128)(2,1)S(1)} %collective-permute-done.14.refs_8_), channel_id=1, source_target_pairs={{1,0},{0,1},{5,4},{4,5},{9,8},{8,9},{13,12},{12,13},{17,16},{16,17... | collective-permute-start | bytes 1966088 | tf_op jit(solution)/shard_map/ppermute | solution.py:36
  77.6 6.6 %copy-start.13 = (bf16[2,8,160,128]{3,2,1,0:T(8,128)(2,1)}, bf16[2,8,160,128]{3,2,1,0:T(8,128)(2,1)S(1)}, u32[]{:S(2)}) copy-start(bf16[2,8,160,128]{3,2,1,0:T(8,128)(2,1)S(1)} %collective-permute-done.17.refs_11_) | copy-start | bytes 1966084
  77.6 6.5 %collective-permute-start.18 = (bf16[2,8,160,128]{3,2,1,0:T(8,128)(2,1)S(1)}, bf16[2,8,160,128]{3,2,1,0:T(8,128)(2,1)S(1)}, u32[]{:S(2)}, u32[]{:S(2)}) collective-permute-start(bf16[2,8,160,128]{3,2,1,0:T(8,128)(2,1)S(1)} %collective-permute-done.6.refs_12_), channel_id=1, source_target_pairs={{1,0},{0,1},{5,4},{4,5},{9,8},{8,9},{13,12},{12,13},{17,16},{16,17... | collective-permute-start | bytes 1966088 | tf_op jit(solution)/shard_map/ppermute | solution.py:36
  83.1 1.1 %copy-start.14 = (bf16[2,8,160,128]{3,2,1,0:T(8,128)(2,1)}, bf16[2,8,160,128]{3,2,1,0:T(8,128)(2,1)S(1)}, u32[]{:S(2)}) copy-start(bf16[2,8,160,128]{3,2,1,0:T(8,128)(2,1)S(1)} %collective-permute-done.19.refs_14_) | copy-start | bytes 1966084
  83.1 2.9 %collective-permute-start.20 = (bf16[2,8,160,128]{3,2,1,0:T(8,128)(2,1)S(1)}, bf16[2,8,160,128]{3,2,1,0:T(8,128)(2,1)}, u32[]{:S(2)}, u32[]{:S(2)}) collective-permute-start(bf16[2,8,160,128]{3,2,1,0:T(8,128)(2,1)S(1)} %collective-permute-done.19.refs_14_), channel_id=1, source_target_pairs={{1,0},{0,1},{5,4},{4,5},{9,8},{8,9},{13,12},{12,13},{17,16},{16,17... | collective-permute-start | bytes 1966088 | tf_op jit(solution)/shard_map/ppermute | solution.py:36
  84.1 2.3 %copy-start.15 = (bf16[2,8,160,128]{3,2,1,0:T(8,128)(2,1)}, bf16[2,8,160,128]{3,2,1,0:T(8,128)(2,1)S(1)}, u32[]{:S(2)}) copy-start(bf16[2,8,160,128]{3,2,1,0:T(8,128)(2,1)S(1)} %collective-permute-done.11.refs_5_) | copy-start | bytes 1966084
  84.1 0.9 copy-start.17
  84.1 1.1 %copy-start.16 = (bf16[2,8,160,128]{3,2,1,0:T(8,128)(2,1)}, bf16[2,8,160,128]{3,2,1,0:T(8,128)(2,1)S(1)}, u32[]{:S(2)}) copy-start(bf16[2,8,160,128]{3,2,1,0:T(8,128)(2,1)S(1)} %collective-permute-done.13.refs_7_) | copy-start | bytes 1966084
  85.2 0.8 copy-start.18
